TPU v7x, 128 devices: a whole 4x4x4 slice. The times are simulated.
128 devices in a mesh: blk: 16 (over z, y_lo, core), rep: 8 (over y_hi, x).
Axes of the slice: x: 4, y: 4 (y_hi: 2, y_lo: 2; y = y_hi * 2 + y_lo), z: 4, core: 2. Of those that a mesh axis runs over, the one named last changes fastest.
Arguments:
- features: bfloat16 [131072, 256], P(('blk', 'rep'))
- weight: bfloat16 [256, 256], replicated, may hold values from -0.375 to 0.375
- norm_gain: float32 [256], replicated, may hold values from 0.1 to 1.9
- norm_shift: float32 [256], replicated, may hold values from -3 to 3
- tile_values: bfloat16 [16, 128, 32, 128, 128], P('blk', 'rep'), may hold values from 0 to 0.0625
- tile_rows: int32 [16, 128, 32], P('blk', 'rep'), may hold values from 0 to 63
- tile_cols: int32 [16, 128, 32], P('blk', 'rep'), may hold values from 0 to 7
- tile_counts: int32 [16, 128], P('blk', 'rep'), may hold values from 8 to 32, as said below
- cotangent: bfloat16 [131072, 256], P(('blk', 'rep')), may hold values from -6 to 6
Outputs:
- output: bfloat16 [131072, 256], P(('blk', 'rep'))
- grad_x: bfloat16 [131072, 256], P(('blk', 'rep'))
- grad_w: float32 [256, 256], replicated
- grad_gamma: float32 [256], replicated
- grad_beta: float32 [256], replicated
Inputs may be any that keep to these rules, and one draw needn't show every extreme that they name: `tile_counts`: A device's count for its own position along blk is 32.
All inputs are finite; a program needn't handle non-finite values.
Results may differ from a plain program's by a relative error of at most 0.024.
Values may be sent and summed in bfloat16 or wider, within the bound.
No kernel may reach another device: no remote copies, remote signals or barrier semaphores. Data moves between devices by JAX's collectives and lax.ppermute only.
A program may use at most 192 MiB of HBM per device.

v0:
```python
import jax
import jax.numpy as jnp
from jax import lax
from jax.sharding import PartitionSpec as P

norm_eps = 1e-05


def on_device(
    features,
    weight,
    norm_gain,
    norm_shift,
    tile_values,
    tile_rows,
    tile_cols,
    tile_counts,
    cotangent,
):
    blocks_all = tile_values[0]
    row_lists = tile_rows[0]
    col_lists = tile_cols[0]
    live_counts = tile_counts[0]
    local_rows, feat_width = features.shape
    tile_size = blocks_all.shape[-1]
    slot_count = blocks_all.shape[1]
    col_count = local_rows // tile_size
    blk_count = lax.axis_size("blk")
    rep_count = lax.axis_size("rep")
    node_count = local_rows * blk_count * rep_count
    slot_ids = jnp.arange(slot_count, dtype=jnp.int32)
    proj = jnp.dot(features, weight, preferred_element_type=jnp.float32).astype(jnp.bfloat16)
    proj_tiles = proj.reshape(col_count, tile_size, feat_width)

    def source_lists(source):
        blocks = lax.dynamic_index_in_dim(blocks_all, source, 0, keepdims=False)
        row_index = lax.dynamic_index_in_dim(row_lists, source, 0, keepdims=False)
        col_index = lax.dynamic_index_in_dim(col_lists, source, 0, keepdims=False)
        live_count = lax.dynamic_index_in_dim(live_counts, source, 0, keepdims=False)
        return (blocks, row_index, col_index, live_count)

    blank_total = jnp.zeros((col_count * rep_count, tile_size, feat_width), jnp.float32)
    segment = lax.all_gather(proj_tiles, "blk", axis=0, tiled=True)
    offset = jnp.int32(0)
    seg_rows = segment.shape[0]
    first_source = offset // col_count
    end_source = (offset + seg_rows - 1) // col_count + 1

    def forward_visit_source(source, summed_terms):
        blocks, row_index, col_index, live_count = source_lists(source)
        local_index = source * col_count + col_index
        is_valid = (local_index >= 0) & (local_index < seg_rows) & (slot_ids < live_count)
        panel_rows = jnp.take(segment, jnp.clip(local_index, 0, seg_rows - 1), axis=0)
        product = jnp.einsum("kij,kjf->kif", blocks, panel_rows, preferred_element_type=jnp.float32)
        product = jnp.where(is_valid[:, None, None], product, 0.0)
        return summed_terms.at[row_index].add(product)

    partial_sums = lax.fori_loop(first_source, end_source, forward_visit_source, blank_total)
    summed = lax.psum_scatter(partial_sums, "rep", scatter_dimension=0, tiled=True).reshape(
        local_rows, feat_width
    )
    feat_sum = lax.psum(jnp.sum(summed, axis=0), ("blk", "rep"))
    feat_mean = feat_sum / node_count
    centered = summed - feat_mean
    square_sum = lax.psum(jnp.sum(centered * centered, axis=0), ("blk", "rep"))
    variance = square_sum / node_count
    inv_std = lax.rsqrt(variance + norm_eps)
    normed = centered * inv_std
    affine = norm_gain * normed + norm_shift
    gate_value = jax.nn.sigmoid(affine)
    output = (affine * gate_value).astype(jnp.bfloat16)
    grad_affine = cotangent.astype(jnp.float32) * gate_value * (1.0 + affine * (1.0 - gate_value))
    grad_beta, grad_gamma = lax.psum(
        (jnp.sum(grad_affine, axis=0), jnp.sum(grad_affine * normed, axis=0)), ("blk", "rep")
    )
    grad_summed = (
        norm_gain
        * inv_std
        * (grad_affine - grad_beta / node_count - normed * grad_gamma / node_count)
    ).astype(jnp.bfloat16)
    group_grads = lax.all_gather(
        grad_summed.reshape(col_count, tile_size, feat_width), "rep", axis=0, tiled=True
    )
    offset = jnp.int32(0)
    amount = col_count * lax.axis_size("blk")
    first_source = offset // col_count
    end_source = (offset + amount - 1) // col_count + 1

    def backward_visit_source(source, summed_terms):
        blocks, row_index, col_index, live_count = source_lists(source)
        local_index = source * col_count + col_index
        is_valid = (local_index >= 0) & (local_index < amount) & (slot_ids < live_count)
        panel_rows = jnp.take(group_grads, row_index, axis=0)
        product = jnp.einsum("kji,kjf->kif", blocks, panel_rows, preferred_element_type=jnp.float32)
        product = jnp.where(is_valid[:, None, None], product, 0.0)
        return summed_terms.at[jnp.clip(local_index, 0, amount - 1)].add(product)

    start_terms = jnp.zeros((amount, tile_size, feat_width), jnp.float32)
    grad_proj = lax.psum_scatter(
        lax.fori_loop(first_source, end_source, backward_visit_source, start_terms).astype(
            jnp.bfloat16
        ),
        "blk",
        scatter_dimension=0,
        tiled=True,
    ).astype(jnp.float32)
    proj_grad = grad_proj.reshape(local_rows, feat_width).astype(jnp.bfloat16)
    grad_x = lax.dot_general(
        proj_grad, weight, (((1,), (1,)), ((), ())), preferred_element_type=jnp.float32
    ).astype(jnp.bfloat16)
    weight_term = lax.dot_general(
        features, proj_grad, (((0,), (0,)), ((), ())), preferred_element_type=jnp.float32
    )
    grad_w = lax.psum(weight_term, ("blk", "rep"))
    return (output, grad_x, grad_w, grad_gamma, grad_beta)


def solution(mesh):
    return jax.shard_map(
        on_device,
        mesh=mesh,
        in_specs=(
            P(("blk", "rep"), None),
            P(),
            P(),
            P(),
            P("blk", "rep", None, None, None),
            P("blk", "rep", None),
            P("blk", "rep", None),
            P("blk", "rep"),
            P(("blk", "rep"), None),
        ),
        out_specs=(P(("blk", "rep"), None), P(("blk", "rep"), None), P(), P(), P()),
        check_vma=False,
    )
```

profile of v0, /device:TPU:1, one launch (start us, length us, event | category | flops | bytes accessed | tf_op | source)
XLA Modules:
  0.0 1353.7 jit_solution(13606504992103751880)
XLA Ops:
  10.3 55.9 %all-gather.3.cloned.1.call-done = bf16[128,128,256]{2,1,0:T(8,128)(2,1)} async-done(((bf16[8,128,256]{2,1,0:T(8,128)(2,1)}), bf16[128,128,256]{2,1,0:T(8,128)(2,1)}) %all-gather.3.cloned.1.call-update) | async-done | bytes 8388624 | tf_op jit(solution)/shard_map/all_gather | solution.py:43
  70.4 330.4 %while.24 = (s32[]{:T(128)}, f32[64,128,256]{2,1,0:T(8,128)}, s32[16,32]{1,0:T(8,128)}, s32[16,32]{1,0:T(8,128)}, s32[16]{0:T(128)S(1)}, /*index=5*/bf16[16,32,1...) while((s32[]{:T(128)}, f32[64,128,256]{2,1,0:T(8,128)}, ...), condition=%wide.region_2.3_spmd.clone, body=%wide.region_0.2_spmd.clone.sunk | while | flops 271582848 | bytes 24122896 | solution.py:58
  81.1 10.0 scatter_fusion
  101.7 10.0 scatter_fusion
  122.3 9.9 scatter_fusion
  142.9 10.0 scatter_fusion
  163.6 9.9 scatter_fusion
  184.1 10.0 scatter_fusion
  204.8 10.0 scatter_fusion
  225.4 9.9 scatter_fusion
  246.0 10.1 scatter_fusion
  266.7 9.9 scatter_fusion
  287.3 10.1 scatter_fusion
  308.0 10.0 scatter_fusion
  328.6 10.0 scatter_fusion
  349.3 10.0 scatter_fusion
  369.9 10.1 scatter_fusion
  390.7 10.1 scatter_fusion
  400.8 116.1 %reduce-scatter.3.cloned.1.call-done = f32[8,128,256]{2,1,0:T(8,128)} async-done(((f32[64,128,256]{2,1,0:T(8,128)}), f32[8,128,256]{2,1,0:T(8,128)}) %reduce-scatter.3.cloned.1.call-update) | async-done | bytes 1048592 | tf_op jit(solution)/shard_map/reduce_scatter | solution.py:59
  518.4 64.7 %psum.35 = f32[256]{0:T(256)S(1)} all-reduce(f32[256]{0:T(256)S(1)} %reduce_sum.36), channel_id=1, replica_groups=mesh['blk'=16,'rep'=8] {'blk','rep'}, use_global_device_ids=true, to_apply=%region_5.6 | all-reduce | flops 256 | bytes 2048 | tf_op jit(solution)/shard_map/psum | solution.py:62
  584.5 62.7 %psum.36 = f32[256]{0:T(256)S(1)} all-reduce(f32[256]{0:T(256)S(1)} %multiply_reduce_fusion.1), channel_id=1, replica_groups=mesh['blk'=16,'rep'=8] {'blk','rep'}, use_global_device_ids=true, to_apply=%region_7.8 | all-reduce | flops 256 | bytes 2048 | tf_op jit(solution)/shard_map/psum | solution.py:65
  649.0 64.1 %all-reduce = (f32[256]{0:T(256)S(1)}, f32[256]{0:T(256)S(1)}) all-reduce(f32[256]{0:T(256)S(1)} %get-tuple-element.192, f32[256]{0:T(256)S(1)} %get-tuple-element.191), channel_id=1, replica_groups=mesh['blk'=16,'rep'=8] {'blk','rep'}, use_global_device_ids=true, to_apply=%region_11.12 | all-reduce | flops 512 | bytes 4096 | tf_op jit(solution)/shard_map/psum | solution.py:73
  715.1 21.3 %copy.17 = bf16[1,16,32,128,128]{3,4,2,1,0:T(8,128)(2,1)} copy(bf16[1,16,32,128,128]{4,3,2,1,0:T(8,128)(2,1)} %bitcast.93) | data formatting | bytes 33554432 | tf_op args[4]
  736.4 46.2 %all-gather.5.cloned.1.call-done = bf16[64,128,256]{2,1,0:T(8,128)(2,1)} async-done(((bf16[8,128,256]{2,1,0:T(8,128)(2,1)}), bf16[64,128,256]{2,1,0:T(8,128)(2,1)}) %all-gather.5.cloned.1.call-update) | async-done | bytes 4194320 | tf_op jit(solution)/shard_map/all_gather | solution.py:81
  790.4 304.0 %while.25 = (s32[]{:T(128)}, f32[128,128,256]{2,1,0:T(8,128)}, s32[16,32]{1,0:T(8,128)}, s32[16]{0:T(128)S(1)}, bf16[16,32,128,128]{2,3,1,0:T(8,128)(2,1)}, /*in...) while((s32[]{:T(128)}, f32[128,128,256]{2,1,0:T(8,128)}, ...), condition=%wide.region_14.15_spmd.clone, body=%wide.region_12.14_spmd.clone.sunk | while | flops 271582848 | bytes 24122772 | solution.py:100
  818.8 9.6 scatter_fusion.1
  913.8 9.5 scatter_fusion.1
  951.8 9.5 scatter_fusion.1
  1027.8 9.6 scatter_fusion.1
  1065.8 9.5 scatter_fusion.1
  1103.4 94.7 %reduce-scatter.5.cloned.1.call-done = bf16[8,128,256]{2,1,0:T(8,128)(2,1)} async-done(((bf16[128,128,256]{2,1,0:T(8,128)(2,1)}), bf16[8,128,256]{2,1,0:T(8,128)(2,1)}) %reduce-scatter.5.cloned.1.call-update) | async-done | bytes 524304 | tf_op jit(solution)/shard_map/reduce_scatter | solution.py:99
  1202.4 143.0 %all-reduce.3.cloned.1.call-done = f32[256,256]{0,1:T(8,128)} async-done(((f32[256,256]{0,1:T(8,128)}), f32[256,256]{0,1:T(8,128)}) %all-reduce.3.cloned.1.call-update) | async-done | bytes 262160 | tf_op jit(solution)/shard_map/psum | solution.py:114
  (261 shorter events, 463.2 us)
Async XLA Ops:
  7.2 1.0 copy-start
  7.2 59.0 %all-gather.3.cloned.1.call-start = ((), (), s32[]{:S(2)}) async-start(), calls=%async_computation.2 | async-start | bytes 8912896 | tf_op jit(solution)/shard_map/all_gather | solution.py:43
  10.2 506.7 %reduce-scatter.3.cloned.1.call-start = ((), (), s32[]{:S(2)}) async-start(), calls=%async_computation.3 | async-start | bytes 9437184 | tf_op jit(solution)/shard_map/reduce_scatter | solution.py:59
  66.2 4.2 copy-start.8
  400.8 246.4 %copy-start.4 = (f32[256]{0:T(256)S(1)}, f32[256]{0:T(256)}, u32[]{:S(2)}) copy-start(f32[256]{0:T(256)} %param.15) | copy-start | bytes 3076
  400.8 246.4 %copy-start.2 = (bf16[1024,256]{1,0:T(8,128)(2,1)S(1)}, bf16[1024,256]{1,0:T(8,128)(2,1)}, u32[]{:S(2)}) copy-start(bf16[1024,256]{1,0:T(8,128)(2,1)} %param.21) | copy-start | bytes 1572868
  400.8 246.4 %copy-start.5 = (f32[256]{0:T(256)S(1)}, f32[256]{0:T(256)}, u32[]{:S(2)}) copy-start(f32[256]{0:T(256)} %param.16) | copy-start | bytes 3076
  400.8 381.7 %all-gather.5.cloned.1.call-start = ((), (), s32[]{:S(2)}) async-start(), calls=%async_computation.4 | async-start | bytes 4718592 | tf_op jit(solution)/shard_map/all_gather | solution.py:81
  516.9 196.2 %copy-start.1 = (f32[8,128,256]{2,1,0:T(8,128)S(1)}, f32[8,128,256]{2,1,0:T(8,128)}, u32[]{:S(2)}) copy-start(f32[8,128,256]{2,1,0:T(8,128)} %reduce-scatter.3.cloned.1.call-done) | copy-start | bytes 3145732
  713.1 23.3 %copy-start.6 = (f32[256]{0:T(256)}, f32[256]{0:T(256)S(1)}, u32[]{:S(2)}) copy-start(f32[256]{0:T(256)S(1)} %get-tuple-element.221) | copy-start | bytes 3076
  713.1 23.3 %copy-start.7 = (f32[256]{0:T(256)}, f32[256]{0:T(256)S(1)}, u32[]{:S(2)}) copy-start(f32[256]{0:T(256)S(1)} %get-tuple-element.222) | copy-start | bytes 3076
  714.8 483.3 %reduce-scatter.5.cloned.1.call-start = ((), (), s32[]{:S(2)}) async-start(), calls=%async_computation.5 | async-start | bytes 8912896 | tf_op jit(solution)/shard_map/reduce_scatter | solution.py:99
  1103.3 96.9 %copy-start.3 = (bf16[256,256]{1,0:T(8,128)(2,1)S(1)}, bf16[256,256]{1,0:T(8,128)(2,1)}, u32[]{:S(2)}) copy-start(bf16[256,256]{1,0:T(8,128)(2,1)} %param.14) | copy-start | bytes 393220
  1103.4 242.0 %all-reduce.3.cloned.1.call-start = ((), (), s32[]{:S(2)}) async-start(), calls=%async_computation.6 | async-start | bytes 524288 | tf_op jit(solution)/shard_map/psum | solution.py:114
Sparse Core Ops, SparseCore 0:
  10.3 55.7 all-gather.2
  400.9 115.9 reduce-scatter.2
  715.0 67.5 all-gather.4
  1103.5 94.5 reduce-scatter.4
  1203.3 142.0 all-reduce.2
where the time goes:
time: 1360 us; the launch traced here: 1350 us
  waiting for transfers between devices  456 us (34%)
  other arithmetic  394 us (29%)
  blocking collectives  191 us (14%)
  local copies, waits for them, and re-layouts  166 us (12%)
  matrix products  132 us (10%)
  between operations  13.8 us (1%)
    scatter-add x16, other arithmetic, forward_visit_source(): return summed_terms.at[row_index].add(product)  160 us
    scatter-add x16, other arithmetic, backward_visit_source(): return summed_terms.at[jnp.clip(local_index, 0, amount - 1)].add(product)  152 us
    psum x1, waiting for transfers between devices, on_device(): grad_w = lax.psum(weight_term, ('blk', 'rep'))  143 us
    reduce_scatter x1, waiting for transfers between devices, on_device(): lax.psum_scatter(partial_sums, 'rep', scatter_dimension=0, tiled=True)  116 us
    reduce_scatter x1, waiting for transfers between devices, on_device(): lax.psum_scatter(lax.fori_loop(first_source, end_source, backward_visit_s...  94.7 us
    gather x16, local copies, waits for them, and re-layouts, forward_visit_source(): jnp.take(segment, jnp.clip(local_index, 0, seg_rows - 1), axis=0)  65 us
    psum x1, blocking collectives, on_device(): feat_sum = lax.psum(jnp.sum(summed, axis=0), ('blk', 'rep'))  64.7 us
    psum x1, blocking collectives, on_device(): lax.psum((jnp.sum(grad_affine, axis=0), jnp.sum(grad_affine * normed, axi...  64.1 us
  transfers between devices with their start and end apart: 5, of which 5 were waited for; matrix products, arithmetic and copies ran while one was open for 2% of the time, Pallas kernels for 0%

commit v1 on v0

v1 whole, which is shorter than its diff:
```python
import functools

import jax
import jax.numpy as jnp
from jax import lax
from jax.experimental import pallas as pl
from jax.experimental.pallas import tpu as pltpu
from jax.sharding import PartitionSpec as P

norm_eps = 1e-05
GROUP = 8
BF16, F32 = jnp.bfloat16, jnp.float32
VMEM_LIMIT = 48 * 2**20


def forward_kernel(rows_ref, cols_ref, counts_ref, tiles_ref, proj_ref, out_ref, offset_ref, acc_ref):
    step = pl.program_id(0)
    row_tiles = out_ref.shape[0]

    @pl.when(step == 0)
    def _():
        def zero(i, carry):
            acc_ref[i] = jnp.zeros(acc_ref.shape[1:], F32)
            return carry

        lax.fori_loop(0, row_tiles + 1, zero, 0)

    count = counts_ref[step]

    def add_group(g, carry):
        products, where = [], []
        for j in range(GROUP):
            k = g * GROUP + j
            products.append(
                jnp.dot(tiles_ref[0, k], proj_ref[0, cols_ref[step, k]], preferred_element_type=F32)
            )
            where.append(jnp.where(k < count, rows_ref[step, k], row_tiles))
        for j in range(GROUP):
            acc_ref[where[j]] += products[j]
        return carry

    lax.fori_loop(0, (count + GROUP - 1) // GROUP, add_group, 0)

    @pl.when(step == pl.num_programs(0) - 1)
    def _():
        def total(i, carry):
            return carry + jnp.sum(acc_ref[i].reshape(-1, 8, acc_ref.shape[2]), axis=0)

        sums = lax.fori_loop(0, row_tiles, total, jnp.zeros((8, acc_ref.shape[2]), F32))
        offset = jnp.sum(sums, axis=0, keepdims=True) / (row_tiles * acc_ref.shape[1])
        offset_ref[...] = offset

        def put(i, carry):
            out_ref[i] = (acc_ref[i] - offset).astype(out_ref.dtype)
            return carry

        lax.fori_loop(0, row_tiles, put, 0)


def forward_tiles(tiles, rows, cols, counts, proj, row_tiles):
    sources, slots, tile, _ = tiles.shape
    col_tiles, width = proj.shape[1], proj.shape[3]
    return pl.pallas_call(
        forward_kernel,
        grid_spec=pltpu.PrefetchScalarGridSpec(
            num_scalar_prefetch=3,
            grid=(sources,),
            in_specs=[
                pl.BlockSpec((1, slots, tile, tile), lambda s, *_: (s, 0, 0, 0)),
                pl.BlockSpec((1, col_tiles, tile, width), lambda s, *_: (s, 0, 0, 0)),
            ],
            out_specs=[
                pl.BlockSpec((row_tiles, tile, width), lambda s, *_: (0, 0, 0)),
                pl.BlockSpec((1, width), lambda s, *_: (0, 0)),
            ],
            scratch_shapes=[pltpu.VMEM((row_tiles + 1, tile, width), F32)],
        ),
        out_shape=[
            jax.ShapeDtypeStruct((row_tiles, tile, width), BF16),
            jax.ShapeDtypeStruct((1, width), F32),
        ],
        compiler_params=pltpu.CompilerParams(vmem_limit_bytes=VMEM_LIMIT),
        name="forward_tiles",
    )(rows, cols, counts, tiles, proj)


def backward_kernel(rows_ref, cols_ref, counts_ref, tiles_ref, grad_ref, out_ref, acc_ref):
    step = pl.program_id(0)
    col_tiles = out_ref.shape[1]
    for i in range(col_tiles + 1):
        acc_ref[i] = jnp.zeros(acc_ref.shape[1:], F32)
    count = counts_ref[step]

    def add_group(g, carry):
        products, where = [], []
        for j in range(GROUP):
            k = g * GROUP + j
            products.append(
                lax.dot_general(
                    tiles_ref[0, k],
                    grad_ref[rows_ref[step, k]],
                    (((0,), (0,)), ((), ())),
                    preferred_element_type=F32,
                )
            )
            where.append(jnp.where(k < count, cols_ref[step, k], col_tiles))
        for j in range(GROUP):
            acc_ref[where[j]] += products[j]
        return carry

    lax.fori_loop(0, (count + GROUP - 1) // GROUP, add_group, 0)
    for i in range(col_tiles):
        out_ref[0, i] = acc_ref[i].astype(out_ref.dtype)


def backward_tiles(tiles, rows, cols, counts, grads, col_tiles):
    sources, slots, tile, _ = tiles.shape
    row_tiles, _, width = grads.shape
    return pl.pallas_call(
        backward_kernel,
        grid_spec=pltpu.PrefetchScalarGridSpec(
            num_scalar_prefetch=3,
            grid=(sources,),
            in_specs=[
                pl.BlockSpec((1, slots, tile, tile), lambda s, *_: (s, 0, 0, 0)),
                pl.BlockSpec((row_tiles, tile, width), lambda s, *_: (0, 0, 0)),
            ],
            out_specs=pl.BlockSpec((1, col_tiles, tile, width), lambda s, *_: (s, 0, 0, 0)),
            scratch_shapes=[pltpu.VMEM((col_tiles + 1, tile, width), F32)],
        ),
        out_shape=jax.ShapeDtypeStruct((sources, col_tiles, tile, width), BF16),
        compiler_params=pltpu.CompilerParams(vmem_limit_bytes=VMEM_LIMIT),
        name="backward_tiles",
    )(rows, cols, counts, tiles, grads)


def copies_of_all(value, axis):
    count = lax.axis_size(axis)
    return lax.all_to_all(jnp.broadcast_to(value[None], (count, *value.shape)), axis, 0, 0)


def sum_over_all(value):
    value = jnp.sum(copies_of_all(value, "rep"), axis=0)
    return jnp.sum(copies_of_all(value, "blk"), axis=0)


def on_device(
    features,
    weight,
    norm_gain,
    norm_shift,
    tile_values,
    tile_rows,
    tile_cols,
    tile_counts,
    cotangent,
):
    tiles, rows, cols, counts = tile_values[0], tile_rows[0], tile_cols[0], tile_counts[0]
    local_rows, width = features.shape
    tile = tiles.shape[-1]
    col_tiles = local_rows // tile
    blk_count = lax.axis_size("blk")
    rep_count = lax.axis_size("rep")
    row_tiles = col_tiles * rep_count
    node_count = local_rows * blk_count * rep_count

    proj = jnp.dot(features, weight, preferred_element_type=F32).astype(BF16)
    gathered = lax.all_gather(proj.reshape(1, col_tiles, tile, width), "blk", axis=0, tiled=True)
    partial_sums, offset = forward_tiles(tiles, rows, cols, counts, gathered, row_tiles)
    parts = lax.all_to_all(partial_sums.reshape(rep_count, local_rows, width), "rep", 0, 0)
    shifted = jnp.sum(parts.astype(F32), axis=0)
    own_mean = jnp.sum(shifted, axis=0) / local_rows
    own_square = jnp.sum((shifted - own_mean) ** 2, axis=0)
    group = copies_of_all(jnp.stack([own_mean, own_square, offset[0]]), "rep")
    group_mean = jnp.sum(group[:, 0], axis=0) / rep_count
    group_square = jnp.sum(group[:, 1], axis=0) + local_rows * jnp.sum(
        (group[:, 0] - group_mean) ** 2, axis=0
    )
    group_offset = jnp.sum(group[:, 2], axis=0)
    everyone = copies_of_all(jnp.stack([group_mean + group_offset, group_square]), "blk")
    feat_mean = jnp.sum(everyone[:, 0], axis=0) / blk_count
    square_sum = jnp.sum(everyone[:, 1], axis=0) + local_rows * rep_count * jnp.sum(
        (everyone[:, 0] - feat_mean) ** 2, axis=0
    )
    inv_std = lax.rsqrt(square_sum / node_count + norm_eps)
    normed = (shifted + (group_offset - feat_mean)) * inv_std
    affine = norm_gain * normed + norm_shift
    gate_value = jax.nn.sigmoid(affine)
    output = (affine * gate_value).astype(BF16)
    grad_affine = cotangent.astype(F32) * gate_value * (1.0 + affine * (1.0 - gate_value))
    grad_beta, grad_gamma = sum_over_all(
        jnp.stack([jnp.sum(grad_affine, axis=0), jnp.sum(grad_affine * normed, axis=0)])
    )
    grad_summed = (
        norm_gain
        * inv_std
        * (grad_affine - grad_beta / node_count - normed * grad_gamma / node_count)
    ).astype(BF16)
    group_grads = lax.all_gather(
        grad_summed.reshape(col_tiles, tile, width), "rep", axis=0, tiled=True
    )
    products = backward_tiles(tiles, rows, cols, counts, group_grads, col_tiles)

    core = lax.axis_index("blk") % 2
    by_core = products.reshape(blk_count // 2, 2, local_rows, width)
    kept = lax.dynamic_index_in_dim(by_core, core, 1, keepdims=False)
    given = lax.dynamic_index_in_dim(by_core, 1 - core, 1, keepdims=False)
    taken = lax.ppermute(given, "blk", [(i, i ^ 1) for i in range(blk_count)])
    chip_sums = (kept.astype(F32) + taken.astype(F32)).astype(BF16)
    same_core = [list(range(c, blk_count, 2)) for c in range(2)]
    terms = lax.all_to_all(chip_sums, "blk", 0, 0, axis_index_groups=same_core)
    proj_grad = jnp.sum(terms.astype(F32), axis=0).astype(BF16)

    grad_x = lax.dot_general(
        proj_grad, weight, (((1,), (1,)), ((), ())), preferred_element_type=F32
    ).astype(BF16)
    weight_term = lax.dot_general(
        features, proj_grad, (((0,), (0,)), ((), ())), preferred_element_type=F32
    )
    pieces = lax.all_to_all(weight_term.reshape(blk_count, -1, width), "blk", 0, 0)
    piece = jnp.sum(copies_of_all(jnp.sum(pieces, axis=0), "rep"), axis=0)
    grad_w = copies_of_all(piece, "blk").reshape(weight.shape)
    return (output, grad_x, grad_w, grad_gamma, grad_beta)


def solution(mesh):
    return jax.shard_map(
        on_device,
        mesh=mesh,
        in_specs=(
            P(("blk", "rep"), None),
            P(),
            P(),
            P(),
            P("blk", "rep", None, None, None),
            P("blk", "rep", None),
            P("blk", "rep", None),
            P("blk", "rep"),
            P(("blk", "rep"), None),
        ),
        out_specs=(P(("blk", "rep"), None), P(("blk", "rep"), None), P(), P(), P()),
        check_vma=False,
    )
```

time: 1360 us -> 407 us (0.30)
  other arithmetic: 394 us -> 13.2 us
  waiting for transfers between devices: 456 us -> 135 us
  local copies, waits for them, and re-layouts: 166 us -> 11.2 us
  matrix products: 132 us -> 3.48 us
  Pallas kernels: 0 us -> 48.3 us
  blocking collectives: 191 us -> 172 us
    scatter-add x32 -> x0, other arithmetic: 312 us -> none  [the longest x16 160 us: forward_visit_source(): return summed_terms.at[row_index].add(product)]
    reduce_scatter x2 -> x0, waiting for transfers between devices: 211 us -> none  [the longest x1 116 us: on_device(): lax.psum_scatter(partial_sums, 'rep', scatter_dimension=0, tiled=True)]
    psum x3 -> x0, blocking collectives: 191 us -> none  [the longest x1 64.7 us: on_device(): feat_sum = lax.psum(jnp.sum(summed, axis=0), ('blk', 'rep'))]
    all_to_all x0 -> x8, blocking collectives: none -> 172 us  [the longest x1 57.1 us: on_device(): lax.all_to_all(partial_sums.reshape(rep_count, local_rows, width), 'rep',...]
    psum x1 -> x0, waiting for transfers between devices: 143 us -> none  [on_device(): grad_w = lax.psum(weight_term, ('blk', 'rep'))]
    dot_general x33 -> x1, matrix products: 128 us -> 2 us  [on_device(): proj = jnp.dot(features, weight, preferred_element_type=F32).astype(BF16)]
    gather x32 -> x0, local copies, waits for them, and re-layouts: 111 us -> none  [the longest x16 65 us: forward_visit_source(): jnp.take(segment, jnp.clip(local_index, 0, seg_rows - 1), axis=0)]
    pallas_call x0 -> x2, Pallas kernels: none -> 48.3 us  [the longest x1 24.5 us: backward_tiles(): pl.pallas_call(backward_kernel, grid_spec=pltpu.PrefetchScalarGridSpec(nu...]
  transfers between devices with their start and end apart: 5 -> 4, of which waited for: 5 -> 4; matrix products, arithmetic and copies ran while one was open for 2% -> 0% of each run, Pallas kernels for 0% -> 0%
where the time goes in v1:
time: 407 us; the launch traced here: 405 us
  blocking collectives  172 us (42%)
  waiting for transfers between devices  135 us (33%)
  Pallas kernels  48.3 us (12%)
  between operations  14.2 us (3%)
  other arithmetic  13.2 us (3%)
  local copies, waits for them, and re-layouts  11.2 us (3%)
  starting transfers between devices  6.92 us (2%)
    all_gather x1, waiting for transfers between devices, on_device(): lax.all_gather(grad_summed.reshape(col_tiles, tile, width), 'rep', axis=0...  66.1 us
    all_to_all x1, blocking collectives, on_device(): lax.all_to_all(partial_sums.reshape(rep_count, local_rows, width), 'rep',...  57.1 us
    all_gather x1, waiting for transfers between devices, on_device(): lax.all_gather(proj.reshape(1, col_tiles, tile, width), 'blk', axis=0, ti...  55.9 us
    all_to_all x1, blocking collectives, on_device(): terms = lax.all_to_all(chip_sums, 'blk', 0, 0, axis_index_groups=same_core)  52.8 us
    all_to_all x5, blocking collectives, copies_of_all(): lax.all_to_all(jnp.broadcast_to(value[None], (count, *value.shape)), axis...  51 us
    pallas_call x1, Pallas kernels, backward_tiles(): pl.pallas_call(backward_kernel, grid_spec=pltpu.PrefetchScalarGridSpec(nu...  24.5 us
    pallas_call x1, Pallas kernels, forward_tiles(): pl.pallas_call(forward_kernel, grid_spec=pltpu.PrefetchScalarGridSpec(num...  23.8 us
    all_to_all x1, blocking collectives, on_device(): lax.all_to_all(weight_term.reshape(blk_count, -1, width), 'blk', 0, 0)  11.5 us
  transfers between devices with their start and end apart: 4, of which 4 were waited for; matrix products, arithmetic and copies ran while one was open for 0% of the time, Pallas kernels for 0%

profile of v1, /device:TPU:1, one launch (start us, length us, event | category | flops | bytes accessed | tf_op | source)
XLA Modules:
  0.0 405.0 jit_solution(2951744115735942056)
XLA Ops:
  7.2 1.0 copy-done
  8.2 2.0 convolution_convert_fusion.1
  10.3 55.9 %all-gather.3.cloned.1.call-done.proj_ref = bf16[16,8,128,256]{3,2,1,0:T(8,128)(2,1)} async-done(((bf16[1,8,128,256]{3,2,1,0:T(8,128)(2,1)}), bf16[16,8,128,256]{3,2,1,0:T(8,128)(2,1)}) %all-gather.3.cloned.1.call-update) | async-done | bytes 8388624 | tf_op jit(solution)/shard_map/all_gather | solution.py:168
  66.2 0.7 copy-done.2
  66.9 0.7 copy-done.4
  67.6 0.7 copy-done.6
  68.2 23.8 %forward_tiles.1 = (bf16[64,128,256]{2,1,0:T(8,128)(2,1)S(1)}, f32[1,256]{1,0:T(1,128)S(1)}) custom-call(s32[16,32]{1,0:T(8,128)S(1)} %bitcast.45, s32[16,32]{1,0:T(8,128)S(1)} %bitcast.47, s32[16]{0:T(128)S(1)} %bitcast.49, bf16[16,32,128,128]{3,2,1,0:T(8,128)(2,1)} %bitcast.51, bf16[16,8,128,256]{3,2,1,0:T(8,128)(2,1)} %all-gather.3.cloned.1.call-done.proj_ref), custom_call_target="tpu_custom_call" | custom-call | tf_op jit(solution)/shard_map/forward_tiles/pallas_call | solution.py:63
  92.0 57.1 %all_to_all.45 = bf16[8,1024,256]{2,1,0:T(8,128)(2,1)S(1)} all-to-all(bf16[8,1024,256]{2,1,0:T(8,128)(2,1)S(1)} %bitcast.44), channel_id=1, replica_groups=mesh['blk'=16,'rep'=8] {'rep'}, dimensions={0} | all-to-all | bytes 8388608 | tf_op jit(solution)/shard_map/all_to_all | solution.py:170
  149.1 2.3 convert_reduce_fusion
  151.7 9.0 %all_to_all.46 = f32[8,3,256]{2,1,0:T(4,128)S(1)} all-to-all(f32[8,3,256]{2,1,0:T(4,128)S(1)} %broadcast_in_dim.12), channel_id=1, replica_groups=mesh['blk'=16,'rep'=8] {'rep'}, dimensions={0} | all-to-all | bytes 49152 | tf_op jit(solution)/shard_map/all_to_all | solution.py:139
  160.8 12.1 %all_to_all.47 = f32[16,2,256]{2,1,0:T(2,128)S(1)} all-to-all(f32[16,2,256]{2,1,0:T(2,128)S(1)} %broadcast_in_dim.13), channel_id=1, replica_groups=mesh['blk'=16,'rep'=8] {'blk'}, dimensions={0} | all-to-all | bytes 65536 | tf_op jit(solution)/shard_map/all_to_all | solution.py:139
  173.0 0.6 fusion.7
  173.6 9.2 %all_to_all.48 = f32[8,2,256]{2,1,0:T(2,128)S(1)} all-to-all(f32[8,2,256]{2,1,0:T(2,128)S(1)} %broadcast_in_dim.14), channel_id=1, replica_groups=mesh['blk'=16,'rep'=8] {'rep'}, dimensions={0} | all-to-all | bytes 32768 | tf_op jit(solution)/shard_map/all_to_all | solution.py:139
  182.9 10.1 %all_to_all.49 = f32[16,2,256]{2,1,0:T(2,128)S(1)} all-to-all(f32[16,2,256]{2,1,0:T(2,128)S(1)} %broadcast_in_dim.15), channel_id=1, replica_groups=mesh['blk'=16,'rep'=8] {'blk'}, dimensions={0} | all-to-all | bytes 65536 | tf_op jit(solution)/shard_map/all_to_all | solution.py:139
  193.0 0.6 fusion.9
  193.6 1.7 multiply_convert_fusion
  195.3 66.1 %all-gather.5.cloned.1.call-done.grad_ref = bf16[64,128,256]{2,1,0:T(8,128)(2,1)} async-done(((bf16[8,128,256]{2,1,0:T(8,128)(2,1)}), bf16[64,128,256]{2,1,0:T(8,128)(2,1)}) %all-gather.5.cloned.1.call-update) | async-done | bytes 4194320 | tf_op jit(solution)/shard_map/all_gather | solution.py:199
  261.4 2.2 copy-done.1
  263.6 24.5 %backward_tiles.1 = bf16[16,8,128,256]{3,2,1,0:T(8,128)(2,1)} custom-call(s32[16,32]{1,0:T(8,128)S(1)} %bitcast.46, s32[16,32]{1,0:T(8,128)S(1)} %bitcast.48, s32[16]{0:T(128)S(1)} %bitcast.50, bf16[16,32,128,128]{3,2,1,0:T(8,128)(2,1)} %bitcast.52, bf16[64,128,256]{2,1,0:T(8,128)(2,1)S(1)} %copy-done.1), custom_call_target="tpu_custom_call" | custom-call | tf_op jit(solution)/shard_map/backward_tiles/pallas_call | solution.py:119
  288.1 4.4 %dynamic-slice_bitcast_fusion = bf16[8,1024,256]{2,1,0:T(8,128)(2,1)} fusion(bf16[8,2,1024,256]{3,2,1,0:T(8,128)(2,1)} %bitcast.53, s32[]{:T(128)S(6)} %select_n.16), kind=kLoop, calls=%fused_computation.4 | loop fusion | bytes 8388612 | tf_op jit(solution)/shard_map/jit(dynamic_index_in_dim)/squeeze | solution.py:207
  292.5 1.1 collective-permute-start
  293.6 7.1 %collective-permute-done = bf16[8,1024,256]{2,1,0:T(8,128)(2,1)} collective-permute-done((bf16[8,1024,256]{2,1,0:T(8,128)(2,1)}, bf16[8,1024,256]{2,1,0:T(8,128)(2,1)}, u32[]{:S(2)}, u32[]{:S(2)}) %collective-permute-start) | collective-permute-done | bytes 4194336 | tf_op jit(solution)/shard_map/ppermute | solution.py:208
  300.8 4.5 %fusion = bf16[8,1024,256]{2,1,0:T(8,128)(2,1)S(1)} fusion(bf16[8,1024,256]{2,1,0:T(8,128)(2,1)} %collective-permute-done, bf16[8,2,1024,256]{3,2,1,0:T(8,128)(2,1)} %bitcast.54, s32[]{:T(128)S(6)} %select_n.15), kind=kLoop, calls=%fused_computation.3 | loop fusion | flops 8388608 | bytes 12582916 | tf_op jit(solution)/shard_map/convert_element_type | solution.py:209
  305.2 52.8 %all_to_all.50 = bf16[8,1024,256]{2,1,0:T(8,128)(2,1)} all-to-all(bf16[8,1024,256]{2,1,0:T(8,128)(2,1)S(1)} %fusion), channel_id=1, replica_groups={{0,16,32,48,64,80,96,112},{8,24,40,56,72,88,104,120},{1,17,33,49,65,81,..., dimensions={0} | all-to-all | bytes 8388608 | tf_op jit(solution)/shard_map/all_to_all | solution.py:211
  358.1 3.1 reduce_sum.170
  361.5 11.5 %all_to_all.51 = f32[16,16,256]{2,1,0:T(8,128)S(1)} all-to-all(f32[16,16,256]{2,1,0:T(8,128)S(1)} %bitcast.57), channel_id=1, replica_groups=mesh['blk'=16,'rep'=8] {'blk'}, dimensions={0} | all-to-all | bytes 524288 | tf_op jit(solution)/shard_map/all_to_all | solution.py:220
  373.1 10.6 %all_to_all.52 = f32[8,16,256]{2,1,0:T(8,128)S(1)} all-to-all(f32[8,16,256]{2,1,0:T(8,128)S(1)} %broadcast_in_dim.16), channel_id=1, replica_groups=mesh['blk'=16,'rep'=8] {'rep'}, dimensions={0} | all-to-all | bytes 262144 | tf_op jit(solution)/shard_map/all_to_all | solution.py:139
  383.7 0.7 broadcast_in_dim.17
  384.5 5.7 %all-to-all-start.8 = ((f32[16,16,256]{2,1,0:T(8,128)}), f32[16,16,256]{2,1,0:T(8,128)S(1)}, u32[]{:S(2)}, u32[]{:S(2)}) async-start(f32[16,16,256]{2,1,0:T(8,128)} %broadcast_in_dim.17), calls=%async_computation.8 | async-start | bytes 524288 | tf_op jit(solution)/shard_map/all_to_all | solution.py:139
  390.2 1.1 convolution_convert_fusion
  391.3 6.1 %all-to-all-done.8 = f32[16,16,256]{2,1,0:T(8,128)S(1)} async-done(((f32[16,16,256]{2,1,0:T(8,128)}), f32[16,16,256]{2,1,0:T(8,128)S(1)}, u32[]{:S(2)}, u32[]{:S(2)}) %all-to-all-start.8) | async-done | bytes 262176 | tf_op jit(solution)/shard_map/all_to_all | solution.py:139
  397.4 0.7 copy.35
  (48 shorter events, 1.0 us)
Async XLA Ops:
  7.2 1.0 copy-start
  7.2 59.0 %all-gather.3.cloned.1.call-start = ((), (), s32[]{:S(2)}) async-start(), calls=%async_computation.9 | async-start | bytes 8912896 | tf_op jit(solution)/shard_map/all_gather | solution.py:168
  10.2 251.2 %all-gather.5.cloned.1.call-start = ((), (), s32[]{:S(2)}) async-start(), calls=%async_computation.10 | async-start | bytes 4718592 | tf_op jit(solution)/shard_map/all_gather | solution.py:199
  66.2 0.7 copy-start.2
  66.9 0.7 copy-start.4
  67.6 0.7 copy-start.6
  149.1 23.8 %copy-start.10 = (f32[256]{0:T(256)S(1)}, f32[256]{0:T(256)}, u32[]{:S(2)}) copy-start(f32[256]{0:T(256)} %param.11) | copy-start | bytes 3076
  149.1 23.9 %copy-start.8 = (bf16[1024,256]{1,0:T(8,128)(2,1)S(1)}, bf16[1024,256]{1,0:T(8,128)(2,1)}, u32[]{:S(2)}) copy-start(bf16[1024,256]{1,0:T(8,128)(2,1)} %param.17) | copy-start | bytes 1572868
  149.1 23.9 %copy-start.11 = (f32[256]{0:T(256)S(1)}, f32[256]{0:T(256)}, u32[]{:S(2)}) copy-start(f32[256]{0:T(256)} %param.12) | copy-start | bytes 3076
  151.5 109.9 %copy-start.3 = (s32[1,16,32]{2,1,0:T(8,128)S(1)}, s32[1,16,32]{2,1,0:T(8,128)}, u32[]{:S(2)}) copy-start(s32[1,16,32]{2,1,0:T(8,128)} %param.14) | copy-start | bytes 6148
  151.5 109.9 %copy-start.5 = (s32[1,16,32]{2,1,0:T(8,128)S(1)}, s32[1,16,32]{2,1,0:T(8,128)}, u32[]{:S(2)}) copy-start(s32[1,16,32]{2,1,0:T(8,128)} %param.15) | copy-start | bytes 6148
  151.5 109.9 %copy-start.7 = (s32[1,16]{1,0:T(1,128)S(1)}, s32[1,16]{1,0:T(1,128)}, u32[]{:S(2)}) copy-start(s32[1,16]{1,0:T(1,128)} %param.16) | copy-start | bytes 196
  193.6 94.5 %copy-start.12 = (f32[1,256]{1,0:T(1,128)}, f32[1,256]{1,0:T(1,128)S(1)}, u32[]{:S(2)}) copy-start(f32[1,256]{1,0:T(1,128)S(1)} %get-tuple-element.26) | copy-start | bytes 3076
  261.4 2.2 copy-start.1
  292.5 8.2 %collective-permute-start = (bf16[8,1024,256]{2,1,0:T(8,128)(2,1)}, bf16[8,1024,256]{2,1,0:T(8,128)(2,1)}, u32[]{:S(2)}, u32[]{:S(2)}) collective-permute-start(bf16[8,1024,256]{2,1,0:T(8,128)(2,1)} %dynamic-slice_bitcast_fusion), channel_id=1, source_target_pairs={{0,8},{8,0},{16,24},{24,16},{32,40},{40,32},{48,56},{56,48},{64,72... | collective-permute-start | bytes 12582920 | tf_op jit(solution)/shard_map/ppermute | solution.py:208
  358.1 32.1 %copy-start.9 = (bf16[256,256]{1,0:T(8,128)(2,1)S(1)}, bf16[256,256]{1,0:T(8,128)(2,1)}, u32[]{:S(2)}) copy-start(bf16[256,256]{1,0:T(8,128)(2,1)} %param.10) | copy-start | bytes 393220
  384.5 13.0 %all-to-all-start.8 = ((f32[16,16,256]{2,1,0:T(8,128)}), f32[16,16,256]{2,1,0:T(8,128)S(1)}, u32[]{:S(2)}, u32[]{:S(2)}) async-start(f32[16,16,256]{2,1,0:T(8,128)} %broadcast_in_dim.17), calls=%async_computation.8 | async-start | bytes 524288 | tf_op jit(solution)/shard_map/all_to_all | solution.py:139
Sparse Core Ops, SparseCore 0:
  10.4 55.7 all-gather.2
  195.4 65.9 all-gather.4

commit v2 on v0

v2 whole, which is shorter than its diff:
```python
import functools

import jax
import jax.numpy as jnp
from jax import lax
from jax.experimental import pallas as pl
from jax.experimental.pallas import tpu as pltpu
from jax.sharding import PartitionSpec as P

norm_eps = 1e-05
GROUP = 8
BF16, F32 = jnp.bfloat16, jnp.float32
VMEM_LIMIT = 56 * 2**20
RING = 4
PLACES = ((2, 1), (1, 1), (-1, 1), (2, 0), (0, 1), (1, 0), (-1, 0), (0, 0))
CUTS = (0, 3, 6, 8)
ANY = pl.BlockSpec(memory_space=pl.ANY)
VMEM = pl.BlockSpec(memory_space=pltpu.VMEM)
SMEM = pl.BlockSpec(memory_space=pltpu.SMEM)


def blk_index(z, y, core):
    return (z % RING) * 4 + (y % 2) * 2 + core % 2


def rep_index(x, y):
    return (y % 2) * RING + x % RING


def blk_links():
    spots = [(z, y, c) for z in range(RING) for y in range(2) for c in range(2)]

    def link(dz, dy, dc):
        pairs = [(blk_index(z, y, c), blk_index(z + dz, y + dy, c + dc)) for z, y, c in spots]
        return lambda value: lax.ppermute(value, "blk", pairs)

    return link(1, 0, 0), link(-1, 0, 0), link(0, 1, 0), link(0, 0, 1)


def rep_links():
    spots = [(x, y) for x in range(RING) for y in range(2)]

    def link(dx, dy):
        pairs = [(rep_index(x, y), rep_index(x + dx, y + dy)) for x, y in spots]
        return lambda value: lax.ppermute(value, "rep", pairs)

    return link(1, 0), link(-1, 0), link(0, 1)


def gather_tree(own, up, down, pair):
    below, above, beside = up(own), down(own), pair(own)
    below_beside, above_beside, far = pair(below), down(beside), up(below)
    a, b, c, _ = CUTS[1], CUTS[2], CUTS[3], None
    far_beside = [(0, pair(far[:a])), (a, down(above_beside[a:b])), (b, up(below_beside[b:c]))]
    whole = {
        (0, 0): own,
        (-1, 0): below,
        (1, 0): above,
        (0, 1): beside,
        (-1, 1): below_beside,
        (1, 1): above_beside,
        (2, 0): far,
    }
    return [far_beside if place == (2, 1) else [(0, whole[place])] for place in PLACES]


def placed(part, first, like):
    after = like.shape[0] - first - part.shape[0]
    return jnp.pad(part.astype(F32), ((first, after), (0, 0), (0, 0)))


def scatter_tree(blocks, up, down, pair):
    wide = {place: block.astype(F32) for place, block in blocks.items()}
    sent = {place: block.astype(BF16) for place, block in blocks.items()}
    a, b = CUTS[1], CUTS[2]
    corner = sent[2, 1]
    far = wide[2, 0] + placed(pair(corner[:a]), 0, corner)
    above_beside = wide[1, 1] + placed(up(corner[a:b]), a, corner)
    below_beside = wide[-1, 1] + placed(down(corner[b:]), b, corner)
    below = (
        wide[-1, 0] + pair(below_beside.astype(BF16)).astype(F32) + down(far.astype(BF16)).astype(F32)
    )
    beside = wide[0, 1] + up(above_beside.astype(BF16)).astype(F32)
    return (
        wide[0, 0]
        + up(sent[1, 0]).astype(F32)
        + down(below.astype(BF16)).astype(F32)
        + pair(beside.astype(BF16)).astype(F32)
    )


def forward_kernel(layout, order_ref, dest_ref, rows_ref, cols_ref, counts_ref, tiles_ref, *refs):
    sources, row_groups = len(layout), len(PLACES)
    parts = sum(len(firsts) for firsts in layout)
    shard_refs, refs = refs[:parts], refs[parts:]
    out_refs, offset_ref = refs[:row_groups], refs[row_groups]
    tiles_v, shards_v, acc_ref, tile_sem, part_sem = refs[row_groups + 1 :]
    col_tiles = out_refs[0].shape[0]
    row_tiles = row_groups * col_tiles

    copies, part = [], 0
    for i, firsts in enumerate(layout):
        source = order_ref[i]
        own = [pltpu.make_async_copy(tiles_ref.at[source], tiles_v.at[i], tile_sem.at[i])]
        for first in firsts:
            size = shard_refs[part].shape[0]
            own.append(
                pltpu.make_async_copy(
                    shard_refs[part], shards_v.at[i, pl.ds(first, size)], part_sem.at[part]
                )
            )
            part += 1
        for copy in own:
            copy.start()
        copies.append(own)

    def zero(i, carry):
        acc_ref[i] = jnp.zeros(acc_ref.shape[1:], F32)
        return carry

    lax.fori_loop(0, row_tiles + 1, zero, 0)

    for i in range(sources):
        for copy in copies[i]:
            copy.wait()
        source = order_ref[i]
        count = counts_ref[source]

        def add_group(g, carry, i=i, source=source, count=count):
            products, where = [], []
            for j in range(GROUP):
                k = g * GROUP + j
                products.append(
                    jnp.dot(tiles_v[i, k], shards_v[i, cols_ref[source, k]], preferred_element_type=F32)
                )
                where.append(jnp.where(k < count, rows_ref[source, k], row_tiles))
            for j in range(GROUP):
                acc_ref[where[j]] += products[j]
            return carry

        lax.fori_loop(0, (count + GROUP - 1) // GROUP, add_group, 0)

    def total(i, carry):
        return carry + jnp.sum(acc_ref[i].reshape(-1, 8, acc_ref.shape[2]), axis=0)

    sums = lax.fori_loop(0, row_tiles, total, jnp.zeros((8, acc_ref.shape[2]), F32))
    offset = jnp.sum(sums, axis=0, keepdims=True) / (row_tiles * acc_ref.shape[1])
    offset_ref[...] = offset
    for d in range(row_groups):
        base = dest_ref[d] * col_tiles

        def put(i, carry, d=d, base=base):
            out_refs[d][i] = (acc_ref[base + i] - offset).astype(BF16)
            return carry

        lax.fori_loop(0, col_tiles, put, 0)


def forward_tiles(order, dests, rows, cols, counts, tiles, shards):
    arrays = [array for parts in shards for _, array in parts]
    layout = tuple(tuple(first for first, _ in parts) for parts in shards)
    sources, slots, tile, _ = tiles.shape
    col_tiles, width = CUTS[-1], arrays[0].shape[2]
    row_tiles = col_tiles * len(PLACES)
    return pl.pallas_call(
        functools.partial(forward_kernel, layout),
        in_specs=[SMEM] * 5 + [ANY] * (1 + len(arrays)),
        out_specs=[VMEM] * (len(PLACES) + 1),
        out_shape=[jax.ShapeDtypeStruct((col_tiles, tile, width), BF16)] * len(PLACES)
        + [jax.ShapeDtypeStruct((1, width), F32)],
        scratch_shapes=[
            pltpu.VMEM((sources, slots, tile, tile), BF16),
            pltpu.VMEM((sources, col_tiles, tile, width), BF16),
            pltpu.VMEM((row_tiles + 1, tile, width), F32),
            pltpu.SemaphoreType.DMA((sources,)),
            pltpu.SemaphoreType.DMA((len(arrays),)),
        ],
        compiler_params=pltpu.CompilerParams(vmem_limit_bytes=VMEM_LIMIT),
        cost_estimate=pl.CostEstimate(flops=6 * 10**9, bytes_accessed=30 * 2**20, transcendentals=0),
        name="forward_tiles",
    )(order, dests, rows, cols, counts, tiles, *arrays)


def backward_kernel(layout, split, order_ref, dest_ref, rows_ref, cols_ref, counts_ref, tiles_ref, *refs):
    parts = sum(len(firsts) for firsts in layout)
    grad_refs, refs = refs[:parts], refs[parts:]
    out_refs, (tiles_v, grads_v, acc_ref, tile_sem, part_sem) = refs[: len(split)], refs[len(split) :]
    sources = sum(split)
    col_tiles = out_refs[0].shape[1]

    copies, part = [], 0
    for i, firsts in enumerate(layout):
        base = dest_ref[i] * col_tiles
        for first in firsts:
            size = grad_refs[part].shape[0]
            copies.append(
                pltpu.make_async_copy(
                    grad_refs[part], grads_v.at[pl.ds(base + first, size)], part_sem.at[part]
                )
            )
            part += 1
    tile_copies = [
        pltpu.make_async_copy(tiles_ref.at[order_ref[i]], tiles_v.at[i], tile_sem.at[i])
        for i in range(sources)
    ]
    for copy in copies + tile_copies:
        copy.start()
    for copy in copies:
        copy.wait()

    spots = [(n, m) for n, size in enumerate(split) for m in range(size)]
    for i in range(sources):
        for t in range(col_tiles + 1):
            acc_ref[t] = jnp.zeros(acc_ref.shape[1:], F32)
        tile_copies[i].wait()
        source = order_ref[i]
        count = counts_ref[source]

        def add_group(g, carry, i=i, source=source, count=count):
            products, where = [], []
            for j in range(GROUP):
                k = g * GROUP + j
                products.append(
                    lax.dot_general(
                        tiles_v[i, k],
                        grads_v[rows_ref[source, k]],
                        (((0,), (0,)), ((), ())),
                        preferred_element_type=F32,
                    )
                )
                where.append(jnp.where(k < count, cols_ref[source, k], col_tiles))
            for j in range(GROUP):
                acc_ref[where[j]] += products[j]
            return carry

        lax.fori_loop(0, (count + GROUP - 1) // GROUP, add_group, 0)
        n, m = spots[i]
        for t in range(col_tiles):
            out_refs[n][m, t] = acc_ref[t].astype(BF16)


def backward_tiles(split, order, dests, rows, cols, counts, tiles, grads):
    arrays = [array for parts in grads for _, array in parts]
    layout = tuple(tuple(first for first, _ in parts) for parts in grads)
    _, slots, tile, _ = tiles.shape
    sources = sum(split)
    col_tiles, width = CUTS[-1], arrays[0].shape[2]
    return pl.pallas_call(
        functools.partial(backward_kernel, layout, split),
        in_specs=[SMEM] * 5 + [ANY] * (1 + len(arrays)),
        out_specs=[VMEM] * len(split),
        out_shape=[jax.ShapeDtypeStruct((n, col_tiles, tile, width), BF16) for n in split],
        scratch_shapes=[
            pltpu.VMEM((sources, slots, tile, tile), BF16),
            pltpu.VMEM((col_tiles * len(PLACES), tile, width), BF16),
            pltpu.VMEM((col_tiles + 1, tile, width), F32),
            pltpu.SemaphoreType.DMA((sources,)),
            pltpu.SemaphoreType.DMA((len(arrays),)),
        ],
        compiler_params=pltpu.CompilerParams(vmem_limit_bytes=VMEM_LIMIT),
        cost_estimate=pl.CostEstimate(flops=3 * 10**9, bytes_accessed=20 * 2**20, transcendentals=0),
        name="backward_tiles",
    )(order, dests, rows, cols, counts, tiles, *arrays)


def copies_of_all(value, axis):
    count = lax.axis_size(axis)
    return lax.all_to_all(jnp.broadcast_to(value[None], (count, *value.shape)), axis, 0, 0)


def sum_over_all(value):
    value = jnp.sum(copies_of_all(value, "rep"), axis=0)
    return jnp.sum(copies_of_all(value, "blk"), axis=0)


def on_device(
    features,
    weight,
    norm_gain,
    norm_shift,
    tile_values,
    tile_rows,
    tile_cols,
    tile_counts,
    cotangent,
):
    tiles, rows, cols, counts = tile_values[0], tile_rows[0], tile_cols[0], tile_counts[0]
    local_rows, width = features.shape
    tile = tiles.shape[-1]
    col_tiles = local_rows // tile
    blk_count = lax.axis_size("blk")
    rep_count = lax.axis_size("rep")
    node_count = local_rows * blk_count * rep_count
    blk, rep = lax.axis_index("blk"), lax.axis_index("rep")
    z, y_low, core = blk // 4, (blk // 2) % 2, blk % 2
    y_high, x = rep // RING, rep % RING
    own_core = jnp.stack([blk_index(z + a + RING, y_low + b, core) for a, b in PLACES])
    other_core = own_core + (1 - 2 * core)
    dests = jnp.stack([rep_index(x + a + RING, y_high + b) for a, b in PLACES])
    *blk_tree, across = blk_links()
    rep_tree = rep_links()

    mine = gather_tree(features.reshape(col_tiles, tile, width), *blk_tree)
    theirs = [[(first, across(array)) for first, array in parts] for parts in mine]
    backwards = slice(None, None, -1)
    *blocks, offset = forward_tiles(
        jnp.stack([own_core[backwards], other_core[backwards]], axis=1).reshape(-1),
        dests,
        rows,
        cols,
        counts,
        tiles,
        [parts for both in zip(mine[backwards], theirs[backwards]) for parts in both],
    )
    shifted = scatter_tree(dict(zip(PLACES, blocks)), *rep_tree).reshape(local_rows, width)
    aggregate = shifted.astype(BF16)
    projected = jnp.dot(aggregate, weight, preferred_element_type=F32)
    own_mean = jnp.sum(projected, axis=0) / local_rows
    own_square = jnp.sum((projected - own_mean) ** 2, axis=0)
    moved = jnp.dot(offset, weight.astype(F32), precision=lax.Precision.HIGHEST)
    group = copies_of_all(jnp.stack([own_mean, own_square, moved[0], offset[0]]), "rep")
    group_mean = jnp.sum(group[:, 0], axis=0) / rep_count
    group_square = jnp.sum(group[:, 1], axis=0) + local_rows * jnp.sum(
        (group[:, 0] - group_mean) ** 2, axis=0
    )
    group_moved = jnp.sum(group[:, 2], axis=0)
    group_offset = jnp.sum(group[:, 3], axis=0)
    everyone = copies_of_all(jnp.stack([group_mean + group_moved, group_square]), "blk")
    feat_mean = jnp.sum(everyone[:, 0], axis=0) / blk_count
    square_sum = jnp.sum(everyone[:, 1], axis=0) + local_rows * rep_count * jnp.sum(
        (everyone[:, 0] - feat_mean) ** 2, axis=0
    )
    inv_std = lax.rsqrt(square_sum / node_count + norm_eps)
    normed = (projected + (group_moved - feat_mean)) * inv_std
    affine = norm_gain * normed + norm_shift
    gate_value = jax.nn.sigmoid(affine)
    output = (affine * gate_value).astype(BF16)
    grad_affine = cotangent.astype(F32) * gate_value * (1.0 + affine * (1.0 - gate_value))
    grad_beta, grad_gamma = sum_over_all(
        jnp.stack([jnp.sum(grad_affine, axis=0), jnp.sum(grad_affine * normed, axis=0)])
    )
    grad_summed = (
        norm_gain
        * inv_std
        * (grad_affine - grad_beta / node_count - normed * grad_gamma / node_count)
    ).astype(BF16)

    sent = lax.dot_general(
        grad_summed, weight, (((1,), (1,)), ((), ())), preferred_element_type=F32
    ).astype(BF16)
    grads = gather_tree(sent.reshape(col_tiles, tile, width), *rep_tree)
    products = {}
    for low, high, cuts in ((0, 4, (1, 3)), (4, 8, (4,))):
        order = jnp.concatenate([other_core[low:high], own_core[low:high]])
        given_kept = backward_tiles(
            (*cuts, high - low), order, dests, rows, cols, counts, tiles, grads
        )
        kept, given = given_kept[-1], given_kept[:-1]
        taken = [(array, n) for block in given for array in [across(block)] for n in range(block.shape[0])]
        for i, place in enumerate(PLACES[low:high]):
            array, n = taken[i]
            products[place] = kept[i].astype(F32) + array[n].astype(F32)
    grad_x = scatter_tree(products, *blk_tree).astype(BF16).reshape(local_rows, width)

    weight_term = lax.dot_general(
        aggregate, grad_summed, (((0,), (0,)), ((), ())), preferred_element_type=F32
    ) + group_offset[:, None] * jnp.sum(grad_summed.astype(F32), axis=0)
    pieces = lax.all_to_all(weight_term.reshape(blk_count, -1, width), "blk", 0, 0)
    piece = jnp.sum(copies_of_all(jnp.sum(pieces, axis=0), "rep"), axis=0)
    grad_w = copies_of_all(piece, "blk").reshape(weight.shape)
    return (output, grad_x, grad_w, grad_gamma, grad_beta)


def solution(mesh):
    return jax.shard_map(
        on_device,
        mesh=mesh,
        in_specs=(
            P(("blk", "rep"), None),
            P(),
            P(),
            P(),
            P("blk", "rep", None, None, None),
            P("blk", "rep", None),
            P("blk", "rep", None),
            P("blk", "rep"),
            P(("blk", "rep"), None),
        ),
        out_specs=(P(("blk", "rep"), None), P(("blk", "rep"), None), P(), P(), P()),
        check_vma=False,
    )
```

time: 1360 us -> 303 us (0.22)
  other arithmetic: 394 us -> 14.9 us
  waiting for transfers between devices: 456 us -> 79.2 us
  local copies, waits for them, and re-layouts: 166 us -> 8.95 us
  matrix products: 132 us -> 1.88 us
  blocking collectives: 191 us -> 78.3 us
  Pallas kernels: 0 us -> 59.2 us
  starting transfers between devices: 0.39 us -> 59.2 us
    scatter-add x32 -> x0, other arithmetic: 312 us -> none  [the longest x16 160 us: forward_visit_source(): return summed_terms.at[row_index].add(product)]
    reduce_scatter x2 -> x0, waiting for transfers between devices: 211 us -> none  [the longest x1 116 us: on_device(): lax.psum_scatter(partial_sums, 'rep', scatter_dimension=0, tiled=True)]
    psum x3 -> x0, blocking collectives: 191 us -> none  [the longest x1 64.7 us: on_device(): feat_sum = lax.psum(jnp.sum(summed, axis=0), ('blk', 'rep'))]
    psum x1 -> x0, waiting for transfers between devices: 143 us -> none  [on_device(): grad_w = lax.psum(weight_term, ('blk', 'rep'))]
    dot_general x35 -> x4, matrix products: 132 us -> 1.88 us  [the longest x1 1.04 us: on_device(): lax.dot_general(aggregate, grad_summed, (((0,), (0,)), ((), ())), preferr...]
    gather x32 -> x0, local copies, waits for them, and re-layouts: 111 us -> none  [the longest x16 65 us: forward_visit_source(): jnp.take(segment, jnp.clip(local_index, 0, seg_rows - 1), axis=0)]
    all_gather x2 -> x0, waiting for transfers between devices: 102 us -> none  [the longest x1 55.9 us: on_device(): segment = lax.all_gather(proj_tiles, 'blk', axis=0, tiled=True)]
    ppermute x0 -> x49, waiting for transfers between devices: none -> 79.2 us  [the longest x18 51.7 us: link(): return lambda value: lax.ppermute(value, 'rep', pairs)]
  transfers between devices with their start and end apart: 5 -> 50, of which waited for: 5 -> 19; matrix products, arithmetic and copies ran while one was open for 2% -> 6% of each run, Pallas kernels for 0% -> 6%
where the time goes in v2:
time: 303 us
  waiting for transfers between devices  79.2 us (26%)
  blocking collectives  78.3 us (26%)
  starting transfers between devices  59.2 us (20%)
  Pallas kernels  59.2 us (20%)
  other arithmetic  14.9 us (5%)
  local copies, waits for them, and re-layouts  8.95 us (3%)
    all_to_all x6, blocking collectives, copies_of_all(): lax.all_to_all(jnp.broadcast_to(value[None], (count, *value.shape)), axis...  78.3 us
    ppermute x18, waiting for transfers between devices, link(): return lambda value: lax.ppermute(value, 'rep', pairs)  51.7 us
    pallas_call x2, Pallas kernels, backward_tiles(): pl.pallas_call(functools.partial(backward_kernel, layout, split), in_spec...  35.6 us
    ppermute x31, starting transfers between devices, link(): return lambda value: lax.ppermute(value, 'blk', pairs)  32 us
    ppermute x31, waiting for transfers between devices, link(): return lambda value: lax.ppermute(value, 'blk', pairs)  27.5 us
    pallas_call x1, Pallas kernels, forward_tiles(): pl.pallas_call(functools.partial(forward_kernel, layout), in_specs=[SMEM]...  23.6 us
    ppermute x18, starting transfers between devices, link(): return lambda value: lax.ppermute(value, 'rep', pairs)  20 us
    all_to_all x1, starting transfers between devices, on_device(): lax.all_to_all(weight_term.reshape(blk_count, -1, width), 'blk', 0, 0)  7.27 us
  transfers between devices with their start and end apart: 50, of which 19 were waited for; matrix products, arithmetic and copies ran while one was open for 6% of the time, Pallas kernels for 6%

profile of v2, /device:TPU:1, one launch (start us, length us, event | category | flops | bytes accessed | tf_op | source)
XLA Modules:
  0.0 303.0 jit_solution(2426112158653492858)
XLA Ops:
  0.6 2.5 collective-permute-start.1
  7.7 9.5 %collective-permute-done.1.refs_2_ = bf16[8,128,256]{2,1,0:T(8,128)(2,1)S(1)} collective-permute-done((bf16[8,128,256]{2,1,0:T(8,128)(2,1)}, bf16[8,128,256]{2,1,0:T(8,128)(2,1)S(1)}, u32[]{:S(2)}, u32[]{:S(2)}) %collective-permute-start.1) | collective-permute-done | bytes 524320 | tf_op jit(solution)/shard_map/ppermute | solution.py:35
  18.5 2.7 collective-permute-start.11
  23.3 7.2 %collective-permute-done.7.refs_8_ = bf16[8,128,256]{2,1,0:T(8,128)(2,1)S(1)} collective-permute-done((bf16[8,128,256]{2,1,0:T(8,128)(2,1)S(1)}, bf16[8,128,256]{2,1,0:T(8,128)(2,1)S(1)}, u32[]{:S(2)}, u32[]{:S(2)}) %collective-permute-start.7) | collective-permute-done | bytes 524320 | tf_op jit(solution)/shard_map/ppermute | solution.py:35
  30.6 2.2 collective-permute-start.6
  35.0 2.6 collective-permute-start.14
  45.4 23.6 %forward_tiles.1 = (bf16[8,128,256]{2,1,0:T(8,128)(2,1)}, bf16[8,128,256]{2,1,0:T(8,128)(2,1)}, bf16[8,128,256]{2,1,0:T(8,128)(2,1)}, bf16[8,128,256]{2,1,0:T(8,...) custom-call(s32[16]{0:T(128)} %reshape.136.order_ref, ...), custom_call_target="tpu_custom_call" | custom-call | flops 6000000000 | bytes 31457280 | tf_op jit(solution)/shard_map/forward_tiles/pallas_call | solution.py:165
  73.5 2.6 collective-permute-start.20
  78.2 2.7 collective-permute-start.21
  81.0 2.7 collective-permute-start.23
  83.7 8.4 %collective-permute-done.26 = bf16[8,128,256]{2,1,0:T(8,128)(2,1)S(1)} collective-permute-done((bf16[8,128,256]{2,1,0:T(8,128)(2,1)S(1)}, bf16[8,128,256]{2,1,0:T(8,128)(2,1)S(1)}, u32[]{:S(2)}, u32[]{:S(2)}) %collective-permute-start.26) | collective-permute-done | bytes 524320 | tf_op jit(solution)/shard_map/ppermute | solution.py:45
  94.5 2.3 collective-permute-start.24
  96.9 6.6 %collective-permute-done.19 = bf16[8,128,256]{2,1,0:T(8,128)(2,1)S(1)} collective-permute-done((bf16[8,128,256]{2,1,0:T(8,128)(2,1)S(1)}, bf16[8,128,256]{2,1,0:T(8,128)(2,1)S(1)}, u32[]{:S(2)}, u32[]{:S(2)}) %collective-permute-start.19) | collective-permute-done | bytes 524320 | tf_op jit(solution)/shard_map/ppermute | solution.py:45
  106.0 11.1 %all_to_all.35 = f32[8,4,256]{2,1,0:T(4,128)S(1)} all-to-all(f32[8,4,256]{2,1,0:T(4,128)S(1)} %broadcast_in_dim.12), channel_id=1, replica_groups=mesh['blk'=16,'rep'=8] {'rep'}, dimensions={0} | all-to-all | bytes 65536 | tf_op jit(solution)/shard_map/all_to_all | solution.py:268
  117.2 16.8 %all_to_all.36 = f32[16,2,256]{2,1,0:T(2,128)S(1)} all-to-all(f32[16,2,256]{2,1,0:T(2,128)S(1)} %broadcast_in_dim.13), channel_id=1, replica_groups=mesh['blk'=16,'rep'=8] {'blk'}, dimensions={0} | all-to-all | bytes 65536 | tf_op jit(solution)/shard_map/all_to_all | solution.py:268
  134.8 9.2 %all_to_all.37 = f32[8,2,256]{2,1,0:T(2,128)S(1)} all-to-all(f32[8,2,256]{2,1,0:T(2,128)S(1)} %broadcast_in_dim.14), channel_id=1, replica_groups=mesh['blk'=16,'rep'=8] {'rep'}, dimensions={0} | all-to-all | bytes 32768 | tf_op jit(solution)/shard_map/all_to_all | solution.py:268
  144.1 10.1 %all_to_all.38 = f32[16,2,256]{2,1,0:T(2,128)S(1)} all-to-all(f32[16,2,256]{2,1,0:T(2,128)S(1)} %broadcast_in_dim.15), channel_id=1, replica_groups=mesh['blk'=16,'rep'=8] {'blk'}, dimensions={0} | all-to-all | bytes 65536 | tf_op jit(solution)/shard_map/all_to_all | solution.py:268
  157.3 13.7 %collective-permute-done.28.refs_8_ = bf16[8,128,256]{2,1,0:T(8,128)(2,1)S(1)} collective-permute-done((bf16[8,128,256]{2,1,0:T(8,128)(2,1)S(1)}, bf16[8,128,256]{2,1,0:T(8,128)(2,1)S(1)}, u32[]{:S(2)}, u32[]{:S(2)}) %collective-permute-start.28) | collective-permute-done | bytes 524320 | tf_op jit(solution)/shard_map/ppermute | solution.py:45
  171.3 2.5 collective-permute-start.32
  174.2 10.3 %collective-permute-done.29.refs_5_ = bf16[8,128,256]{2,1,0:T(8,128)(2,1)S(1)} collective-permute-done((bf16[8,128,256]{2,1,0:T(8,128)(2,1)S(1)}, bf16[8,128,256]{2,1,0:T(8,128)(2,1)S(1)}, u32[]{:S(2)}, u32[]{:S(2)}) %collective-permute-start.29) | collective-permute-done | bytes 524320 | tf_op jit(solution)/shard_map/ppermute | solution.py:45
  189.1 5.6 %collective-permute-done.36.refs_7_ = bf16[8,128,256]{2,1,0:T(8,128)(2,1)} collective-permute-done((bf16[8,128,256]{2,1,0:T(8,128)(2,1)S(1)}, bf16[8,128,256]{2,1,0:T(8,128)(2,1)}, u32[]{:S(2)}, u32[]{:S(2)}) %collective-permute-start.36) | collective-permute-done | bytes 524320 | tf_op jit(solution)/shard_map/ppermute | solution.py:45
  194.7 4.3 %collective-permute-done.33.refs_1_ = bf16[3,128,256]{2,1,0:T(8,128)(2,1)} collective-permute-done((bf16[3,128,256]{2,1,0:T(8,128)(2,1)}, bf16[3,128,256]{2,1,0:T(8,128)(2,1)}, u32[]{:S(2)}, u32[]{:S(2)}) %collective-permute-start.33) | collective-permute-done | bytes 196640 | tf_op jit(solution)/shard_map/ppermute | solution.py:45
  199.1 18.0 %backward_tiles.3 = (bf16[1,8,128,256]{3,2,1,0:T(8,128)(2,1)}, bf16[3,8,128,256]{3,2,1,0:T(8,128)(2,1)}, bf16[4,8,128,256]{3,2,1,0:T(8,128)(2,1)}) custom-call(s32[8]{0:T(128)} %concatenate.11.order_ref, s32[8]{0:T(128)} %stack.104.dest_ref, s32[16,32]{1,0:T(8,128)} %bitcast.118, s32[16,32]{1,0:T(8,128)} %bitcast.121, s32[16]{0:T(128)} %bitcast.125, ...), custom_call_target="tpu_custom_call" | custom-call | flops 3000000000 | bytes 20971520 | tf_op jit(solution)/shard_map/backward_tiles/pallas_call | solution.py:248
  218.7 17.6 %backward_tiles.2 = (bf16[4,8,128,256]{3,2,1,0:T(8,128)(2,1)}, bf16[4,8,128,256]{3,2,1,0:T(8,128)(2,1)}) custom-call(s32[8]{0:T(128)} %concatenate.10.order_ref, s32[8]{0:T(128)} %stack.104.dest_ref, s32[16,32]{1,0:T(8,128)} %bitcast.119, s32[16,32]{1,0:T(8,128)} %bitcast.122, s32[16]{0:T(128)} %bitcast.126, bf16[16,32,128,128]{3,2,1,0:T(8,128)(2,1)} %bitcast.102, ...), custom_call_target="tpu_custom_call" | custom-call | flops 3000000000 | bytes 20971520 | tf_op jit(solution)/shard_map/backward_tiles/pallas_call | solution.py:248
  239.4 3.3 %collective-permute-done.41 = bf16[2,128,256]{2,1,0:T(8,128)(2,1)S(1)} collective-permute-done((bf16[2,128,256]{2,1,0:T(8,128)(2,1)S(1)}, bf16[2,128,256]{2,1,0:T(8,128)(2,1)S(1)}, u32[]{:S(2)}, u32[]{:S(2)}) %collective-permute-start.41) | collective-permute-done | bytes 131104 | tf_op jit(solution)/shard_map/ppermute | solution.py:35
  243.9 3.0 fusion.3
  249.9 7.3 %all-to-all-start.4 = ((f32[16,16,256]{2,1,0:T(8,128)}), f32[16,16,256]{2,1,0:T(8,128)S(1)}, u32[]{:S(2)}, u32[]{:S(2)}) async-start(f32[16,16,256]{2,1,0:T(8,128)} %bitcast.47), calls=%async_computation.4 | async-start | bytes 524288 | tf_op jit(solution)/shard_map/all_to_all | solution.py:368
  257.2 2.6 collective-permute-done.44
  261.1 3.1 %fusion.5 = (bf16[8,128,256]{2,1,0:T(8,128)(2,1)}, bf16[8,128,256]{2,1,0:T(8,128)(2,1)}) fusion(bf16[8,128,256]{2,1,0:T(8,128)(2,1)S(1)} %collective-permute-done.44, bf16[8,128,256]{2,1,0:T(8,128)(2,1)} %collective-permute-done.42, bf16[4,8,128,256]{3,2,1,0:T(8,128)(2,1)} %collective-permute-done.37, bf16[4,8,128,256]{3,2,1,0:T(8,128)(2,1)S(1)} %copy-done.12, ...), kind=kLoop, calls=%fused_computation.12 | loop fusion | flops 3670016 | bytes 4718592 | tf_op jit(solution)/shard_map/convert_element_type | solution.py:87
  268.6 13.2 %all_to_all.39 = f32[8,16,256]{2,1,0:T(8,128)S(1)} all-to-all(f32[8,16,256]{2,1,0:T(8,128)S(1)} %broadcast_in_dim.16), channel_id=1, replica_groups=mesh['blk'=16,'rep'=8] {'rep'}, dimensions={0} | all-to-all | bytes 262144 | tf_op jit(solution)/shard_map/all_to_all | solution.py:268
  281.9 17.8 %all_to_all.40 = f32[16,16,256]{2,1,0:T(8,128)S(1)} all-to-all(f32[16,16,256]{2,1,0:T(8,128)S(1)} %broadcast_in_dim.17), channel_id=1, replica_groups=mesh['blk'=16,'rep'=8] {'blk'}, dimensions={0} | all-to-all | bytes 524288 | tf_op jit(solution)/shard_map/all_to_all | solution.py:268
  299.8 2.5 fusion.8
  (212 shorter events, 54.1 us)
Async XLA Ops:
  0.6 16.5 %collective-permute-start.1 = (bf16[8,128,256]{2,1,0:T(8,128)(2,1)}, bf16[8,128,256]{2,1,0:T(8,128)(2,1)S(1)}, u32[]{:S(2)}, u32[]{:S(2)}) collective-permute-start(bf16[8,128,256]{2,1,0:T(8,128)(2,1)} %bitcast.111), channel_id=1, source_target_pairs={{0,32},{8,40},{16,48},{24,56},{32,64},{40,72},{48,80},{56,88},{64,... | collective-permute-start | bytes 1572872 | tf_op jit(solution)/shard_map/ppermute | solution.py:35
  3.2 15.3 %collective-permute-start.5 = (bf16[8,128,256]{2,1,0:T(8,128)(2,1)}, bf16[8,128,256]{2,1,0:T(8,128)(2,1)S(1)}, u32[]{:S(2)}, u32[]{:S(2)}) collective-permute-start(bf16[8,128,256]{2,1,0:T(8,128)(2,1)} %bitcast.112), channel_id=1, source_target_pairs={{0,16},{8,24},{16,0},{24,8},{32,48},{40,56},{48,32},{56,40},{64,80... | collective-permute-start | bytes 1572872 | tf_op jit(solution)/shard_map/ppermute | solution.py:35
  4.5 16.7 %collective-permute-start = (bf16[8,128,256]{2,1,0:T(8,128)(2,1)}, bf16[8,128,256]{2,1,0:T(8,128)(2,1)S(1)}, u32[]{:S(2)}, u32[]{:S(2)}) collective-permute-start(bf16[8,128,256]{2,1,0:T(8,128)(2,1)} %bitcast.113), channel_id=1, source_target_pairs={{0,8},{8,0},{16,24},{24,16},{32,40},{40,32},{48,56},{56,48},{64,72... | collective-permute-start | bytes 1572872 | tf_op jit(solution)/shard_map/ppermute | solution.py:35
  5.7 17.5 %collective-permute-start.3 = (bf16[8,128,256]{2,1,0:T(8,128)(2,1)}, bf16[8,128,256]{2,1,0:T(8,128)(2,1)S(1)}, u32[]{:S(2)}, u32[]{:S(2)}) collective-permute-start(bf16[8,128,256]{2,1,0:T(8,128)(2,1)} %bitcast.114), channel_id=1, source_target_pairs={{0,96},{8,104},{16,112},{24,120},{32,0},{40,8},{48,16},{56,24},{64... | collective-permute-start | bytes 1572872 | tf_op jit(solution)/shard_map/ppermute | solution.py:35
  17.2 13.4 %collective-permute-start.7 = (bf16[8,128,256]{2,1,0:T(8,128)(2,1)S(1)}, bf16[8,128,256]{2,1,0:T(8,128)(2,1)S(1)}, u32[]{:S(2)}, u32[]{:S(2)}) collective-permute-start(bf16[8,128,256]{2,1,0:T(8,128)(2,1)S(1)} %collective-permute-done.1.refs_2_), channel_id=1, source_target_pairs={{0,32},{8,40},{16,48},{24,56},{32,64},{40,72},{48,80},{56,88},{64,... | collective-permute-start | bytes 1572872 | tf_op jit(solution)/shard_map/ppermute | solution.py:35
  17.2 15.6 %collective-permute-start.9 = (bf16[8,128,256]{2,1,0:T(8,128)(2,1)S(1)}, bf16[8,128,256]{2,1,0:T(8,128)(2,1)S(1)}, u32[]{:S(2)}, u32[]{:S(2)}) collective-permute-start(bf16[8,128,256]{2,1,0:T(8,128)(2,1)S(1)} %collective-permute-done.1.refs_2_), channel_id=1, source_target_pairs={{0,16},{8,24},{16,0},{24,8},{32,48},{40,56},{48,32},{56,40},{64,80... | collective-permute-start | bytes 1572872 | tf_op jit(solution)/shard_map/ppermute | solution.py:35
  18.5 15.7 %collective-permute-start.11 = (bf16[8,128,256]{2,1,0:T(8,128)(2,1)S(1)}, bf16[8,128,256]{2,1,0:T(8,128)(2,1)S(1)}, u32[]{:S(2)}, u32[]{:S(2)}) collective-permute-start(bf16[8,128,256]{2,1,0:T(8,128)(2,1)S(1)} %collective-permute-done.5.refs_6_), channel_id=1, source_target_pairs={{0,96},{8,104},{16,112},{24,120},{32,0},{40,8},{48,16},{56,24},{64... | collective-permute-start | bytes 1572872 | tf_op jit(solution)/shard_map/ppermute | solution.py:35
  21.2 13.9 %collective-permute-start.2 = (bf16[8,128,256]{2,1,0:T(8,128)(2,1)S(1)}, bf16[8,128,256]{2,1,0:T(8,128)(2,1)S(1)}, u32[]{:S(2)}, u32[]{:S(2)}) collective-permute-start(bf16[8,128,256]{2,1,0:T(8,128)(2,1)S(1)} %collective-permute-done.1.refs_2_), channel_id=1, source_target_pairs={{0,8},{8,0},{16,24},{24,16},{32,40},{40,32},{48,56},{56,48},{64,72... | collective-permute-start | bytes 1572872 | tf_op jit(solution)/shard_map/ppermute | solution.py:35
  23.2 14.4 %collective-permute-start.4 = (bf16[8,128,256]{2,1,0:T(8,128)(2,1)S(1)}, bf16[8,128,256]{2,1,0:T(8,128)(2,1)S(1)}, u32[]{:S(2)}, u32[]{:S(2)}) collective-permute-start(bf16[8,128,256]{2,1,0:T(8,128)(2,1)S(1)} %collective-permute-done.3.refs_4_), channel_id=1, source_target_pairs={{0,8},{8,0},{16,24},{24,16},{32,40},{40,32},{48,56},{56,48},{64,72... | collective-permute-start | bytes 1572872 | tf_op jit(solution)/shard_map/ppermute | solution.py:35
  78.0 14.2 %collective-permute-start.26 = (bf16[8,128,256]{2,1,0:T(8,128)(2,1)S(1)}, bf16[8,128,256]{2,1,0:T(8,128)(2,1)S(1)}, u32[]{:S(2)}, u32[]{:S(2)}) collective-permute-start(bf16[8,128,256]{2,1,0:T(8,128)(2,1)S(1)} %add_convert_fusion.4), channel_id=1, source_target_pairs={{0,1},{4,5},{1,2},{5,6},{2,3},{6,7},{3,0},{7,4},{8,9},{12,13},{9,1... | collective-permute-start | bytes 1572872 | tf_op jit(solution)/shard_map/ppermute | solution.py:45
  78.2 16.1 %collective-permute-start.21 = (bf16[8,128,256]{2,1,0:T(8,128)(2,1)S(1)}, bf16[8,128,256]{2,1,0:T(8,128)(2,1)S(1)}, u32[]{:S(2)}, u32[]{:S(2)}) collective-permute-start(bf16[8,128,256]{2,1,0:T(8,128)(2,1)S(1)} %add_convert_fusion.7), channel_id=1, source_target_pairs={{0,4},{4,0},{1,5},{5,1},{2,6},{6,2},{3,7},{7,3},{8,12},{12,8},{9,1... | collective-permute-start | bytes 1572872 | tf_op jit(solution)/shard_map/ppermute | solution.py:45
  81.0 13.2 %collective-permute-start.23 = (bf16[8,128,256]{2,1,0:T(8,128)(2,1)S(1)}, bf16[8,128,256]{2,1,0:T(8,128)(2,1)S(1)}, u32[]{:S(2)}, u32[]{:S(2)}) collective-permute-start(bf16[8,128,256]{2,1,0:T(8,128)(2,1)S(1)} %add_convert_fusion.6), channel_id=1, source_target_pairs={{0,3},{4,7},{1,0},{5,4},{2,1},{6,5},{3,2},{7,6},{8,11},{12,15},{9,... | collective-permute-start | bytes 1572872 | tf_op jit(solution)/shard_map/ppermute | solution.py:45
  83.7 19.7 %collective-permute-start.19 = (bf16[8,128,256]{2,1,0:T(8,128)(2,1)S(1)}, bf16[8,128,256]{2,1,0:T(8,128)(2,1)S(1)}, u32[]{:S(2)}, u32[]{:S(2)}) collective-permute-start(bf16[8,128,256]{2,1,0:T(8,128)(2,1)S(1)} %copy-done.35), channel_id=1, source_target_pairs={{0,1},{4,5},{1,2},{5,6},{2,3},{6,7},{3,0},{7,4},{8,9},{12,13},{9,1... | collective-permute-start | bytes 1572872 | tf_op jit(solution)/shard_map/ppermute | solution.py:45
  92.3 12.2 %collective-permute-start.27 = (bf16[8,128,256]{2,1,0:T(8,128)(2,1)S(1)}, bf16[8,128,256]{2,1,0:T(8,128)(2,1)S(1)}, u32[]{:S(2)}, u32[]{:S(2)}) collective-permute-start(bf16[8,128,256]{2,1,0:T(8,128)(2,1)S(1)} %add_convert_fusion.3), channel_id=1, source_target_pairs={{0,4},{4,0},{1,5},{5,1},{2,6},{6,2},{3,7},{7,3},{8,12},{12,8},{9,1... | collective-permute-start | bytes 1572872 | tf_op jit(solution)/shard_map/ppermute | solution.py:45
  94.5 10.6 %collective-permute-start.24 = (bf16[8,128,256]{2,1,0:T(8,128)(2,1)S(1)}, bf16[8,128,256]{2,1,0:T(8,128)(2,1)S(1)}, u32[]{:S(2)}, u32[]{:S(2)}) collective-permute-start(bf16[8,128,256]{2,1,0:T(8,128)(2,1)S(1)} %add_convert_fusion.5), channel_id=1, source_target_pairs={{0,3},{4,7},{1,0},{5,4},{2,1},{6,5},{3,2},{7,6},{8,11},{12,15},{9,... | collective-permute-start | bytes 1572872 | tf_op jit(solution)/shard_map/ppermute | solution.py:45
  156.6 14.4 %collective-permute-start.28 = (bf16[8,128,256]{2,1,0:T(8,128)(2,1)S(1)}, bf16[8,128,256]{2,1,0:T(8,128)(2,1)S(1)}, u32[]{:S(2)}, u32[]{:S(2)}) collective-permute-start(bf16[8,128,256]{2,1,0:T(8,128)(2,1)S(1)} %bitcast.103), channel_id=1, source_target_pairs={{0,1},{4,5},{1,2},{5,6},{2,3},{6,7},{3,0},{7,4},{8,9},{12,13},{9,1... | collective-permute-start | bytes 1572872 | tf_op jit(solution)/shard_map/ppermute | solution.py:45
  157.0 14.3 %collective-permute-start.31 = (bf16[8,128,256]{2,1,0:T(8,128)(2,1)S(1)}, bf16[8,128,256]{2,1,0:T(8,128)(2,1)S(1)}, u32[]{:S(2)}, u32[]{:S(2)}) collective-permute-start(bf16[8,128,256]{2,1,0:T(8,128)(2,1)S(1)} %bitcast.104), channel_id=1, source_target_pairs={{0,4},{4,0},{1,5},{5,1},{2,6},{6,2},{3,7},{7,3},{8,12},{12,8},{9,1... | collective-permute-start | bytes 1572872 | tf_op jit(solution)/shard_map/ppermute | solution.py:45
  171.0 13.4 %collective-permute-start.29 = (bf16[8,128,256]{2,1,0:T(8,128)(2,1)S(1)}, bf16[8,128,256]{2,1,0:T(8,128)(2,1)S(1)}, u32[]{:S(2)}, u32[]{:S(2)}) collective-permute-start(bf16[8,128,256]{2,1,0:T(8,128)(2,1)S(1)} %collective-permute-done.28.refs_8_), channel_id=1, source_target_pairs={{0,1},{4,5},{1,2},{5,6},{2,3},{6,7},{3,0},{7,4},{8,9},{12,13},{9,1... | collective-permute-start | bytes 1572872 | tf_op jit(solution)/shard_map/ppermute | solution.py:45
  171.3 14.1 %collective-permute-start.32 = (bf16[8,128,256]{2,1,0:T(8,128)(2,1)S(1)}, bf16[8,128,256]{2,1,0:T(8,128)(2,1)S(1)}, u32[]{:S(2)}, u32[]{:S(2)}) collective-permute-start(bf16[8,128,256]{2,1,0:T(8,128)(2,1)S(1)} %collective-permute-done.31.refs_6_), channel_id=1, source_target_pairs={{0,3},{4,7},{1,0},{5,4},{2,1},{6,5},{3,2},{7,6},{8,11},{12,15},{9,... | collective-permute-start | bytes 1572872 | tf_op jit(solution)/shard_map/ppermute | solution.py:45
  173.8 13.8 %collective-permute-start.34 = (bf16[8,128,256]{2,1,0:T(8,128)(2,1)S(1)}, bf16[8,128,256]{2,1,0:T(8,128)(2,1)S(1)}, u32[]{:S(2)}, u32[]{:S(2)}) collective-permute-start(bf16[8,128,256]{2,1,0:T(8,128)(2,1)S(1)} %collective-permute-done.28.refs_8_), channel_id=1, source_target_pairs={{0,4},{4,0},{1,5},{5,1},{2,6},{6,2},{3,7},{7,3},{8,12},{12,8},{9,1... | collective-permute-start | bytes 1572872 | tf_op jit(solution)/shard_map/ppermute | solution.py:45
  174.1 20.7 %collective-permute-start.36 = (bf16[8,128,256]{2,1,0:T(8,128)(2,1)S(1)}, bf16[8,128,256]{2,1,0:T(8,128)(2,1)}, u32[]{:S(2)}, u32[]{:S(2)}) collective-permute-start(bf16[8,128,256]{2,1,0:T(8,128)(2,1)S(1)} %bitcast.105), channel_id=1, source_target_pairs={{0,3},{4,7},{1,0},{5,4},{2,1},{6,5},{3,2},{7,6},{8,11},{12,15},{9,... | collective-permute-start | bytes 1572872 | tf_op jit(solution)/shard_map/ppermute | solution.py:45
  186.2 12.9 %collective-permute-start.33 = (bf16[3,128,256]{2,1,0:T(8,128)(2,1)}, bf16[3,128,256]{2,1,0:T(8,128)(2,1)}, u32[]{:S(2)}, u32[]{:S(2)}) collective-permute-start(bf16[3,128,256]{2,1,0:T(8,128)(2,1)} %slice.167), channel_id=1, source_target_pairs={{0,3},{4,7},{1,0},{5,4},{2,1},{6,5},{3,2},{7,6},{8,11},{12,15},{9,... | collective-permute-start | bytes 589832 | tf_op jit(solution)/shard_map/ppermute | solution.py:45
  217.1 26.7 %collective-permute-start.39 = (bf16[3,8,128,256]{3,2,1,0:T(8,128)(2,1)}, bf16[3,8,128,256]{3,2,1,0:T(8,128)(2,1)}, u32[]{:S(2)}, u32[]{:S(2)}) collective-permute-start(bf16[3,8,128,256]{3,2,1,0:T(8,128)(2,1)} %get-tuple-element.31), channel_id=1, source_target_pairs={{0,8},{8,0},{16,24},{24,16},{32,40},{40,32},{48,56},{56,48},{64,72... | collective-permute-start | bytes 4718600 | tf_op jit(solution)/shard_map/ppermute | solution.py:35
  218.6 17.7 %collective-permute-start.40 = (bf16[1,8,128,256]{3,2,1,0:T(8,128)(2,1)}, bf16[1,8,128,256]{3,2,1,0:T(8,128)(2,1)S(1)}, u32[]{:S(2)}, u32[]{:S(2)}) collective-permute-start(bf16[1,8,128,256]{3,2,1,0:T(8,128)(2,1)} %get-tuple-element.32), channel_id=1, source_target_pairs={{0,8},{8,0},{16,24},{24,16},{32,40},{40,32},{48,56},{56,48},{64,72... | collective-permute-start | bytes 1572872 | tf_op jit(solution)/shard_map/ppermute | solution.py:35
  236.3 24.8 %collective-permute-start.37 = (bf16[4,8,128,256]{3,2,1,0:T(8,128)(2,1)}, bf16[4,8,128,256]{3,2,1,0:T(8,128)(2,1)}, u32[]{:S(2)}, u32[]{:S(2)}) collective-permute-start(bf16[4,8,128,256]{3,2,1,0:T(8,128)(2,1)} %get-tuple-element.29), channel_id=1, source_target_pairs={{0,8},{8,0},{16,24},{24,16},{32,40},{40,32},{48,56},{56,48},{64,72... | collective-permute-start | bytes 6291464 | tf_op jit(solution)/shard_map/ppermute | solution.py:35
  246.9 12.9 %collective-permute-start.44 = (bf16[8,128,256]{2,1,0:T(8,128)(2,1)}, bf16[8,128,256]{2,1,0:T(8,128)(2,1)S(1)}, u32[]{:S(2)}, u32[]{:S(2)}) collective-permute-start(bf16[8,128,256]{2,1,0:T(8,128)(2,1)} %get-tuple-element.49), channel_id=1, source_target_pairs={{0,96},{8,104},{16,112},{24,120},{32,0},{40,8},{48,16},{56,24},{64... | collective-permute-start | bytes 1572872 | tf_op jit(solution)/shard_map/ppermute | solution.py:35
  248.2 12.1 %collective-permute-start.42 = (bf16[8,128,256]{2,1,0:T(8,128)(2,1)}, bf16[8,128,256]{2,1,0:T(8,128)(2,1)}, u32[]{:S(2)}, u32[]{:S(2)}) collective-permute-start(bf16[8,128,256]{2,1,0:T(8,128)(2,1)} %get-tuple-element.47), channel_id=1, source_target_pairs={{0,16},{8,24},{16,0},{24,8},{32,48},{40,56},{48,32},{56,40},{64,80... | collective-permute-start | bytes 1572872 | tf_op jit(solution)/shard_map/ppermute | solution.py:35
  248.9 12.2 %collective-permute-start.47 = (bf16[8,128,256]{2,1,0:T(8,128)(2,1)}, bf16[8,128,256]{2,1,0:T(8,128)(2,1)}, u32[]{:S(2)}, u32[]{:S(2)}) collective-permute-start(bf16[8,128,256]{2,1,0:T(8,128)(2,1)} %get-tuple-element.48), channel_id=1, source_target_pairs={{0,32},{8,40},{16,48},{24,56},{32,64},{40,72},{48,80},{56,88},{64,... | collective-permute-start | bytes 1572872 | tf_op jit(solution)/shard_map/ppermute | solution.py:35
  249.9 18.6 %all-to-all-start.4 = ((f32[16,16,256]{2,1,0:T(8,128)}), f32[16,16,256]{2,1,0:T(8,128)S(1)}, u32[]{:S(2)}, u32[]{:S(2)}) async-start(f32[16,16,256]{2,1,0:T(8,128)} %bitcast.47), calls=%async_computation.4 | async-start | bytes 524288 | tf_op jit(solution)/shard_map/all_to_all | solution.py:368
  264.2 35.6 %collective-permute-start.48 = (bf16[8,128,256]{2,1,0:T(8,128)(2,1)}, bf16[8,128,256]{2,1,0:T(8,128)(2,1)S(1)}, u32[]{:S(2)}, u32[]{:S(2)}) collective-permute-start(bf16[8,128,256]{2,1,0:T(8,128)(2,1)} %get-tuple-element.46), channel_id=1, source_target_pairs={{0,16},{8,24},{16,0},{24,8},{32,48},{40,56},{48,32},{56,40},{64,80... | collective-permute-start | bytes 1572872 | tf_op jit(solution)/shard_map/ppermute | solution.py:35
  265.9 33.9 %collective-permute-start.45 = (bf16[8,128,256]{2,1,0:T(8,128)(2,1)}, bf16[8,128,256]{2,1,0:T(8,128)(2,1)}, u32[]{:S(2)}, u32[]{:S(2)}) collective-permute-start(bf16[8,128,256]{2,1,0:T(8,128)(2,1)} %get-tuple-element.45), channel_id=1, source_target_pairs={{0,96},{8,104},{16,112},{24,120},{32,0},{40,8},{48,16},{56,24},{64... | collective-permute-start | bytes 1572872 | tf_op jit(solution)/shard_map/ppermute | solution.py:35
  267.9 31.9 %collective-permute-start.38 = (bf16[8,128,256]{2,1,0:T(8,128)(2,1)S(1)}, bf16[8,128,256]{2,1,0:T(8,128)(2,1)}, u32[]{:S(2)}, u32[]{:S(2)}) collective-permute-start(bf16[8,128,256]{2,1,0:T(8,128)(2,1)S(1)} %fusion.9), channel_id=1, source_target_pairs={{0,32},{8,40},{16,48},{24,56},{32,64},{40,72},{48,80},{56,88},{64,... | collective-permute-start | bytes 1572872 | tf_op jit(solution)/shard_map/ppermute | solution.py:35
  (54 other events, 803.7 us)

commit v3 on v2

v3 whole, which is shorter than its diff:
```python
import functools

import jax
import jax.numpy as jnp
from jax import lax
from jax.experimental import pallas as pl
from jax.experimental.pallas import tpu as pltpu
from jax.sharding import PartitionSpec as P

norm_eps = 1e-05
GROUP = 16
BF16, F32 = jnp.bfloat16, jnp.float32
VMEM_LIMIT = 56 * 2**20
RING = 4
PLACES = ((2, 1), (1, 1), (-1, 1), (2, 0), (0, 1), (1, 0), (-1, 0), (0, 0))
ANY = pl.BlockSpec(memory_space=pl.ANY)
VMEM = pl.BlockSpec(memory_space=pltpu.VMEM)
SMEM = pl.BlockSpec(memory_space=pltpu.SMEM)


def blk_index(z, y, core):
    return (z % RING) * 4 + (y % 2) * 2 + core % 2


def rep_index(x, y):
    return (y % 2) * RING + x % RING


def blk_links():
    spots = [(z, y, c) for z in range(RING) for y in range(2) for c in range(2)]

    def link(dz, dy, dc):
        pairs = [(blk_index(z, y, c), blk_index(z + dz, y + dy, c + dc)) for z, y, c in spots]
        return lambda value: lax.ppermute(value, "blk", pairs)

    return link(1, 0, 0), link(-1, 0, 0), link(0, 1, 0), link(0, 0, 1)


def rep_links():
    spots = [(x, y) for x in range(RING) for y in range(2)]

    def link(dx, dy):
        pairs = [(rep_index(x, y), rep_index(x + dx, y + dy)) for x, y in spots]
        return lambda value: lax.ppermute(value, "rep", pairs)

    return link(1, 0), link(-1, 0), link(0, 1)


def gather_tree(own, up, down, pair):
    half = own.shape[0] // 2
    below, above, beside = up(own), down(own), pair(own)
    below_beside, above_beside, far = pair(below), down(beside), up(below)
    far_beside = [(0, down(above_beside[:half])), (half, up(below_beside[half:]))]
    whole = {
        (0, 0): own,
        (-1, 0): below,
        (1, 0): above,
        (0, 1): beside,
        (-1, 1): below_beside,
        (1, 1): above_beside,
        (2, 0): far,
    }
    return [far_beside if place == (2, 1) else [(0, whole[place])] for place in PLACES]


def scatter_first(corner, blocks, up, down):
    low, high = corner
    half = low.shape[0]
    none = ((0, 0), (0, 0))
    above_beside = blocks[1, 1].astype(F32) + jnp.pad(
        up(low.astype(BF16)).astype(F32), ((0, half), *none)
    )
    below_beside = blocks[-1, 1].astype(F32) + jnp.pad(
        down(high.astype(BF16)).astype(F32), ((half, 0), *none)
    )
    return above_beside.astype(BF16), below_beside.astype(BF16), blocks[2, 0].astype(BF16)


def scatter_second(leaving, blocks, up, down, pair):
    above_beside, below_beside, far = leaving
    below = blocks[-1, 0].astype(F32) + pair(below_beside).astype(F32) + down(far).astype(F32)
    beside = blocks[0, 1].astype(F32) + up(above_beside).astype(F32)
    return below.astype(BF16), beside.astype(BF16), blocks[1, 0].astype(BF16)


def scatter_third(leaving, own, up, down, pair):
    below, beside, above = leaving
    return (
        own.astype(F32)
        + up(above).astype(F32)
        + down(below).astype(F32)
        + pair(beside).astype(F32)
    )


def run_list(first, last, spare, tile_list, panel_list, key_list, multiply, acc_ref):
    def add_group(g, carry):
        products = [
            multiply(tile_list[g * GROUP + j], panel_list[g * GROUP + j]) for j in range(GROUP)
        ]
        for j in range(GROUP):
            acc_ref[key_list[g * GROUP + j]] += products[j]
        return carry

    lax.fori_loop(first, last, add_group, 0)


def zero_all(acc_ref):
    def zero(i, carry):
        acc_ref[i] = jnp.zeros(acc_ref.shape[1:], F32)
        return carry

    lax.fori_loop(0, acc_ref.shape[0], zero, 0)


def fill_tail(count, spare, tile_list, panel_list, key_list):
    for j in range(GROUP):
        tile_list[count + j] = 0
        panel_list[count + j] = 0
        key_list[count + j] = spare


def forward_kernel(layout, low, high, waits, order_ref, dest_ref, rows_ref, cols_ref, counts_ref, tiles_ref, *refs):
    first_call = low == 0
    sources = len(layout)
    slots = rows_ref.shape[1]
    parts = sum(len(firsts) for firsts in layout)
    shard_refs, refs = refs[:parts], refs[parts + waits :]
    if not first_call:
        given_offset_ref, refs = refs[0], refs[1:]
    places = high - low
    outs = places + 2 * first_call
    out_refs, refs = refs[:outs], refs[outs:]
    tiles_v, shards_v, acc_ref, tile_list, panel_list, key_list, place_of, tile_sem, part_sem = refs
    col_tiles = out_refs[-2].shape[0]
    row_tiles = places * col_tiles

    copies, part = [], 0
    for i, firsts in enumerate(layout):
        own = [
            pltpu.make_async_copy(
                tiles_ref.at[order_ref[i]], tiles_v.at[pl.ds(i * slots, slots)], tile_sem.at[i]
            )
        ]
        for first in firsts:
            size = shard_refs[part].shape[0]
            own.append(
                pltpu.make_async_copy(
                    shard_refs[part],
                    shards_v.at[pl.ds(i * col_tiles + first, size)],
                    part_sem.at[part],
                )
            )
            part += 1
        for copy in own:
            copy.start()
        copies.append(own)

    zero_all(acc_ref)
    for d in range(len(PLACES)):
        place_of[dest_ref[d]] = d - low
    count, ends = jnp.int32(0), []
    for i in range(sources):
        source = order_ref[i]

        def enlist(k, count, i=i, source=source):
            row = rows_ref[source, k]
            place = place_of[row // col_tiles]
            tile_list[count] = i * slots + k
            panel_list[count] = i * col_tiles + cols_ref[source, k]
            key_list[count] = place * col_tiles + row % col_tiles
            return count + jnp.where((place >= 0) & (place < places), 1, 0)

        count = lax.fori_loop(0, counts_ref[source], enlist, count)
        ends.append(count)
    fill_tail(count, row_tiles, tile_list, panel_list, key_list)

    def multiply(tile, panel):
        return jnp.dot(tiles_v[tile], shards_v[panel], preferred_element_type=F32)

    lists = (row_tiles, tile_list, panel_list, key_list, multiply, acc_ref)
    for own in copies[: sources // 2]:
        for copy in own:
            copy.wait()
    middle = ends[sources // 2 - 1] // GROUP
    run_list(0, middle, *lists)
    for own in copies[sources // 2 :]:
        for copy in own:
            copy.wait()
    run_list(middle, (count + GROUP - 1) // GROUP, *lists)

    if first_call:

        def total(i, carry):
            return carry + jnp.sum(acc_ref[i].reshape(-1, 8, acc_ref.shape[2]), axis=0)

        sums = lax.fori_loop(0, row_tiles, total, jnp.zeros((8, acc_ref.shape[2]), F32))
        offset = jnp.sum(sums, axis=0, keepdims=True) / (row_tiles * acc_ref.shape[1])
        out_refs[-1][...] = offset
        half = col_tiles // 2
        spans = [(out_refs[0], 0, half), (out_refs[1], half, half)]
        spans += [(out_refs[d + 1], d * col_tiles, col_tiles) for d in range(1, places)]
    else:
        offset = given_offset_ref[...]
        spans = [(out_refs[d], d * col_tiles, col_tiles) for d in range(places)]
    for out_ref, base, size in spans:

        def put(i, carry, out_ref=out_ref, base=base):
            out_ref[i] = (acc_ref[base + i] - offset).astype(BF16)
            return carry

        lax.fori_loop(0, size, put, 0)


def forward_tiles(low, high, order, dests, rows, cols, counts, tiles, shards, offset=None, after=()):
    arrays = [array for parts in shards for _, array in parts]
    layout = tuple(tuple(first for first, _ in parts) for parts in shards)
    sources, slots, tile, _ = tiles.shape
    width = arrays[0].shape[2]
    col_tiles = arrays[0].shape[0]
    places = high - low
    cap = sources * slots + GROUP
    sizes = [col_tiles] * places
    out_shape = [jax.ShapeDtypeStruct((size, tile, width), BF16) for size in sizes]
    if low == 0:
        halves = [jax.ShapeDtypeStruct((col_tiles // 2, tile, width), BF16)] * 2
        out_shape = halves + out_shape[1:] + [jax.ShapeDtypeStruct((1, width), F32)]
    given = [] if low == 0 else [offset]
    return pl.pallas_call(
        functools.partial(forward_kernel, layout, low, high, len(after)),
        in_specs=[SMEM] * 5 + [ANY] * (1 + len(arrays) + len(after)) + [VMEM] * len(given),
        out_specs=[VMEM] * len(out_shape),
        out_shape=out_shape,
        scratch_shapes=[
            pltpu.VMEM((sources * slots, tile, tile), BF16),
            pltpu.VMEM((sources * col_tiles, tile, width), BF16),
            pltpu.VMEM((places * col_tiles + 1, tile, width), F32),
            pltpu.SMEM((cap,), jnp.int32),
            pltpu.SMEM((cap,), jnp.int32),
            pltpu.SMEM((cap,), jnp.int32),
            pltpu.SMEM((len(PLACES),), jnp.int32),
            pltpu.SemaphoreType.DMA((sources,)),
            pltpu.SemaphoreType.DMA((len(arrays),)),
        ],
        compiler_params=pltpu.CompilerParams(vmem_limit_bytes=VMEM_LIMIT),
        cost_estimate=pl.CostEstimate(flops=3 * 10**9, bytes_accessed=30 * 2**20, transcendentals=0),
        name="forward_tiles",
    )(order, dests, rows, cols, counts, tiles, *arrays, *after, *given)


def backward_kernel(layout, split, waits, order_ref, dest_ref, rows_ref, cols_ref, counts_ref, tiles_ref, *refs):
    parts = sum(len(firsts) for firsts in layout)
    grad_refs, refs = refs[:parts], refs[parts + waits :]
    out_refs, refs = refs[: len(split)], refs[len(split) :]
    tiles_v, grads_v, acc_ref, tile_list, panel_list, key_list, tile_sem, part_sem = refs
    sources = sum(split)
    slots = rows_ref.shape[1]
    col_tiles = out_refs[0].shape[1]

    copies, part = [], 0
    for i, firsts in enumerate(layout):
        base = dest_ref[i] * col_tiles
        for first in firsts:
            size = grad_refs[part].shape[0]
            copies.append(
                pltpu.make_async_copy(
                    grad_refs[part], grads_v.at[pl.ds(base + first, size)], part_sem.at[part]
                )
            )
            part += 1
    tile_copies = [
        pltpu.make_async_copy(
            tiles_ref.at[order_ref[i]], tiles_v.at[pl.ds(i * slots, slots)], tile_sem.at[i]
        )
        for i in range(sources)
    ]
    for copy in copies + tile_copies:
        copy.start()

    zero_all(acc_ref)
    count, ends = jnp.int32(0), []
    for i in range(sources):
        source = order_ref[i]

        def enlist(k, count, i=i, source=source):
            tile_list[count] = i * slots + k
            panel_list[count] = rows_ref[source, k]
            key_list[count] = i * col_tiles + cols_ref[source, k]
            return count + 1

        count = lax.fori_loop(0, counts_ref[source], enlist, count)
        ends.append(count)
    fill_tail(count, sources * col_tiles, tile_list, panel_list, key_list)

    def multiply(tile, panel):
        return lax.dot_general(
            tiles_v[tile], grads_v[panel], (((0,), (0,)), ((), ())), preferred_element_type=F32
        )

    lists = (sources * col_tiles, tile_list, panel_list, key_list, multiply, acc_ref)
    for copy in copies + tile_copies[: sources // 2]:
        copy.wait()
    middle = ends[sources // 2 - 1] // GROUP
    run_list(0, middle, *lists)
    for copy in tile_copies[sources // 2 :]:
        copy.wait()
    run_list(middle, (count + GROUP - 1) // GROUP, *lists)

    first = 0
    for n, size in enumerate(split):
        for m in range(size):

            def put(t, carry, n=n, m=m, base=(first + m) * col_tiles):
                out_refs[n][m, t] = acc_ref[base + t].astype(BF16)
                return carry

            lax.fori_loop(0, col_tiles, put, 0)
        first += size


def backward_tiles(split, order, dests, rows, cols, counts, tiles, grads, after=()):
    arrays = [array for parts in grads for _, array in parts]
    layout = tuple(tuple(first for first, _ in parts) for parts in grads)
    _, slots, tile, _ = tiles.shape
    sources = sum(split)
    width = arrays[0].shape[2]
    row_tiles = sum(array.shape[0] for array in arrays)
    col_tiles = row_tiles // len(PLACES)
    cap = sources * slots + GROUP
    return pl.pallas_call(
        functools.partial(backward_kernel, layout, split, len(after)),
        in_specs=[SMEM] * 5 + [ANY] * (1 + len(arrays) + len(after)),
        out_specs=[VMEM] * len(split),
        out_shape=[jax.ShapeDtypeStruct((n, col_tiles, tile, width), BF16) for n in split],
        scratch_shapes=[
            pltpu.VMEM((sources * slots, tile, tile), BF16),
            pltpu.VMEM((row_tiles, tile, width), BF16),
            pltpu.VMEM((sources * col_tiles + 1, tile, width), F32),
            pltpu.SMEM((cap,), jnp.int32),
            pltpu.SMEM((cap,), jnp.int32),
            pltpu.SMEM((cap,), jnp.int32),
            pltpu.SemaphoreType.DMA((sources,)),
            pltpu.SemaphoreType.DMA((len(arrays),)),
        ],
        compiler_params=pltpu.CompilerParams(vmem_limit_bytes=VMEM_LIMIT),
        cost_estimate=pl.CostEstimate(flops=3 * 10**9, bytes_accessed=20 * 2**20, transcendentals=0),
        name="backward_tiles",
    )(order, dests, rows, cols, counts, tiles, *arrays, *after)


def sum_first_kernel(value_ref, *refs):
    refs[-1][...] = jnp.sum(value_ref[...], axis=0)


def sum_first(value, after):
    return pl.pallas_call(
        sum_first_kernel,
        in_specs=[VMEM] + [ANY] * len(after),
        out_specs=VMEM,
        out_shape=jax.ShapeDtypeStruct(value.shape[1:], value.dtype),
        name="sum_first",
    )(value, *after)


def weight_kernel(aggregate_ref, grad_ref, offset_ref, *refs):
    grads = grad_ref[...]
    sums = jnp.sum(grads.astype(F32), axis=0, keepdims=True)
    refs[-1][...] = (
        lax.dot_general(
            aggregate_ref[...], grads, (((0,), (0,)), ((), ())), preferred_element_type=F32
        )
        + offset_ref[...] * sums
    )


def weight_terms(aggregate, grads, offset, after):
    width = grads.shape[1]
    return pl.pallas_call(
        weight_kernel,
        in_specs=[VMEM] * 3 + [ANY] * len(after),
        out_specs=VMEM,
        out_shape=jax.ShapeDtypeStruct((width, width), F32),
        name="weight_terms",
    )(aggregate, grads, jnp.broadcast_to(offset[:, None], (width, width)), *after)


def copies_of_all(value, axis):
    count = lax.axis_size(axis)
    return lax.all_to_all(jnp.broadcast_to(value[None], (count, *value.shape)), axis, 0, 0)


def on_device(
    features,
    weight,
    norm_gain,
    norm_shift,
    tile_values,
    tile_rows,
    tile_cols,
    tile_counts,
    cotangent,
):
    tiles, rows, cols, counts = tile_values[0], tile_rows[0], tile_cols[0], tile_counts[0]
    local_rows, width = features.shape
    tile = tiles.shape[-1]
    col_tiles = local_rows // tile
    blk_count = lax.axis_size("blk")
    rep_count = lax.axis_size("rep")
    node_count = local_rows * blk_count * rep_count
    blk, rep = lax.axis_index("blk"), lax.axis_index("rep")
    z, y_low, core = blk // 4, (blk // 2) % 2, blk % 2
    y_high, x = rep // RING, rep % RING
    own_core = jnp.stack([blk_index(z + a + RING, y_low + b, core) for a, b in PLACES])
    other_core = own_core + (1 - 2 * core)
    dests = jnp.stack([rep_index(x + a + RING, y_high + b) for a, b in PLACES])
    *blk_tree, across = blk_links()
    rep_tree = rep_links()

    mine = gather_tree(features.reshape(col_tiles, tile, width), *blk_tree)
    theirs = [[(first, across(array)) for first, array in parts] for parts in mine]
    backwards = slice(None, None, -1)
    lists = (dests, rows, cols, counts, tiles)
    order = jnp.stack([own_core[backwards], other_core[backwards]], axis=1).reshape(-1)
    shards = [parts for both in zip(mine[backwards], theirs[backwards]) for parts in both]
    up, down, pair = rep_tree
    *corner, above_beside, below_beside, far, offset = forward_tiles(0, 4, order, *lists, shards)
    blocks = {(1, 1): above_beside, (-1, 1): below_beside, (2, 0): far}
    leaving = scatter_first(corner, blocks, up, down)
    blocks.update(
        zip(PLACES[4:], forward_tiles(4, 8, order, *lists, shards, offset, [leaving[0][:1, :16, :128]]))
    )
    leaving = scatter_second(leaving, blocks, *rep_tree)
    shifted = scatter_third(leaving, blocks[0, 0], *rep_tree).reshape(local_rows, width)
    aggregate = shifted.astype(BF16)
    projected = jnp.dot(aggregate, weight, preferred_element_type=F32)
    own_mean = jnp.sum(projected, axis=0) / local_rows
    own_square = jnp.sum((projected - own_mean) ** 2, axis=0)
    moved = jnp.dot(offset, weight.astype(F32), precision=lax.Precision.HIGHEST)
    everyone = copies_of_all(
        jnp.stack([own_mean, own_square, moved[0], offset[0]]), ("blk", "rep")
    ).reshape(blk_count, rep_count, 4, width)
    moves = jnp.sum(everyone[:, :, 2], axis=1)
    means = everyone[:, :, 0] + moves[:, None]
    feat_mean = jnp.sum(means, axis=(0, 1)) / (blk_count * rep_count)
    square_sum = jnp.sum(everyone[:, :, 1], axis=(0, 1)) + local_rows * jnp.sum(
        (means - feat_mean) ** 2, axis=(0, 1)
    )
    group = lax.dynamic_index_in_dim(everyone, blk, 0, keepdims=False)
    group_moved, group_offset = jnp.sum(group[:, 2], axis=0), jnp.sum(group[:, 3], axis=0)
    inv_std = lax.rsqrt(square_sum / node_count + norm_eps)
    normed = (projected + (group_moved - feat_mean)) * inv_std
    affine = norm_gain * normed + norm_shift
    gate_value = jax.nn.sigmoid(affine)
    output = (affine * gate_value).astype(BF16)
    grad_affine = cotangent.astype(F32) * gate_value * (1.0 + affine * (1.0 - gate_value))
    grad_beta, grad_gamma = jnp.sum(
        copies_of_all(
            jnp.stack([jnp.sum(grad_affine, axis=0), jnp.sum(grad_affine * normed, axis=0)]),
            ("blk", "rep"),
        ),
        axis=0,
    )
    grad_summed = (
        norm_gain
        * inv_std
        * (grad_affine - grad_beta / node_count - normed * grad_gamma / node_count)
    ).astype(BF16)

    sent = lax.dot_general(
        grad_summed, weight, (((1,), (1,)), ((), ())), preferred_element_type=F32
    ).astype(BF16)
    grads = gather_tree(sent.reshape(col_tiles, tile, width), *rep_tree)
    arrived = {place: parts[0][1] for place, parts in zip(PLACES, grads)}
    weight_term = weight_terms(
        aggregate, grad_summed, group_offset, [arrived[1, 0]]
    )
    pieces = lax.all_to_all(weight_term.reshape(blk_count, -1, width), "blk", 0, 0)
    piece = sum_first(pieces, [arrived[-1, 1]])
    terms = copies_of_all(piece, "rep")

    def of_chip(low, high, cuts, after):
        order = jnp.concatenate([other_core[low:high], own_core[low:high]])
        *given, kept = backward_tiles((*cuts, high - low), order, *lists, grads, after)
        taken = [block for part in given for block in across(part)]
        return {
            place: kept[i].astype(F32) + taken[i].astype(F32)
            for i, place in enumerate(PLACES[low:high])
        }

    up, down, pair = blk_tree
    products = of_chip(0, 4, (1, 3), [terms])
    half = col_tiles // 2
    corner = products[2, 1]
    leaving = scatter_first((corner[:half], corner[half:]), products, up, down)
    products.update(of_chip(4, 8, (4,), [leaving[0][:1, :16, :128]]))
    leaving = scatter_second(leaving, products, *blk_tree)
    grad_w = copies_of_all(sum_first(terms, [leaving[0][:1, :16, :128]]), "blk").reshape(weight.shape)
    grad_x = scatter_third(leaving, products[0, 0], *blk_tree).astype(BF16)
    return (output, grad_x.reshape(local_rows, width), grad_w, grad_gamma, grad_beta)


def solution(mesh):
    return jax.shard_map(
        on_device,
        mesh=mesh,
        in_specs=(
            P(("blk", "rep"), None),
            P(),
            P(),
            P(),
            P("blk", "rep", None, None, None),
            P("blk", "rep", None),
            P("blk", "rep", None),
            P("blk", "rep"),
            P(("blk", "rep"), None),
        ),
        out_specs=(P(("blk", "rep"), None), P(("blk", "rep"), None), P(), P(), P()),
        check_vma=False,
    )
```

time: 303 us -> 296 us (0.977)
  blocking collectives: 78.3 us -> 29.1 us
  waiting for transfers between devices: 79.2 us -> 99.3 us
  starting transfers between devices: 59.2 us -> 69.1 us
  local copies, waits for them, and re-layouts: 8.95 us -> 13.3 us
  other arithmetic: 14.9 us -> 19.2 us
  Pallas kernels: 59.2 us -> 62.8 us
    all_to_all x6 -> x2, blocking collectives: 78.3 us -> 29.1 us  [copies_of_all(): lax.all_to_all(jnp.broadcast_to(value[None], (count, *value.shape)), axis...]
    ppermute x18 -> x16, waiting for transfers between devices: 51.7 us -> 28.3 us  [link(): return lambda value: lax.ppermute(value, 'rep', pairs)]
    all_to_all x0 -> x2, waiting for transfers between devices: none -> 20.1 us  [copies_of_all(): lax.all_to_all(jnp.broadcast_to(value[None], (count, *value.shape)), axis...]
    ppermute x31 -> x28, waiting for transfers between devices: 27.5 us -> 46.6 us  [link(): return lambda value: lax.ppermute(value, 'blk', pairs)]
    all_to_all x0 -> x2, starting transfers between devices: none -> 10.7 us  [copies_of_all(): lax.all_to_all(jnp.broadcast_to(value[None], (count, *value.shape)), axis...]
    convert_element_type x10, other arithmetic: 11.4 us -> 17 us  [the longest x4 5.93 us: scatter_second(): return (below.astype(BF16), beside.astype(BF16), blocks[1, 0].astype(BF16))]
    all_to_all x1, waiting for transfers between devices: 0.01 us -> 4.26 us  [on_device(): lax.all_to_all(weight_term.reshape(blk_count, -1, width), 'blk', 0, 0)]
    pallas_call x3 -> x7, Pallas kernels: 59.2 us -> 62.8 us  [the longest x2 30.2 us: forward_tiles(): pl.pallas_call(functools.partial(forward_kernel, layout, low, high, len(a...]
  transfers between devices with their start and end apart: 50 -> 47, of which waited for: 19 -> 19; matrix products, arithmetic and copies ran while one was open for 6% -> 6% of each run, Pallas kernels for 6% -> 7%
where the time goes in v3:
time: 296 us; the launch traced here: 295 us
  waiting for transfers between devices  99.3 us (34%)
  starting transfers between devices  69.1 us (23%)
  Pallas kernels  62.8 us (21%)
  blocking collectives  29.1 us (10%)
  other arithmetic  19.2 us (6%)
  local copies, waits for them, and re-layouts  13.3 us (4%)
    ppermute x28, waiting for transfers between devices, link(): return lambda value: lax.ppermute(value, 'blk', pairs)  46.6 us
    pallas_call x2, Pallas kernels, forward_tiles(): pl.pallas_call(functools.partial(forward_kernel, layout, low, high, len(a...  30.2 us
    ppermute x28, starting transfers between devices, link(): return lambda value: lax.ppermute(value, 'blk', pairs)  29.7 us
    all_to_all x2, blocking collectives, copies_of_all(): lax.all_to_all(jnp.broadcast_to(value[None], (count, *value.shape)), axis...  29.1 us
    ppermute x16, waiting for transfers between devices, link(): return lambda value: lax.ppermute(value, 'rep', pairs)  28.3 us
    pallas_call x2, Pallas kernels, backward_tiles(): pl.pallas_call(functools.partial(backward_kernel, layout, split, len(afte...  27.2 us
    ppermute x16, starting transfers between devices, link(): return lambda value: lax.ppermute(value, 'rep', pairs)  23.3 us
    all_to_all x2, waiting for transfers between devices, copies_of_all(): lax.all_to_all(jnp.broadcast_to(value[None], (count, *value.shape)), axis...  20.1 us
  transfers between devices with their start and end apart: 47, of which 19 were waited for; matrix products, arithmetic and copies ran while one was open for 6% of the time, Pallas kernels for 7%

profile of v3, /device:TPU:1, one launch (start us, length us, event | category | flops | bytes accessed | tf_op | source)
XLA Modules:
  0.0 294.7 jit_solution(10542455268570927492)
XLA Ops:
  0.6 2.5 collective-permute-start.1
  6.7 10.5 %collective-permute-done.1.refs_2_ = bf16[8,128,256]{2,1,0:T(8,128)(2,1)S(1)} collective-permute-done((bf16[8,128,256]{2,1,0:T(8,128)(2,1)}, bf16[8,128,256]{2,1,0:T(8,128)(2,1)S(1)}, u32[]{:S(2)}, u32[]{:S(2)}) %collective-permute-start.1) | collective-permute-done | bytes 524320 | tf_op jit(solution)/shard_map/ppermute | solution.py:34
  22.0 7.4 %collective-permute-done.9.refs_10_ = bf16[8,128,256]{2,1,0:T(8,128)(2,1)S(1)} collective-permute-done((bf16[8,128,256]{2,1,0:T(8,128)(2,1)S(1)}, bf16[8,128,256]{2,1,0:T(8,128)(2,1)S(1)}, u32[]{:S(2)}, u32[]{:S(2)}) %collective-permute-start.9) | collective-permute-done | bytes 524320 | tf_op jit(solution)/shard_map/ppermute | solution.py:34
  34.3 2.3 collective-permute-done.7.refs_8_
  38.7 4.8 %collective-permute-done.14.refs_15_ = bf16[4,128,256]{2,1,0:T(8,128)(2,1)S(1)} collective-permute-done((bf16[4,128,256]{2,1,0:T(8,128)(2,1)}, bf16[4,128,256]{2,1,0:T(8,128)(2,1)S(1)}, u32[]{:S(2)}, u32[]{:S(2)}) %collective-permute-start.14) | collective-permute-done | bytes 262176 | tf_op jit(solution)/shard_map/ppermute | solution.py:34
  47.2 15.4 %forward_tiles.2 = (bf16[4,128,256]{2,1,0:T(8,128)(2,1)}, bf16[4,128,256]{2,1,0:T(8,128)(2,1)}, bf16[8,128,256]{2,1,0:T(8,128)(2,1)}, bf16[8,128,256]{2,1,0:T(8,...) custom-call(s32[16]{0:T(128)} %reshape.103.order_ref, s32[8]{0:T(128)} %stack.99.dest_ref, s32[16,32]{1,0:T(8,128)} %bitcast.114, ...), custom_call_target="tpu_custom_call" | custom-call | flops 3000000000 | bytes 31457280 | tf_op jit(solution)/shard_map/forward_tiles/pallas_call | solution.py:229
  64.3 2.7 collective-permute-start.21
  66.9 3.6 %collective-permute-done.19 = bf16[4,128,256]{2,1,0:T(8,128)(2,1)S(1)} collective-permute-done((bf16[4,128,256]{2,1,0:T(8,128)(2,1)}, bf16[4,128,256]{2,1,0:T(8,128)(2,1)S(1)}, u32[]{:S(2)}, u32[]{:S(2)}) %collective-permute-start.19) | collective-permute-done | bytes 262176 | tf_op jit(solution)/shard_map/ppermute | solution.py:44
  71.7 4.2 %collective-permute-start.20 = (bf16[8,128,256]{2,1,0:T(8,128)(2,1)S(1)}, bf16[8,128,256]{2,1,0:T(8,128)(2,1)S(1)}, u32[]{:S(2)}, u32[]{:S(2)}) collective-permute-start(bf16[8,128,256]{2,1,0:T(8,128)(2,1)S(1)} %add_convert_fusion.6), channel_id=1, source_target_pairs={{0,4},{4,0},{1,5},{5,1},{2,6},{6,2},{3,7},{7,3},{8,12},{12,8},{9,1... | collective-permute-start | bytes 1572872 | tf_op jit(solution)/shard_map/ppermute | solution.py:44
  79.3 14.7 %forward_tiles.3 = (bf16[8,128,256]{2,1,0:T(8,128)(2,1)}, bf16[8,128,256]{2,1,0:T(8,128)(2,1)}, bf16[8,128,256]{2,1,0:T(8,128)(2,1)}, bf16[8,128,256]{2,1,0:T(8,128)(2,1)}) custom-call(s32[16]{0:T(128)} %reshape.103.order_ref, s32[8]{0:T(128)} %stack.99.dest_ref, s32[16,32]{1,0:T(8,128)} %bitcast.115, s32[16,32]{1,0:T(8,128)} %bitcast.119, s32[16]{0:T(128)} %bitcast.125, ...), custom_call_target="tpu_custom_call" | custom-call | flops 3000000000 | bytes 31457280 | tf_op jit(solution)/shard_map/forward_tiles/pallas_call | solution.py:229
  99.4 9.4 %collective-permute-done.18 = bf16[8,128,256]{2,1,0:T(8,128)(2,1)S(1)} collective-permute-done((bf16[8,128,256]{2,1,0:T(8,128)(2,1)}, bf16[8,128,256]{2,1,0:T(8,128)(2,1)S(1)}, u32[]{:S(2)}, u32[]{:S(2)}) %collective-permute-start.18) | collective-permute-done | bytes 524320 | tf_op jit(solution)/shard_map/ppermute | solution.py:44
  108.8 3.7 %collective-permute-done.24 = bf16[8,128,256]{2,1,0:T(8,128)(2,1)S(1)} collective-permute-done((bf16[8,128,256]{2,1,0:T(8,128)(2,1)S(1)}, bf16[8,128,256]{2,1,0:T(8,128)(2,1)S(1)}, u32[]{:S(2)}, u32[]{:S(2)}) %collective-permute-start.24) | collective-permute-done | bytes 524320 | tf_op jit(solution)/shard_map/ppermute | solution.py:44
  114.3 6.5 %all-to-all-start = ((f32[128,4,256]{2,1,0:T(4,128)}), f32[128,4,256]{2,1,0:T(4,128)S(1)}, u32[]{:S(2)}, u32[]{:S(2)}) async-start(f32[128,4,256]{2,1,0:T(4,128)} %broadcast_in_dim.10), calls=%async_computation | async-start | bytes 1048576 | tf_op jit(solution)/shard_map/all_to_all | solution.py:389
  120.8 13.9 %all-to-all-done = f32[128,4,256]{2,1,0:T(4,128)S(1)} async-done(((f32[128,4,256]{2,1,0:T(4,128)}), f32[128,4,256]{2,1,0:T(4,128)S(1)}, u32[]{:S(2)}, u32[]{:S(2)}) %all-to-all-start) | async-done | bytes 524320 | tf_op jit(solution)/shard_map/all_to_all | solution.py:389
  135.8 15.4 %all_to_all.25 = f32[128,2,256]{2,1,0:T(2,128)S(1)} all-to-all(f32[128,2,256]{2,1,0:T(2,128)S(1)} %broadcast_in_dim.11), channel_id=1, replica_groups=mesh['blk'=16,'rep'=8] {'blk','rep'}, dimensions={0} | all-to-all | bytes 524288 | tf_op jit(solution)/shard_map/all_to_all | solution.py:389
  155.2 2.4 collective-permute-start.32
  157.6 10.6 %collective-permute-done.25.refs_5_ = bf16[8,128,256]{2,1,0:T(8,128)(2,1)S(1)} collective-permute-done((bf16[8,128,256]{2,1,0:T(8,128)(2,1)S(1)}, bf16[8,128,256]{2,1,0:T(8,128)(2,1)S(1)}, u32[]{:S(2)}, u32[]{:S(2)}) %collective-permute-start.25) | collective-permute-done | bytes 524320 | tf_op jit(solution)/shard_map/ppermute | solution.py:44
  174.2 5.4 %all-to-all-start.2 = ((f32[16,16,256]{2,1,0:T(8,128)}), f32[16,16,256]{2,1,0:T(8,128)S(1)}, u32[]{:S(2)}, u32[]{:S(2)}) async-start(f32[16,16,256]{2,1,0:T(8,128)} %bitcast.112), calls=%async_computation.2 | async-start | bytes 524288 | tf_op jit(solution)/shard_map/all_to_all | solution.py:477
  183.2 4.3 %all-to-all-done.2.value_ref = f32[16,16,256]{2,1,0:T(8,128)S(1)} async-done(((f32[16,16,256]{2,1,0:T(8,128)}), f32[16,16,256]{2,1,0:T(8,128)S(1)}, u32[]{:S(2)}, u32[]{:S(2)}) %all-to-all-start.2) | async-done | bytes 262176 | tf_op jit(solution)/shard_map/all_to_all | solution.py:477
  191.1 4.3 %all-to-all-start.3 = ((f32[8,16,256]{2,1,0:T(8,128)}), f32[8,16,256]{2,1,0:T(8,128)S(1)}, u32[]{:S(2)}, u32[]{:S(2)}) async-start(f32[8,16,256]{2,1,0:T(8,128)} %broadcast_in_dim.13), calls=%async_computation.3 | async-start | bytes 262144 | tf_op jit(solution)/shard_map/all_to_all | solution.py:389
  196.0 6.3 %all-to-all-done.3.refs_9_.value_ref = f32[8,16,256]{2,1,0:T(8,128)S(1)} async-done(((f32[8,16,256]{2,1,0:T(8,128)}), f32[8,16,256]{2,1,0:T(8,128)S(1)}, u32[]{:S(2)}, u32[]{:S(2)}) %all-to-all-start.3) | async-done | bytes 131104 | tf_op jit(solution)/shard_map/all_to_all | solution.py:389
  203.8 13.5 %backward_tiles.2 = (bf16[1,8,128,256]{3,2,1,0:T(8,128)(2,1)}, bf16[3,8,128,256]{3,2,1,0:T(8,128)(2,1)}, bf16[4,8,128,256]{3,2,1,0:T(8,128)(2,1)}) custom-call(s32[8]{0:T(128)} %concatenate.11.order_ref, s32[8]{0:T(128)} %stack.99.dest_ref, s32[16,32]{1,0:T(8,128)} %bitcast.116, s32[16,32]{1,0:T(8,128)} %bitcast.120, s32[16]{0:T(128)} %bitcast.126, ...), custom_call_target="tpu_custom_call" | custom-call | flops 3000000000 | bytes 20971520 | tf_op jit(solution)/shard_map/backward_tiles/pallas_call | solution.py:330
  217.3 2.5 collective-permute-start.33
  219.9 3.9 %collective-permute-done.34 = bf16[1,8,128,256]{3,2,1,0:T(8,128)(2,1)S(1)} collective-permute-done((bf16[1,8,128,256]{3,2,1,0:T(8,128)(2,1)}, bf16[1,8,128,256]{3,2,1,0:T(8,128)(2,1)S(1)}, u32[]{:S(2)}, u32[]{:S(2)}) %collective-permute-start.34) | collective-permute-done | bytes 524320 | tf_op jit(solution)/shard_map/ppermute | solution.py:34
  223.8 3.0 %fusion.9 = (bf16[8,128,256]{2,1,0:T(8,128)(2,1)}, bf16[1,8,128,256]{3,2,1,0:T(8,128)(2,1)S(1)}) fusion(bf16[3,8,128,256]{3,2,1,0:T(8,128)(2,1)S(1)} %collective-permute-done.33, bf16[4,8,128,256]{3,2,1,0:T(8,128)(2,1)} %get-tuple-element.30, bf16[1,8,128,256]{3,2,1,0:T(8,128)(2,1)S(1)} %collective-permute-done.34), kind=kLoop, calls=%fused_computation.31 | loop fusion | flops 2097152 | bytes 3145728 | tf_op jit(solution)/shard_map/convert_element_type | solution.py:76
  230.3 5.4 %collective-permute-done.35 = bf16[4,128,256]{2,1,0:T(8,128)(2,1)S(1)} collective-permute-done((bf16[4,128,256]{2,1,0:T(8,128)(2,1)S(1)}, bf16[4,128,256]{2,1,0:T(8,128)(2,1)S(1)}, u32[]{:S(2)}, u32[]{:S(2)}) %collective-permute-start.35) | collective-permute-done | bytes 262176 | tf_op jit(solution)/shard_map/ppermute | solution.py:34
  237.9 13.7 %backward_tiles.3 = (bf16[4,8,128,256]{3,2,1,0:T(8,128)(2,1)}, bf16[4,8,128,256]{3,2,1,0:T(8,128)(2,1)}) custom-call(s32[8]{0:T(128)} %concatenate.10.order_ref, s32[8]{0:T(128)} %stack.99.dest_ref, s32[16,32]{1,0:T(8,128)} %bitcast.117, s32[16,32]{1,0:T(8,128)} %bitcast.121, s32[16]{0:T(128)} %bitcast.127, bf16[16,32,128,128]{3,2,1,0:T(8,128)(2,1)} %bitcast.95, ...), custom_call_target="tpu_custom_call" | custom-call | flops 3000000000 | bytes 20971520 | tf_op jit(solution)/shard_map/backward_tiles/pallas_call | solution.py:330
  252.4 4.2 %collective-permute-start.40 = (bf16[8,128,256]{2,1,0:T(8,128)(2,1)S(1)}, bf16[8,128,256]{2,1,0:T(8,128)(2,1)S(1)}, u32[]{:S(2)}, u32[]{:S(2)}) collective-permute-start(bf16[8,128,256]{2,1,0:T(8,128)(2,1)S(1)} %copy-done.28), channel_id=1, source_target_pairs={{0,96},{8,104},{16,112},{24,120},{32,0},{40,8},{48,16},{56,24},{64... | collective-permute-start | bytes 1572872 | tf_op jit(solution)/shard_map/ppermute | solution.py:34
  258.9 9.0 %collective-permute-done.40 = bf16[8,128,256]{2,1,0:T(8,128)(2,1)S(1)} collective-permute-done((bf16[8,128,256]{2,1,0:T(8,128)(2,1)S(1)}, bf16[8,128,256]{2,1,0:T(8,128)(2,1)S(1)}, u32[]{:S(2)}, u32[]{:S(2)}) %collective-permute-start.40) | collective-permute-done | bytes 524320 | tf_op jit(solution)/shard_map/ppermute | solution.py:34
  271.0 2.6 fusion.3
  277.6 13.7 %all_to_all.26 = f32[16,16,256]{2,1,0:T(8,128)S(1)} all-to-all(f32[16,16,256]{2,1,0:T(8,128)S(1)} %broadcast_in_dim.14), channel_id=1, replica_groups=mesh['blk'=16,'rep'=8] {'blk'}, dimensions={0} | all-to-all | bytes 524288 | tf_op jit(solution)/shard_map/all_to_all | solution.py:389
  291.4 2.7 fusion.6
  (191 shorter events, 69.2 us)
Async XLA Ops:
  0.6 16.5 %collective-permute-start.1 = (bf16[8,128,256]{2,1,0:T(8,128)(2,1)}, bf16[8,128,256]{2,1,0:T(8,128)(2,1)S(1)}, u32[]{:S(2)}, u32[]{:S(2)}) collective-permute-start(bf16[8,128,256]{2,1,0:T(8,128)(2,1)} %bitcast.103), channel_id=1, source_target_pairs={{0,32},{8,40},{16,48},{24,56},{32,64},{40,72},{48,80},{56,88},{64,... | collective-permute-start | bytes 1572872 | tf_op jit(solution)/shard_map/ppermute | solution.py:34
  3.2 15.3 %collective-permute-start.5 = (bf16[8,128,256]{2,1,0:T(8,128)(2,1)}, bf16[8,128,256]{2,1,0:T(8,128)(2,1)S(1)}, u32[]{:S(2)}, u32[]{:S(2)}) collective-permute-start(bf16[8,128,256]{2,1,0:T(8,128)(2,1)} %bitcast.104), channel_id=1, source_target_pairs={{0,16},{8,24},{16,0},{24,8},{32,48},{40,56},{48,32},{56,40},{64,80... | collective-permute-start | bytes 1572872 | tf_op jit(solution)/shard_map/ppermute | solution.py:34
  4.5 17.2 %collective-permute-start.3 = (bf16[8,128,256]{2,1,0:T(8,128)(2,1)}, bf16[8,128,256]{2,1,0:T(8,128)(2,1)S(1)}, u32[]{:S(2)}, u32[]{:S(2)}) collective-permute-start(bf16[8,128,256]{2,1,0:T(8,128)(2,1)} %bitcast.105), channel_id=1, source_target_pairs={{0,96},{8,104},{16,112},{24,120},{32,0},{40,8},{48,16},{56,24},{64... | collective-permute-start | bytes 1572872 | tf_op jit(solution)/shard_map/ppermute | solution.py:34
  17.2 12.3 %collective-permute-start.9 = (bf16[8,128,256]{2,1,0:T(8,128)(2,1)S(1)}, bf16[8,128,256]{2,1,0:T(8,128)(2,1)S(1)}, u32[]{:S(2)}, u32[]{:S(2)}) collective-permute-start(bf16[8,128,256]{2,1,0:T(8,128)(2,1)S(1)} %collective-permute-done.1.refs_2_), channel_id=1, source_target_pairs={{0,16},{8,24},{16,0},{24,8},{32,48},{40,56},{48,32},{56,40},{64,80... | collective-permute-start | bytes 1572872 | tf_op jit(solution)/shard_map/ppermute | solution.py:34
  18.5 13.0 %collective-permute-start.11 = (bf16[8,128,256]{2,1,0:T(8,128)(2,1)S(1)}, bf16[8,128,256]{2,1,0:T(8,128)(2,1)S(1)}, u32[]{:S(2)}, u32[]{:S(2)}) collective-permute-start(bf16[8,128,256]{2,1,0:T(8,128)(2,1)S(1)} %collective-permute-done.5.refs_6_), channel_id=1, source_target_pairs={{0,96},{8,104},{16,112},{24,120},{32,0},{40,8},{48,16},{56,24},{64... | collective-permute-start | bytes 1572872 | tf_op jit(solution)/shard_map/ppermute | solution.py:34
  19.6 14.7 %collective-permute-start = (bf16[8,128,256]{2,1,0:T(8,128)(2,1)}, bf16[8,128,256]{2,1,0:T(8,128)(2,1)S(1)}, u32[]{:S(2)}, u32[]{:S(2)}) collective-permute-start(bf16[8,128,256]{2,1,0:T(8,128)(2,1)} %bitcast.106), channel_id=1, source_target_pairs={{0,8},{8,0},{16,24},{24,16},{32,40},{40,32},{48,56},{56,48},{64,72... | collective-permute-start | bytes 1572872 | tf_op jit(solution)/shard_map/ppermute | solution.py:34
  21.7 14.9 %collective-permute-start.7 = (bf16[8,128,256]{2,1,0:T(8,128)(2,1)S(1)}, bf16[8,128,256]{2,1,0:T(8,128)(2,1)}, u32[]{:S(2)}, u32[]{:S(2)}) collective-permute-start(bf16[8,128,256]{2,1,0:T(8,128)(2,1)S(1)} %collective-permute-done.1.refs_2_), channel_id=1, source_target_pairs={{0,32},{8,40},{16,48},{24,56},{32,64},{40,72},{48,80},{56,88},{64,... | collective-permute-start | bytes 1572872 | tf_op jit(solution)/shard_map/ppermute | solution.py:34
  21.7 15.2 %collective-permute-start.2 = (bf16[8,128,256]{2,1,0:T(8,128)(2,1)S(1)}, bf16[8,128,256]{2,1,0:T(8,128)(2,1)S(1)}, u32[]{:S(2)}, u32[]{:S(2)}) collective-permute-start(bf16[8,128,256]{2,1,0:T(8,128)(2,1)S(1)} %collective-permute-done.1.refs_2_), channel_id=1, source_target_pairs={{0,8},{8,0},{16,24},{24,16},{32,40},{40,32},{48,56},{56,48},{64,72... | collective-permute-start | bytes 1572872 | tf_op jit(solution)/shard_map/ppermute | solution.py:34
  64.3 11.6 %collective-permute-start.17 = (bf16[4,128,256]{2,1,0:T(8,128)(2,1)}, bf16[4,128,256]{2,1,0:T(8,128)(2,1)S(1)}, u32[]{:S(2)}, u32[]{:S(2)}) collective-permute-start(bf16[4,128,256]{2,1,0:T(8,128)(2,1)} %get-tuple-element.21), channel_id=1, source_target_pairs={{0,1},{4,5},{1,2},{5,6},{2,3},{6,7},{3,0},{7,4},{8,9},{12,13},{9,1... | collective-permute-start | bytes 786440 | tf_op jit(solution)/shard_map/ppermute | solution.py:44
  64.3 30.4 %collective-permute-start.21 = (bf16[8,128,256]{2,1,0:T(8,128)(2,1)}, bf16[8,128,256]{2,1,0:T(8,128)(2,1)S(1)}, u32[]{:S(2)}, u32[]{:S(2)}) collective-permute-start(bf16[8,128,256]{2,1,0:T(8,128)(2,1)} %get-tuple-element.28), channel_id=1, source_target_pairs={{0,3},{4,7},{1,0},{5,4},{2,1},{6,5},{3,2},{7,6},{8,11},{12,15},{9,... | collective-permute-start | bytes 1572872 | tf_op jit(solution)/shard_map/ppermute | solution.py:44
  71.7 23.0 %collective-permute-start.20 = (bf16[8,128,256]{2,1,0:T(8,128)(2,1)S(1)}, bf16[8,128,256]{2,1,0:T(8,128)(2,1)S(1)}, u32[]{:S(2)}, u32[]{:S(2)}) collective-permute-start(bf16[8,128,256]{2,1,0:T(8,128)(2,1)S(1)} %add_convert_fusion.6), channel_id=1, source_target_pairs={{0,4},{4,0},{1,5},{5,1},{2,6},{6,2},{3,7},{7,3},{8,12},{12,8},{9,1... | collective-permute-start | bytes 1572872 | tf_op jit(solution)/shard_map/ppermute | solution.py:44
  77.6 20.6 %collective-permute-start.23 = (bf16[8,128,256]{2,1,0:T(8,128)(2,1)S(1)}, bf16[8,128,256]{2,1,0:T(8,128)(2,1)S(1)}, u32[]{:S(2)}, u32[]{:S(2)}) collective-permute-start(bf16[8,128,256]{2,1,0:T(8,128)(2,1)S(1)} %add_convert_fusion.7), channel_id=1, source_target_pairs={{0,1},{4,5},{1,2},{5,6},{2,3},{6,7},{3,0},{7,4},{8,9},{12,13},{9,1... | collective-permute-start | bytes 1572872 | tf_op jit(solution)/shard_map/ppermute | solution.py:44
  94.1 14.7 %collective-permute-start.18 = (bf16[8,128,256]{2,1,0:T(8,128)(2,1)}, bf16[8,128,256]{2,1,0:T(8,128)(2,1)S(1)}, u32[]{:S(2)}, u32[]{:S(2)}) collective-permute-start(bf16[8,128,256]{2,1,0:T(8,128)(2,1)} %get-tuple-element.24), channel_id=1, source_target_pairs={{0,1},{4,5},{1,2},{5,6},{2,3},{6,7},{3,0},{7,4},{8,9},{12,13},{9,1... | collective-permute-start | bytes 1572872 | tf_op jit(solution)/shard_map/ppermute | solution.py:44
  96.0 12.8 %collective-permute-start.22 = (bf16[8,128,256]{2,1,0:T(8,128)(2,1)S(1)}, bf16[8,128,256]{2,1,0:T(8,128)(2,1)S(1)}, u32[]{:S(2)}, u32[]{:S(2)}) collective-permute-start(bf16[8,128,256]{2,1,0:T(8,128)(2,1)S(1)} %add_convert_fusion.5), channel_id=1, source_target_pairs={{0,3},{4,7},{1,0},{5,4},{2,1},{6,5},{3,2},{7,6},{8,11},{12,15},{9,... | collective-permute-start | bytes 1572872 | tf_op jit(solution)/shard_map/ppermute | solution.py:44
  98.3 14.2 %collective-permute-start.24 = (bf16[8,128,256]{2,1,0:T(8,128)(2,1)S(1)}, bf16[8,128,256]{2,1,0:T(8,128)(2,1)S(1)}, u32[]{:S(2)}, u32[]{:S(2)}) collective-permute-start(bf16[8,128,256]{2,1,0:T(8,128)(2,1)S(1)} %add_convert_fusion.4), channel_id=1, source_target_pairs={{0,4},{4,0},{1,5},{5,1},{2,6},{6,2},{3,7},{7,3},{8,12},{12,8},{9,1... | collective-permute-start | bytes 1572872 | tf_op jit(solution)/shard_map/ppermute | solution.py:44
  114.3 20.3 %all-to-all-start = ((f32[128,4,256]{2,1,0:T(4,128)}), f32[128,4,256]{2,1,0:T(4,128)S(1)}, u32[]{:S(2)}, u32[]{:S(2)}) async-start(f32[128,4,256]{2,1,0:T(4,128)} %broadcast_in_dim.10), calls=%async_computation | async-start | bytes 1048576 | tf_op jit(solution)/shard_map/all_to_all | solution.py:389
  153.8 14.4 %collective-permute-start.25 = (bf16[8,128,256]{2,1,0:T(8,128)(2,1)S(1)}, bf16[8,128,256]{2,1,0:T(8,128)(2,1)S(1)}, u32[]{:S(2)}, u32[]{:S(2)}) collective-permute-start(bf16[8,128,256]{2,1,0:T(8,128)(2,1)S(1)} %bitcast.96), channel_id=1, source_target_pairs={{0,4},{4,0},{1,5},{5,1},{2,6},{6,2},{3,7},{7,3},{8,12},{12,8},{9,1... | collective-permute-start | bytes 1572872 | tf_op jit(solution)/shard_map/ppermute | solution.py:44
  154.9 14.2 %collective-permute-start.28 = (bf16[8,128,256]{2,1,0:T(8,128)(2,1)S(1)}, bf16[8,128,256]{2,1,0:T(8,128)(2,1)}, u32[]{:S(2)}, u32[]{:S(2)}) collective-permute-start(bf16[8,128,256]{2,1,0:T(8,128)(2,1)S(1)} %bitcast.97), channel_id=1, source_target_pairs={{0,1},{4,5},{1,2},{5,6},{2,3},{6,7},{3,0},{7,4},{8,9},{12,13},{9,1... | collective-permute-start | bytes 1572872 | tf_op jit(solution)/shard_map/ppermute | solution.py:44
  155.2 15.8 %collective-permute-start.32 = (bf16[8,128,256]{2,1,0:T(8,128)(2,1)S(1)}, bf16[8,128,256]{2,1,0:T(8,128)(2,1)S(1)}, u32[]{:S(2)}, u32[]{:S(2)}) collective-permute-start(bf16[8,128,256]{2,1,0:T(8,128)(2,1)S(1)} %bitcast.98), channel_id=1, source_target_pairs={{0,3},{4,7},{1,0},{5,4},{2,1},{6,5},{3,2},{7,6},{8,11},{12,15},{9,... | collective-permute-start | bytes 1572872 | tf_op jit(solution)/shard_map/ppermute | solution.py:44
  168.2 12.0 %collective-permute-start.26 = (bf16[8,128,256]{2,1,0:T(8,128)(2,1)S(1)}, bf16[8,128,256]{2,1,0:T(8,128)(2,1)S(1)}, u32[]{:S(2)}, u32[]{:S(2)}) collective-permute-start(bf16[8,128,256]{2,1,0:T(8,128)(2,1)S(1)} %collective-permute-done.25.refs_5_), channel_id=1, source_target_pairs={{0,3},{4,7},{1,0},{5,4},{2,1},{6,5},{3,2},{7,6},{8,11},{12,15},{9,... | collective-permute-start | bytes 1572872 | tf_op jit(solution)/shard_map/ppermute | solution.py:44
  169.1 13.5 %collective-permute-start.29 = (bf16[8,128,256]{2,1,0:T(8,128)(2,1)}, bf16[8,128,256]{2,1,0:T(8,128)(2,1)S(1)}, u32[]{:S(2)}, u32[]{:S(2)}) collective-permute-start(bf16[8,128,256]{2,1,0:T(8,128)(2,1)} %collective-permute-done.28.refs_7_), channel_id=1, source_target_pairs={{0,4},{4,0},{1,5},{5,1},{2,6},{6,2},{3,7},{7,3},{8,12},{12,8},{9,1... | collective-permute-start | bytes 1572872 | tf_op jit(solution)/shard_map/ppermute | solution.py:44
  170.7 25.3 %collective-permute-start.31 = (bf16[8,128,256]{2,1,0:T(8,128)(2,1)}, bf16[8,128,256]{2,1,0:T(8,128)(2,1)}, u32[]{:S(2)}, u32[]{:S(2)}) collective-permute-start(bf16[8,128,256]{2,1,0:T(8,128)(2,1)} %collective-permute-done.28.refs_7_), channel_id=1, source_target_pairs={{0,1},{4,5},{1,2},{5,6},{2,3},{6,7},{3,0},{7,4},{8,9},{12,13},{9,1... | collective-permute-start | bytes 1572872 | tf_op jit(solution)/shard_map/ppermute | solution.py:44
  174.2 13.2 %all-to-all-start.2 = ((f32[16,16,256]{2,1,0:T(8,128)}), f32[16,16,256]{2,1,0:T(8,128)S(1)}, u32[]{:S(2)}, u32[]{:S(2)}) async-start(f32[16,16,256]{2,1,0:T(8,128)} %bitcast.112), calls=%async_computation.2 | async-start | bytes 524288 | tf_op jit(solution)/shard_map/all_to_all | solution.py:477
  180.3 22.0 %collective-permute-start.27 = (bf16[4,128,256]{2,1,0:T(8,128)(2,1)S(1)}, bf16[4,128,256]{2,1,0:T(8,128)(2,1)S(1)}, u32[]{:S(2)}, u32[]{:S(2)}) collective-permute-start(bf16[4,128,256]{2,1,0:T(8,128)(2,1)S(1)} %slice.111), channel_id=1, source_target_pairs={{0,3},{4,7},{1,0},{5,4},{2,1},{6,5},{3,2},{7,6},{8,11},{12,15},{9,... | collective-permute-start | bytes 786440 | tf_op jit(solution)/shard_map/ppermute | solution.py:44
  182.7 19.6 %collective-permute-start.30 = (bf16[4,128,256]{2,1,0:T(8,128)(2,1)S(1)}, bf16[4,128,256]{2,1,0:T(8,128)(2,1)S(1)}, u32[]{:S(2)}, u32[]{:S(2)}) collective-permute-start(bf16[4,128,256]{2,1,0:T(8,128)(2,1)S(1)} %slice.112), channel_id=1, source_target_pairs={{0,1},{4,5},{1,2},{5,6},{2,3},{6,7},{3,0},{7,4},{8,9},{12,13},{9,1... | collective-permute-start | bytes 786440 | tf_op jit(solution)/shard_map/ppermute | solution.py:44
  191.1 11.2 %all-to-all-start.3 = ((f32[8,16,256]{2,1,0:T(8,128)}), f32[8,16,256]{2,1,0:T(8,128)S(1)}, u32[]{:S(2)}, u32[]{:S(2)}) async-start(f32[8,16,256]{2,1,0:T(8,128)} %broadcast_in_dim.13), calls=%async_computation.3 | async-start | bytes 262144 | tf_op jit(solution)/shard_map/all_to_all | solution.py:389
  252.4 15.5 %collective-permute-start.40 = (bf16[8,128,256]{2,1,0:T(8,128)(2,1)S(1)}, bf16[8,128,256]{2,1,0:T(8,128)(2,1)S(1)}, u32[]{:S(2)}, u32[]{:S(2)}) collective-permute-start(bf16[8,128,256]{2,1,0:T(8,128)(2,1)S(1)} %copy-done.28), channel_id=1, source_target_pairs={{0,96},{8,104},{16,112},{24,120},{32,0},{40,8},{48,16},{56,24},{64... | collective-permute-start | bytes 1572872 | tf_op jit(solution)/shard_map/ppermute | solution.py:34
  256.6 13.2 %collective-permute-start.39 = (bf16[8,128,256]{2,1,0:T(8,128)(2,1)S(1)}, bf16[8,128,256]{2,1,0:T(8,128)(2,1)S(1)}, u32[]{:S(2)}, u32[]{:S(2)}) collective-permute-start(bf16[8,128,256]{2,1,0:T(8,128)(2,1)S(1)} %get-tuple-element.45), channel_id=1, source_target_pairs={{0,16},{8,24},{16,0},{24,8},{32,48},{40,56},{48,32},{56,40},{64,80... | collective-permute-start | bytes 1572872 | tf_op jit(solution)/shard_map/ppermute | solution.py:34
  256.6 14.4 %collective-permute-start.42 = (bf16[8,128,256]{2,1,0:T(8,128)(2,1)S(1)}, bf16[8,128,256]{2,1,0:T(8,128)(2,1)S(1)}, u32[]{:S(2)}, u32[]{:S(2)}) collective-permute-start(bf16[8,128,256]{2,1,0:T(8,128)(2,1)S(1)} %get-tuple-element.46), channel_id=1, source_target_pairs={{0,32},{8,40},{16,48},{24,56},{32,64},{40,72},{48,80},{56,88},{64,... | collective-permute-start | bytes 1572872 | tf_op jit(solution)/shard_map/ppermute | solution.py:34
  258.6 32.7 %collective-permute-start.37 = (bf16[8,128,256]{2,1,0:T(8,128)(2,1)}, bf16[8,128,256]{2,1,0:T(8,128)(2,1)}, u32[]{:S(2)}, u32[]{:S(2)}) collective-permute-start(bf16[8,128,256]{2,1,0:T(8,128)(2,1)} %fusion.8), channel_id=1, source_target_pairs={{0,32},{8,40},{16,48},{24,56},{32,64},{40,72},{48,80},{56,88},{64,... | collective-permute-start | bytes 1572872 | tf_op jit(solution)/shard_map/ppermute | solution.py:34
  273.6 17.8 %collective-permute-start.41 = (bf16[8,128,256]{2,1,0:T(8,128)(2,1)S(1)}, bf16[8,128,256]{2,1,0:T(8,128)(2,1)}, u32[]{:S(2)}, u32[]{:S(2)}) collective-permute-start(bf16[8,128,256]{2,1,0:T(8,128)(2,1)S(1)} %get-tuple-element.43), channel_id=1, source_target_pairs={{0,96},{8,104},{16,112},{24,120},{32,0},{40,8},{48,16},{56,24},{64... | collective-permute-start | bytes 1572872 | tf_op jit(solution)/shard_map/ppermute | solution.py:34
  273.9 17.5 %collective-permute-start.43 = (bf16[8,128,256]{2,1,0:T(8,128)(2,1)}, bf16[8,128,256]{2,1,0:T(8,128)(2,1)}, u32[]{:S(2)}, u32[]{:S(2)}) collective-permute-start(bf16[8,128,256]{2,1,0:T(8,128)(2,1)} %get-tuple-element.44), channel_id=1, source_target_pairs={{0,16},{8,24},{16,0},{24,8},{32,48},{40,56},{48,32},{56,40},{64,80... | collective-permute-start | bytes 1572872 | tf_op jit(solution)/shard_map/ppermute | solution.py:34
  (48 other events, 625.1 us)

commit v4 on v3

v4 whole, which is shorter than its diff:
```python
import functools

import jax
import jax.numpy as jnp
from jax import lax
from jax.experimental import pallas as pl
from jax.experimental.pallas import tpu as pltpu
from jax.sharding import PartitionSpec as P

norm_eps = 1e-05
GROUP = 32
BF16, F32 = jnp.bfloat16, jnp.float32
RING = 4
PLACES = ((2, 1), (1, 1), (-1, 1), (2, 0), (0, 1), (1, 0), (-1, 0), (0, 0))
ANY = pl.BlockSpec(memory_space=pl.ANY)
VMEM = pl.BlockSpec(memory_space=pltpu.VMEM)
SMEM = pl.BlockSpec(memory_space=pltpu.SMEM)


def blk_index(z, y, core):
    return (z % RING) * 4 + (y % 2) * 2 + core % 2


def rep_index(x, y):
    return (y % 2) * RING + x % RING


def blk_links():
    spots = [(z, y, c) for z in range(RING) for y in range(2) for c in range(2)]

    def link(dz, dy, dc):
        pairs = [(blk_index(z, y, c), blk_index(z + dz, y + dy, c + dc)) for z, y, c in spots]
        return lambda value: lax.ppermute(value, "blk", pairs)

    return link(1, 0, 0), link(-1, 0, 0), link(0, 1, 0), link(0, 0, 1)


def rep_links():
    spots = [(x, y) for x in range(RING) for y in range(2)]

    def link(dx, dy):
        pairs = [(rep_index(x, y), rep_index(x + dx, y + dy)) for x, y in spots]
        return lambda value: lax.ppermute(value, "rep", pairs)

    return link(1, 0), link(-1, 0), link(0, 1)


def nothing(*refs):
    pass


def together(*arrays):
    count = len(arrays)
    return pl.pallas_call(
        nothing,
        in_specs=[ANY] * count,
        out_specs=[ANY] * count,
        out_shape=[jax.ShapeDtypeStruct(a.shape, a.dtype) for a in arrays],
        input_output_aliases={i: i for i in range(count)},
        name="together",
    )(*arrays)


def gather_tree(own, up, down, pair, beside_it=lambda: ()):
    half = own.shape[0] // 2
    below, above, beside = together(up(own), down(own), pair(own))
    below_beside, above_beside, far, *others = together(
        pair(below), down(beside), up(below), *beside_it()
    )
    far_beside = [(0, down(above_beside[:half])), (half, up(below_beside[half:]))]
    whole = {
        (0, 0): own,
        (-1, 0): below,
        (1, 0): above,
        (0, 1): beside,
        (-1, 1): below_beside,
        (1, 1): above_beside,
        (2, 0): far,
    }
    return [far_beside if place == (2, 1) else [(0, whole[place])] for place in PLACES], others


def scatter_first(corner, blocks, up, down):
    low, high = (part.astype(BF16) for part in corner)
    half = low.shape[0]
    none = ((0, 0), (0, 0))
    low, high = together(up(low), down(high))
    above_beside = blocks[1, 1].astype(F32) + jnp.pad(low.astype(F32), ((0, half), *none))
    below_beside = blocks[-1, 1].astype(F32) + jnp.pad(high.astype(F32), ((half, 0), *none))
    return above_beside.astype(BF16), below_beside.astype(BF16), blocks[2, 0].astype(BF16)


def scatter_second(leaving, blocks, up, down, pair, beside_it=()):
    above_beside, below_beside, far = leaving
    below_beside, far, above_beside, *others = together(
        pair(below_beside), down(far), up(above_beside), *beside_it
    )
    below = blocks[-1, 0].astype(F32) + below_beside.astype(F32) + far.astype(F32)
    beside = blocks[0, 1].astype(F32) + above_beside.astype(F32)
    return (below.astype(BF16), beside.astype(BF16), blocks[1, 0].astype(BF16)), others


def scatter_third(leaving, own, up, down, pair):
    below, beside, above = leaving
    above, below, beside = together(up(above), down(below), pair(beside))
    return own.astype(F32) + above.astype(F32) + below.astype(F32) + beside.astype(F32)


def run_list(first, last, tile_list, panel_list, key_list, multiply, acc_ref):
    def add_group(g, carry):
        products = [
            multiply(tile_list[g * GROUP + j], panel_list[g * GROUP + j]) for j in range(GROUP)
        ]
        for j in range(GROUP):
            acc_ref[key_list[g * GROUP + j]] += products[j]
        return carry

    lax.fori_loop(first, last, add_group, 0)


def zero_all(acc_ref):
    def zero(i, carry):
        acc_ref[i] = jnp.zeros(acc_ref.shape[1:], F32)
        return carry

    lax.fori_loop(0, acc_ref.shape[0], zero, 0)


def fill_tail(count, spare, tile_list, panel_list, key_list):
    for j in range(GROUP):
        tile_list[count + j] = 0
        panel_list[count + j] = 0
        key_list[count + j] = spare


def load_sources(layout, order_ref, tiles_ref, shard_refs, tiles_v, shards_v, tile_sem, part_sem, slots, col_tiles):
    copies, part = [], 0
    for i, firsts in enumerate(layout):
        own = [
            pltpu.make_async_copy(
                tiles_ref.at[order_ref[i]], tiles_v.at[pl.ds(i * slots, slots)], tile_sem.at[i]
            )
        ]
        for first in firsts:
            size = shard_refs[part].shape[0]
            own.append(
                pltpu.make_async_copy(
                    shard_refs[part],
                    shards_v.at[pl.ds(i * col_tiles + first, size)],
                    part_sem.at[part],
                )
            )
            part += 1
        for copy in own:
            copy.start()
        copies.append(own)
    return copies


def forward_products(copies, order_ref, rows_ref, cols_ref, counts_ref, tiles_v, shards_v, acc_ref, tile_list, panel_list, key_list):
    sources = len(copies)
    slots = rows_ref.shape[1]
    col_tiles = shards_v.shape[0] // sources
    spare = acc_ref.shape[0] - 1
    count, ends = jnp.int32(0), []
    for i in range(sources):
        source = order_ref[i]

        def enlist(k, count, i=i, source=source):
            tile_list[count] = i * slots + k
            panel_list[count] = i * col_tiles + cols_ref[source, k]
            key_list[count] = rows_ref[source, k]
            return count + 1

        count = lax.fori_loop(0, counts_ref[source], enlist, count)
        ends.append(count)
    fill_tail(count, spare, tile_list, panel_list, key_list)

    def multiply(tile, panel):
        return jnp.dot(tiles_v[tile], shards_v[panel], preferred_element_type=F32)

    lists = (tile_list, panel_list, key_list, multiply, acc_ref)
    half = sources // 2
    for own in copies[:half]:
        for copy in own:
            copy.wait()
    middle = ends[half - 1] // GROUP
    run_list(0, middle, *lists)
    for own in copies[half:]:
        for copy in own:
            copy.wait()
    run_list(middle, (count + GROUP - 1) // GROUP, *lists)


def forward_kernel(layout, order_ref, dest_ref, rows_ref, cols_ref, counts_ref, tiles_ref, *refs):
    parts = sum(len(firsts) for firsts in layout)
    shard_refs, refs = refs[:parts], refs[parts:]
    out_refs, offset_ref, refs = refs[: len(PLACES) + 1], refs[len(PLACES) + 1], refs[len(PLACES) + 2 :]
    acc_ref, tiles_v, shards_v, *lists, tile_sem, part_sem = refs
    slots, col_tiles = rows_ref.shape[1], shards_v.shape[0] // len(layout)
    row_tiles = acc_ref.shape[0] - 1
    copies = load_sources(
        layout, order_ref, tiles_ref, shard_refs, tiles_v, shards_v, tile_sem, part_sem, slots, col_tiles
    )
    zero_all(acc_ref)
    forward_products(
        copies, order_ref, rows_ref, cols_ref, counts_ref, tiles_v, shards_v, acc_ref, *lists
    )

    def total(i, carry):
        return carry + jnp.sum(acc_ref[i].reshape(-1, 8, acc_ref.shape[2]), axis=0)

    sums = lax.fori_loop(0, row_tiles, total, jnp.zeros((8, acc_ref.shape[2]), F32))
    offset = jnp.sum(sums, axis=0, keepdims=True) / (row_tiles * acc_ref.shape[1])
    offset_ref[...] = offset
    half = col_tiles // 2
    spans = [(out_refs[0], 0, 0, half), (out_refs[1], 0, half, half)]
    spans += [(out_refs[d + 1], d, 0, col_tiles) for d in range(1, len(PLACES))]
    for out_ref, d, first, size in spans:
        base = dest_ref[d] * col_tiles + first

        def put(i, carry, out_ref=out_ref, base=base):
            out_ref[i] = (acc_ref[base + i] - offset).astype(BF16)
            return carry

        lax.fori_loop(0, size, put, 0)


def list_shapes(cap):
    return [pltpu.SMEM((cap,), jnp.int32)] * 3


def forward_tiles(order, dests, scalars, tiles, shards):
    arrays = [array for parts in shards for _, array in parts]
    layout = tuple(tuple(first for first, _ in parts) for parts in shards)
    sources, slots, tile, _ = tiles.shape
    width = arrays[0].shape[2]
    col_tiles = sum(array.shape[0] for _, array in shards[0])
    row_tiles = col_tiles * len(PLACES)
    sizes = [col_tiles // 2] * 2 + [col_tiles] * (len(PLACES) - 1)
    out_shape = [jax.ShapeDtypeStruct((size, tile, width), BF16) for size in sizes]
    out_shape.append(jax.ShapeDtypeStruct((1, width), F32))
    return pl.pallas_call(
        functools.partial(forward_kernel, layout),
        in_specs=[SMEM] * 5 + [ANY] * (1 + len(arrays)),
        out_specs=[VMEM] * len(out_shape),
        out_shape=out_shape,
        scratch_shapes=[
            pltpu.VMEM((row_tiles + 1, tile, width), F32),
            pltpu.VMEM((sources * slots, tile, tile), BF16),
            pltpu.VMEM((sources * col_tiles, tile, width), BF16),
            *list_shapes(sources * slots + GROUP),
            pltpu.SemaphoreType.DMA((sources,)),
            pltpu.SemaphoreType.DMA((len(arrays),)),
        ],
        compiler_params=pltpu.CompilerParams(vmem_limit_bytes=44 * 2**20),
        cost_estimate=pl.CostEstimate(flops=6 * 10**9, bytes_accessed=30 * 2**20, transcendentals=0),
        name="forward_tiles",
    )(order, dests, *scalars, tiles, *arrays)


def backward_kernel(layout, sizes, waits, order_ref, dest_ref, rows_ref, cols_ref, counts_ref, tiles_ref, *refs):
    parts = sum(len(firsts) for firsts in layout)
    grad_refs, refs = refs[:parts], refs[parts + waits :]
    out_refs, refs = refs[: len(sizes)], refs[len(sizes) :]
    tiles_v, grads_v, acc_ref, tile_list, panel_list, key_list, tile_sem, part_sem = refs
    slots = rows_ref.shape[1]
    sources = tiles_v.shape[0] // slots
    col_tiles = (acc_ref.shape[0] - 1) // sources

    copies, part = [], 0
    for i, firsts in enumerate(layout):
        base = dest_ref[i] * col_tiles
        for first in firsts:
            size = grad_refs[part].shape[0]
            copies.append(
                pltpu.make_async_copy(
                    grad_refs[part], grads_v.at[pl.ds(base + first, size)], part_sem.at[part]
                )
            )
            part += 1
    tile_copies = [
        pltpu.make_async_copy(
            tiles_ref.at[order_ref[i]], tiles_v.at[pl.ds(i * slots, slots)], tile_sem.at[i]
        )
        for i in range(sources)
    ]
    for copy in copies + tile_copies:
        copy.start()

    zero_all(acc_ref)
    count, ends = jnp.int32(0), []
    for i in range(sources):
        source = order_ref[i]

        def enlist(k, count, i=i, source=source):
            tile_list[count] = i * slots + k
            panel_list[count] = rows_ref[source, k]
            key_list[count] = i * col_tiles + cols_ref[source, k]
            return count + 1

        count = lax.fori_loop(0, counts_ref[source], enlist, count)
        ends.append(count)
    fill_tail(count, sources * col_tiles, tile_list, panel_list, key_list)

    def multiply(tile, panel):
        return lax.dot_general(
            tiles_v[tile], grads_v[panel], (((0,), (0,)), ((), ())), preferred_element_type=F32
        )

    lists = (tile_list, panel_list, key_list, multiply, acc_ref)
    for copy in copies + tile_copies[: sources // 2]:
        copy.wait()
    middle = ends[sources // 2 - 1] // GROUP
    run_list(0, middle, *lists)
    for copy in tile_copies[sources // 2 :]:
        copy.wait()
    run_list(middle, (count + GROUP - 1) // GROUP, *lists)

    base = 0
    for out_ref, size in zip(out_refs, sizes):

        def put(t, carry, out_ref=out_ref, base=base):
            out_ref[t] = acc_ref[base + t].astype(BF16)
            return carry

        lax.fori_loop(0, size, put, 0)
        base += size


def backward_tiles(sizes, order, dests, scalars, tiles, grads, after=()):
    arrays = [array for parts in grads for _, array in parts]
    layout = tuple(tuple(first for first, _ in parts) for parts in grads)
    slots, tile = tiles.shape[1:3]
    width = arrays[0].shape[2]
    row_tiles = sum(array.shape[0] for array in arrays)
    sources = order.shape[0]
    return pl.pallas_call(
        functools.partial(backward_kernel, layout, sizes, len(after)),
        in_specs=[SMEM] * 5 + [ANY] * (1 + len(arrays) + len(after)),
        out_specs=[VMEM] * len(sizes),
        out_shape=[jax.ShapeDtypeStruct((size, tile, width), BF16) for size in sizes],
        scratch_shapes=[
            pltpu.VMEM((sources * slots, tile, tile), BF16),
            pltpu.VMEM((row_tiles, tile, width), BF16),
            pltpu.VMEM((sum(sizes) + 1, tile, width), F32),
            *list_shapes(sources * slots + GROUP),
            pltpu.SemaphoreType.DMA((sources,)),
            pltpu.SemaphoreType.DMA((len(arrays),)),
        ],
        compiler_params=pltpu.CompilerParams(vmem_limit_bytes=52 * 2**20),
        cost_estimate=pl.CostEstimate(flops=8 * 10**9, bytes_accessed=20 * 2**20, transcendentals=0),
        name="backward_tiles",
    )(order, dests, *scalars, tiles, *arrays, *after)


def weight_kernel(aggregate_ref, grad_ref, offset_ref, *refs):
    grads = grad_ref[...]
    sums = jnp.sum(grads.astype(F32), axis=0, keepdims=True)
    refs[-1][...] = (
        lax.dot_general(
            aggregate_ref[...], grads, (((0,), (0,)), ((), ())), preferred_element_type=F32
        )
        + offset_ref[...] * sums
    )


def weight_terms(aggregate, grads, offset, after):
    width = grads.shape[1]
    return pl.pallas_call(
        weight_kernel,
        in_specs=[VMEM] * 3 + [ANY] * len(after),
        out_specs=VMEM,
        out_shape=jax.ShapeDtypeStruct((width, width), F32),
        name="weight_terms",
    )(aggregate, grads, jnp.broadcast_to(offset[:, None], (width, width)), *after)


def copies_of_all(value, axis):
    count = lax.axis_size(axis)
    return lax.all_to_all(jnp.broadcast_to(value[None], (count, *value.shape)), axis, 0, 0)


def on_device(
    features,
    weight,
    norm_gain,
    norm_shift,
    tile_values,
    tile_rows,
    tile_cols,
    tile_counts,
    cotangent,
):
    tiles, rows, cols, counts = tile_values[0], tile_rows[0], tile_cols[0], tile_counts[0]
    local_rows, width = features.shape
    tile = tiles.shape[-1]
    col_tiles = local_rows // tile
    blk_count = lax.axis_size("blk")
    rep_count = lax.axis_size("rep")
    node_count = local_rows * blk_count * rep_count
    blk, rep = lax.axis_index("blk"), lax.axis_index("rep")
    z, y_low, core = blk // 4, (blk // 2) % 2, blk % 2
    y_high, x = rep // RING, rep % RING
    own_core = jnp.stack([blk_index(z + a + RING, y_low + b, core) for a, b in PLACES])
    other_core = own_core + (1 - 2 * core)
    dests = jnp.stack([rep_index(x + a + RING, y_high + b) for a, b in PLACES])
    *blk_tree, across = blk_links()
    rep_tree = rep_links()

    mine, _ = gather_tree(features.reshape(col_tiles, tile, width), *blk_tree)
    theirs = [[(first, across(array)) for first, array in parts] for parts in mine]
    backwards = slice(None, None, -1)
    scalars = (rows, cols, counts)
    order = jnp.stack([own_core[backwards], other_core[backwards]], axis=1).reshape(-1)
    shards = [parts for both in zip(mine[backwards], theirs[backwards]) for parts in both]
    up, down, pair = rep_tree
    low, high, *rest, offset = forward_tiles(order, dests, scalars, tiles, shards)
    blocks = dict(zip(PLACES[1:], rest))
    leaving = scatter_first((low, high), blocks, up, down)
    leaving, _ = scatter_second(leaving, blocks, *rep_tree)
    shifted = scatter_third(leaving, blocks[0, 0], *rep_tree).reshape(local_rows, width)
    aggregate = shifted.astype(BF16)
    projected = jnp.dot(aggregate, weight, preferred_element_type=F32)
    own_mean = jnp.sum(projected, axis=0) / local_rows
    own_square = jnp.sum((projected - own_mean) ** 2, axis=0)
    moved = jnp.dot(offset, weight.astype(F32), precision=lax.Precision.HIGHEST)
    everyone = copies_of_all(
        jnp.stack([own_mean, own_square, moved[0], offset[0]]), ("blk", "rep")
    ).reshape(blk_count, rep_count, 4, width)
    moves = jnp.sum(everyone[:, :, 2], axis=1)
    means = everyone[:, :, 0] + moves[:, None]
    feat_mean = jnp.sum(means, axis=(0, 1)) / (blk_count * rep_count)
    square_sum = jnp.sum(everyone[:, :, 1], axis=(0, 1)) + local_rows * jnp.sum(
        (means - feat_mean) ** 2, axis=(0, 1)
    )
    group = lax.dynamic_index_in_dim(everyone, blk, 0, keepdims=False)
    group_moved, group_offset = jnp.sum(group[:, 2], axis=0), jnp.sum(group[:, 3], axis=0)
    inv_std = lax.rsqrt(square_sum / node_count + norm_eps)
    normed = (projected + (group_moved - feat_mean)) * inv_std
    affine = norm_gain * normed + norm_shift
    gate_value = jax.nn.sigmoid(affine)
    output = (affine * gate_value).astype(BF16)
    grad_affine = cotangent.astype(F32) * gate_value * (1.0 + affine * (1.0 - gate_value))
    grad_beta, grad_gamma = jnp.sum(
        copies_of_all(
            jnp.stack([jnp.sum(grad_affine, axis=0), jnp.sum(grad_affine * normed, axis=0)]),
            ("blk", "rep"),
        ),
        axis=0,
    )
    grad_summed = (
        norm_gain
        * inv_std
        * (grad_affine - grad_beta / node_count - normed * grad_gamma / node_count)
    ).astype(BF16)

    sent = lax.dot_general(
        grad_summed, weight, (((1,), (1,)), ((), ())), preferred_element_type=F32
    ).astype(BF16)
    def weight_pieces():
        term = weight_terms(aggregate, grad_summed, group_offset, [])
        return [lax.all_to_all(term.reshape(blk_count, -1, width), "blk", 0, 0)]

    grads, [pieces] = gather_tree(
        sent.reshape(col_tiles, tile, width), *rep_tree, weight_pieces
    )
    piece = jnp.sum(pieces, axis=0)
    terms = copies_of_all(piece, "rep")

    half = col_tiles // 2
    sizes = (half, half, *(col_tiles,) * (len(PLACES) - 1))
    arrays = backward_tiles(
        sizes * 2,
        jnp.concatenate([other_core, own_core]),
        dests,
        scalars,
        tiles,
        grads,
    )
    given, kept = arrays[: len(sizes)], arrays[len(sizes) :]
    low, high, *rest = [b.astype(F32) + across(a).astype(F32) for a, b in zip(given, kept)]
    products = dict(zip(PLACES[1:], rest))
    up, down, pair = blk_tree
    leaving = scatter_first((low, high), products, up, down)
    leaving, [terms] = scatter_second(leaving, products, *blk_tree, [terms])
    grad_x = scatter_third(leaving, products[0, 0], *blk_tree).astype(BF16)
    grad_w = copies_of_all(jnp.sum(terms, axis=0), "blk").reshape(weight.shape)
    return (output, grad_x.reshape(local_rows, width), grad_w, grad_gamma, grad_beta)


def solution(mesh):
    return jax.shard_map(
        on_device,
        mesh=mesh,
        in_specs=(
            P(("blk", "rep"), None),
            P(),
            P(),
            P(),
            P("blk", "rep", None, None, None),
            P("blk", "rep", None),
            P("blk", "rep", None),
            P("blk", "rep"),
            P(("blk", "rep"), None),
        ),
        out_specs=(P(("blk", "rep"), None), P(("blk", "rep"), None), P(), P(), P()),
        check_vma=False,
    )
```

time: 296 us -> 311 us (1.051)
  Pallas kernels: 62.8 us -> 36.9 us
  local copies, waits for them, and re-layouts: 13.3 us -> 32.7 us
  blocking collectives: 29.1 us -> 43.1 us
  waiting for transfers between devices: 99.3 us -> 85.6 us
  starting transfers between devices: 69.1 us -> 81.6 us
  other arithmetic: 19.2 us -> 28.4 us
    pallas_call x6 -> x12, Pallas kernels: 60.5 us -> 34.6 us  [the longest x1 19.5 us: backward_tiles(): pl.pallas_call(functools.partial(backward_kernel, layout, sizes, len(afte...]
    unnamed x67 -> x109, local copies, waits for them, and re-layouts: 3.2 us -> 25.8 us
    ppermute x28 -> x34, waiting for transfers between devices: 46.6 us -> 29.9 us  [link(): return lambda value: lax.ppermute(value, 'blk', pairs)]
    all_to_all x0 -> x1, blocking collectives: none -> 14 us  [weight_pieces(): return [lax.all_to_all(term.reshape(blk_count, -1, width), 'blk', 0, 0)]]
    ppermute x28 -> x34, starting transfers between devices: 29.7 us -> 39 us  [link(): return lambda value: lax.ppermute(value, 'blk', pairs)]
    ppermute x16, waiting for transfers between devices: 28.3 us -> 37.3 us  [link(): return lambda value: lax.ppermute(value, 'rep', pairs)]
    ppermute x16, starting transfers between devices: 23.3 us -> 29.3 us  [link(): return lambda value: lax.ppermute(value, 'rep', pairs)]
    all_to_all x1 -> x0, starting transfers between devices: 5.39 us -> none  [on_device(): lax.all_to_all(weight_term.reshape(blk_count, -1, width), 'blk', 0, 0)]
  transfers between devices with their start and end apart: 47 -> 52, of which waited for: 19 -> 20; matrix products, arithmetic and copies ran while one was open for 6% -> 7% of each run, Pallas kernels for 7% -> 1%
where the time goes in v4:
time: 311 us; the launch traced here: 310 us
  waiting for transfers between devices  85.6 us (28%)
  starting transfers between devices  81.6 us (26%)
  blocking collectives  43.1 us (14%)
  Pallas kernels  36.9 us (12%)
  local copies, waits for them, and re-layouts  32.7 us (11%)
  other arithmetic  28.4 us (9%)
    ppermute x34, starting transfers between devices, link(): return lambda value: lax.ppermute(value, 'blk', pairs)  39 us
    ppermute x16, waiting for transfers between devices, link(): return lambda value: lax.ppermute(value, 'rep', pairs)  37.3 us
    ppermute x34, waiting for transfers between devices, link(): return lambda value: lax.ppermute(value, 'blk', pairs)  29.9 us
    ppermute x16, starting transfers between devices, link(): return lambda value: lax.ppermute(value, 'rep', pairs)  29.3 us
    all_to_all x2, blocking collectives, copies_of_all(): lax.all_to_all(jnp.broadcast_to(value[None], (count, *value.shape)), axis...  29.1 us
    unnamed x109, local copies, waits for them, and re-layouts  25.8 us
    pallas_call x1, Pallas kernels, backward_tiles(): pl.pallas_call(functools.partial(backward_kernel, layout, sizes, len(afte...  19.5 us
    all_to_all x2, waiting for transfers between devices, copies_of_all(): lax.all_to_all(jnp.broadcast_to(value[None], (count, *value.shape)), axis...  18.4 us
  transfers between devices with their start and end apart: 52, of which 20 were waited for; matrix products, arithmetic and copies ran while one was open for 7% of the time, Pallas kernels for 1%

profile of v4, /device:TPU:1, one launch (start us, length us, event | category | flops | bytes accessed | tf_op | source)
XLA Modules:
  0.0 310.1 jit_solution(12478466768822586801)
XLA Ops:
  2.9 3.8 %collective-permute-start.2 = (bf16[8,128,256]{2,1,0:T(8,128)(2,1)}, bf16[8,128,256]{2,1,0:T(8,128)(2,1)S(1)}, u32[]{:S(2)}, u32[]{:S(2)}) collective-permute-start(bf16[8,128,256]{2,1,0:T(8,128)(2,1)} %bitcast.59), channel_id=1, source_target_pairs={{0,96},{8,104},{16,112},{24,120},{32,0},{40,8},{48,16},{56,24},{64... | collective-permute-start | bytes 1572872 | tf_op jit(solution)/shard_map/ppermute | solution.py:33
  6.6 7.7 %collective-permute-done.3.refs_2_ = bf16[8,128,256]{2,1,0:T(8,128)(2,1)S(1)} collective-permute-done((bf16[8,128,256]{2,1,0:T(8,128)(2,1)}, bf16[8,128,256]{2,1,0:T(8,128)(2,1)S(1)}, u32[]{:S(2)}, u32[]{:S(2)}) %collective-permute-start.3) | collective-permute-done | bytes 524320 | tf_op jit(solution)/shard_map/ppermute | solution.py:33
  14.3 2.9 collective-permute-done.2.refs_1_
  17.2 3.0 collective-permute-done.1.refs_0_
  22.6 3.0 collective-permute-start
  25.7 6.9 %collective-permute-done.8.refs_1_ = bf16[8,128,256]{2,1,0:T(8,128)(2,1)} collective-permute-done((bf16[8,128,256]{2,1,0:T(8,128)(2,1)}, bf16[8,128,256]{2,1,0:T(8,128)(2,1)}, u32[]{:S(2)}, u32[]{:S(2)}) %collective-permute-start.8) | collective-permute-done | bytes 524320 | tf_op jit(solution)/shard_map/ppermute | solution.py:33
  32.6 3.1 collective-permute-start.6
  43.4 3.5 %collective-permute-done.13.refs_14_ = bf16[4,128,256]{2,1,0:T(8,128)(2,1)S(1)} collective-permute-done((bf16[4,128,256]{2,1,0:T(8,128)(2,1)S(1)}, bf16[4,128,256]{2,1,0:T(8,128)(2,1)S(1)}, u32[]{:S(2)}, u32[]{:S(2)}) %collective-permute-start.13) | collective-permute-done | bytes 262176 | tf_op jit(solution)/shard_map/ppermute | solution.py:33
  63.2 15.1 %forward_tiles.1 = (bf16[4,128,256]{2,1,0:T(8,128)(2,1)S(1)}, bf16[4,128,256]{2,1,0:T(8,128)(2,1)S(1)}, bf16[8,128,256]{2,1,0:T(8,128)(2,1)S(1)}, bf16[8,128,256...) custom-call(s32[16]{0:T(128)S(1)} %reshape.73.order_ref, ...), custom_call_target="tpu_custom_call" | custom-call | flops 6000000000 | bytes 31457280 | tf_op jit(solution)/shard_map/forward_tiles/pallas_call | solution.py:243
  85.7 4.4 %collective-permute-done.18.refs_0_ = bf16[4,128,256]{2,1,0:T(8,128)(2,1)S(1)} collective-permute-done((bf16[4,128,256]{2,1,0:T(8,128)(2,1)S(1)}, bf16[4,128,256]{2,1,0:T(8,128)(2,1)S(1)}, u32[]{:S(2)}, u32[]{:S(2)}) %collective-permute-start.18) | collective-permute-done | bytes 262176 | tf_op jit(solution)/shard_map/ppermute | solution.py:43
  93.9 4.5 %collective-permute-start.20 = (bf16[8,128,256]{2,1,0:T(8,128)(2,1)S(1)}, bf16[8,128,256]{2,1,0:T(8,128)(2,1)S(1)}, u32[]{:S(2)}, u32[]{:S(2)}) collective-permute-start(bf16[8,128,256]{2,1,0:T(8,128)(2,1)S(1)} %add_convert_fusion.11), channel_id=1, source_target_pairs={{0,4},{4,0},{1,5},{5,1},{2,6},{6,2},{3,7},{7,3},{8,12},{12,8},{9,1... | collective-permute-start | bytes 1572872 | tf_op jit(solution)/shard_map/ppermute | solution.py:43
  98.4 2.8 collective-permute-start.17
  101.2 2.5 collective-permute-done.22.refs_2_
  103.7 3.1 collective-permute-done.20.refs_0_
  109.1 5.2 %collective-permute-start.23 = (bf16[8,128,256]{2,1,0:T(8,128)(2,1)S(1)}, bf16[8,128,256]{2,1,0:T(8,128)(2,1)S(1)}, u32[]{:S(2)}, u32[]{:S(2)}) collective-permute-start(bf16[8,128,256]{2,1,0:T(8,128)(2,1)S(1)} %add_convert_fusion.9), channel_id=1, source_target_pairs={{0,3},{4,7},{1,0},{5,4},{2,1},{6,5},{3,2},{7,6},{8,11},{12,15},{9,... | collective-permute-start | bytes 1572872 | tf_op jit(solution)/shard_map/ppermute | solution.py:43
  115.5 4.0 %collective-permute-start.24 = (bf16[8,128,256]{2,1,0:T(8,128)(2,1)S(1)}, bf16[8,128,256]{2,1,0:T(8,128)(2,1)}, u32[]{:S(2)}, u32[]{:S(2)}) collective-permute-start(bf16[8,128,256]{2,1,0:T(8,128)(2,1)S(1)} %add_convert_fusion.8), channel_id=1, source_target_pairs={{0,4},{4,0},{1,5},{5,1},{2,6},{6,2},{3,7},{7,3},{8,12},{12,8},{9,1... | collective-permute-start | bytes 1572872 | tf_op jit(solution)/shard_map/ppermute | solution.py:43
  119.6 5.0 %collective-permute-done.23.refs_1_ = bf16[8,128,256]{2,1,0:T(8,128)(2,1)S(1)} collective-permute-done((bf16[8,128,256]{2,1,0:T(8,128)(2,1)S(1)}, bf16[8,128,256]{2,1,0:T(8,128)(2,1)S(1)}, u32[]{:S(2)}, u32[]{:S(2)}) %collective-permute-start.23) | collective-permute-done | bytes 524320 | tf_op jit(solution)/shard_map/ppermute | solution.py:43
  124.6 4.8 %collective-permute-done.24.refs_2_ = bf16[8,128,256]{2,1,0:T(8,128)(2,1)} collective-permute-done((bf16[8,128,256]{2,1,0:T(8,128)(2,1)S(1)}, bf16[8,128,256]{2,1,0:T(8,128)(2,1)}, u32[]{:S(2)}, u32[]{:S(2)}) %collective-permute-start.24) | collective-permute-done | bytes 524320 | tf_op jit(solution)/shard_map/ppermute | solution.py:43
  132.5 9.5 %all-to-all-start = ((f32[128,4,256]{2,1,0:T(4,128)}), f32[128,4,256]{2,1,0:T(4,128)S(1)}, u32[]{:S(2)}, u32[]{:S(2)}) async-start(f32[128,4,256]{2,1,0:T(4,128)} %broadcast_in_dim.10), calls=%async_computation | async-start | bytes 1048576 | tf_op jit(solution)/shard_map/all_to_all | solution.py:381
  142.0 13.9 %all-to-all-done = f32[128,4,256]{2,1,0:T(4,128)S(1)} async-done(((f32[128,4,256]{2,1,0:T(4,128)}), f32[128,4,256]{2,1,0:T(4,128)S(1)}, u32[]{:S(2)}, u32[]{:S(2)}) %all-to-all-start) | async-done | bytes 524320 | tf_op jit(solution)/shard_map/all_to_all | solution.py:381
  158.1 15.4 %all_to_all.25 = f32[128,2,256]{2,1,0:T(2,128)S(1)} all-to-all(f32[128,2,256]{2,1,0:T(2,128)S(1)} %broadcast_in_dim.11), channel_id=1, replica_groups=mesh['blk'=16,'rep'=8] {'blk','rep'}, dimensions={0} | all-to-all | bytes 524288 | tf_op jit(solution)/shard_map/all_to_all | solution.py:381
  174.2 2.6 multiply_convert_fusion
  179.7 11.9 %collective-permute-done.27.refs_2_ = bf16[8,128,256]{2,1,0:T(8,128)(2,1)S(1)} collective-permute-done((bf16[8,128,256]{2,1,0:T(8,128)(2,1)S(1)}, bf16[8,128,256]{2,1,0:T(8,128)(2,1)S(1)}, u32[]{:S(2)}, u32[]{:S(2)}) %collective-permute-start.27) | collective-permute-done | bytes 524320 | tf_op jit(solution)/shard_map/ppermute | solution.py:43
  199.9 14.0 %all_to_all.26.refs_3_ = f32[16,16,256]{2,1,0:T(8,128)} all-to-all(f32[16,16,256]{2,1,0:T(8,128)} %bitcast.76), channel_id=1, replica_groups=mesh['blk'=16,'rep'=8] {'blk'}, dimensions={0} | all-to-all | bytes 524288 | tf_op jit(solution)/shard_map/all_to_all | solution.py:463
  217.5 2.7 collective-permute-start.31
  220.9 4.6 %collective-permute-done.32.refs_1_ = bf16[4,128,256]{2,1,0:T(8,128)(2,1)S(1)} collective-permute-done((bf16[4,128,256]{2,1,0:T(8,128)(2,1)S(1)}, bf16[4,128,256]{2,1,0:T(8,128)(2,1)S(1)}, u32[]{:S(2)}, u32[]{:S(2)}) %collective-permute-start.32) | collective-permute-done | bytes 262176 | tf_op jit(solution)/shard_map/ppermute | solution.py:43
  225.5 19.5 %backward_tiles.1 = (bf16[4,128,256]{2,1,0:T(8,128)(2,1)S(1)}, bf16[4,128,256]{2,1,0:T(8,128)(2,1)S(1)}, bf16[8,128,256]{2,1,0:T(8,128)(2,1)}, bf16[8,128,256]{2...) custom-call(s32[16]{0:T(128)S(1)} %concatenate.4.order_ref, ...), custom_call_target="tpu_custom_call" | custom-call | flops 8000000000 | bytes 20971520 | tf_op jit(solution)/shard_map/backward_tiles/pallas_call | solution.py:338
  254.9 3.9 %collective-permute-done.39.refs_0_ = bf16[4,128,256]{2,1,0:T(8,128)(2,1)S(1)} collective-permute-done((bf16[4,128,256]{2,1,0:T(8,128)(2,1)S(1)}, bf16[4,128,256]{2,1,0:T(8,128)(2,1)S(1)}, u32[]{:S(2)}, u32[]{:S(2)}) %collective-permute-start.39) | collective-permute-done | bytes 262176 | tf_op jit(solution)/shard_map/ppermute | solution.py:33
  270.5 3.9 %all-to-all-start.3 = ((f32[8,16,256]{2,1,0:T(8,128)}), f32[8,16,256]{2,1,0:T(8,128)S(1)}, u32[]{:S(2)}, u32[]{:S(2)}) async-start(f32[8,16,256]{2,1,0:T(8,128)} %broadcast_in_dim.13), calls=%async_computation.3 | async-start | bytes 262144 | tf_op jit(solution)/shard_map/all_to_all | solution.py:381
  276.7 4.6 %all-to-all-done.3.refs_3_ = f32[8,16,256]{2,1,0:T(8,128)S(1)} async-done(((f32[8,16,256]{2,1,0:T(8,128)}), f32[8,16,256]{2,1,0:T(8,128)S(1)}, u32[]{:S(2)}, u32[]{:S(2)}) %all-to-all-start.3) | async-done | bytes 131104 | tf_op jit(solution)/shard_map/all_to_all | solution.py:381
  291.3 13.7 %all_to_all.27 = f32[16,16,256]{2,1,0:T(8,128)S(1)} all-to-all(f32[16,16,256]{2,1,0:T(8,128)S(1)} %broadcast_in_dim.14), channel_id=1, replica_groups=mesh['blk'=16,'rep'=8] {'blk'}, dimensions={0} | all-to-all | bytes 524288 | tf_op jit(solution)/shard_map/all_to_all | solution.py:381
  306.8 2.7 add_convert_fusion
  (250 shorter events, 101.3 us)
Async XLA Ops:
  0.6 13.7 %collective-permute-start.3 = (bf16[8,128,256]{2,1,0:T(8,128)(2,1)}, bf16[8,128,256]{2,1,0:T(8,128)(2,1)S(1)}, u32[]{:S(2)}, u32[]{:S(2)}) collective-permute-start(bf16[8,128,256]{2,1,0:T(8,128)(2,1)} %bitcast.58), channel_id=1, source_target_pairs={{0,16},{8,24},{16,0},{24,8},{32,48},{40,56},{48,32},{56,40},{64,80... | collective-permute-start | bytes 1572872 | tf_op jit(solution)/shard_map/ppermute | solution.py:33
  2.9 14.3 %collective-permute-start.2 = (bf16[8,128,256]{2,1,0:T(8,128)(2,1)}, bf16[8,128,256]{2,1,0:T(8,128)(2,1)S(1)}, u32[]{:S(2)}, u32[]{:S(2)}) collective-permute-start(bf16[8,128,256]{2,1,0:T(8,128)(2,1)} %bitcast.59), channel_id=1, source_target_pairs={{0,96},{8,104},{16,112},{24,120},{32,0},{40,8},{48,16},{56,24},{64... | collective-permute-start | bytes 1572872 | tf_op jit(solution)/shard_map/ppermute | solution.py:33
  6.6 13.6 %collective-permute-start.1 = (bf16[8,128,256]{2,1,0:T(8,128)(2,1)}, bf16[8,128,256]{2,1,0:T(8,128)(2,1)S(1)}, u32[]{:S(2)}, u32[]{:S(2)}) collective-permute-start(bf16[8,128,256]{2,1,0:T(8,128)(2,1)} %bitcast.60), channel_id=1, source_target_pairs={{0,32},{8,40},{16,48},{24,56},{32,64},{40,72},{48,80},{56,88},{64,... | collective-permute-start | bytes 1572872 | tf_op jit(solution)/shard_map/ppermute | solution.py:33
  21.0 11.6 %collective-permute-start.8 = (bf16[8,128,256]{2,1,0:T(8,128)(2,1)}, bf16[8,128,256]{2,1,0:T(8,128)(2,1)}, u32[]{:S(2)}, u32[]{:S(2)}) collective-permute-start(bf16[8,128,256]{2,1,0:T(8,128)(2,1)} %get-tuple-element.65.refs_6_), channel_id=1, source_target_pairs={{0,96},{8,104},{16,112},{24,120},{32,0},{40,8},{48,16},{56,24},{64... | collective-permute-start | bytes 1572872 | tf_op jit(solution)/shard_map/ppermute | solution.py:33
  22.1 13.6 %collective-permute-start.9 = (bf16[8,128,256]{2,1,0:T(8,128)(2,1)}, bf16[8,128,256]{2,1,0:T(8,128)(2,1)S(1)}, u32[]{:S(2)}, u32[]{:S(2)}) collective-permute-start(bf16[8,128,256]{2,1,0:T(8,128)(2,1)} %get-tuple-element.63.refs_2_), channel_id=1, source_target_pairs={{0,32},{8,40},{16,48},{24,56},{32,64},{40,72},{48,80},{56,88},{64,... | collective-permute-start | bytes 1572872 | tf_op jit(solution)/shard_map/ppermute | solution.py:33
  22.5 15.4 %collective-permute-start.7 = (bf16[8,128,256]{2,1,0:T(8,128)(2,1)}, bf16[8,128,256]{2,1,0:T(8,128)(2,1)}, u32[]{:S(2)}, u32[]{:S(2)}) collective-permute-start(bf16[8,128,256]{2,1,0:T(8,128)(2,1)} %get-tuple-element.63.refs_2_), channel_id=1, source_target_pairs={{0,16},{8,24},{16,0},{24,8},{32,48},{40,56},{48,32},{56,40},{64,80... | collective-permute-start | bytes 1572872 | tf_op jit(solution)/shard_map/ppermute | solution.py:33
  22.6 18.1 %collective-permute-start = (bf16[8,128,256]{2,1,0:T(8,128)(2,1)}, bf16[8,128,256]{2,1,0:T(8,128)(2,1)S(1)}, u32[]{:S(2)}, u32[]{:S(2)}) collective-permute-start(bf16[8,128,256]{2,1,0:T(8,128)(2,1)} %bitcast.61), channel_id=1, source_target_pairs={{0,8},{8,0},{16,24},{24,16},{32,40},{40,32},{48,56},{56,48},{64,72... | collective-permute-start | bytes 1572872 | tf_op jit(solution)/shard_map/ppermute | solution.py:33
  25.6 15.7 %collective-permute-start.5 = (bf16[8,128,256]{2,1,0:T(8,128)(2,1)}, bf16[8,128,256]{2,1,0:T(8,128)(2,1)S(1)}, u32[]{:S(2)}, u32[]{:S(2)}) collective-permute-start(bf16[8,128,256]{2,1,0:T(8,128)(2,1)} %get-tuple-element.64.refs_4_), channel_id=1, source_target_pairs={{0,8},{8,0},{16,24},{24,16},{32,40},{40,32},{48,56},{56,48},{64,72... | collective-permute-start | bytes 1572872 | tf_op jit(solution)/shard_map/ppermute | solution.py:33
  84.3 16.9 %collective-permute-start.21 = (bf16[8,128,256]{2,1,0:T(8,128)(2,1)}, bf16[8,128,256]{2,1,0:T(8,128)(2,1)}, u32[]{:S(2)}, u32[]{:S(2)}) collective-permute-start(bf16[8,128,256]{2,1,0:T(8,128)(2,1)} %get-tuple-element.76), channel_id=1, source_target_pairs={{0,3},{4,7},{1,0},{5,4},{2,1},{6,5},{3,2},{7,6},{8,11},{12,15},{9,... | collective-permute-start | bytes 1572872 | tf_op jit(solution)/shard_map/ppermute | solution.py:43
  93.9 12.9 %collective-permute-start.20 = (bf16[8,128,256]{2,1,0:T(8,128)(2,1)S(1)}, bf16[8,128,256]{2,1,0:T(8,128)(2,1)S(1)}, u32[]{:S(2)}, u32[]{:S(2)}) collective-permute-start(bf16[8,128,256]{2,1,0:T(8,128)(2,1)S(1)} %add_convert_fusion.11), channel_id=1, source_target_pairs={{0,4},{4,0},{1,5},{5,1},{2,6},{6,2},{3,7},{7,3},{8,12},{12,8},{9,1... | collective-permute-start | bytes 1572872 | tf_op jit(solution)/shard_map/ppermute | solution.py:43
  98.4 21.2 %collective-permute-start.17 = (bf16[8,128,256]{2,1,0:T(8,128)(2,1)}, bf16[8,128,256]{2,1,0:T(8,128)(2,1)S(1)}, u32[]{:S(2)}, u32[]{:S(2)}) collective-permute-start(bf16[8,128,256]{2,1,0:T(8,128)(2,1)} %copy-done.25), channel_id=1, source_target_pairs={{0,1},{4,5},{1,2},{5,6},{2,3},{6,7},{3,0},{7,4},{8,9},{12,13},{9,1... | collective-permute-start | bytes 1572872 | tf_op jit(solution)/shard_map/ppermute | solution.py:43
  109.1 15.4 %collective-permute-start.23 = (bf16[8,128,256]{2,1,0:T(8,128)(2,1)S(1)}, bf16[8,128,256]{2,1,0:T(8,128)(2,1)S(1)}, u32[]{:S(2)}, u32[]{:S(2)}) collective-permute-start(bf16[8,128,256]{2,1,0:T(8,128)(2,1)S(1)} %add_convert_fusion.9), channel_id=1, source_target_pairs={{0,3},{4,7},{1,0},{5,4},{2,1},{6,5},{3,2},{7,6},{8,11},{12,15},{9,... | collective-permute-start | bytes 1572872 | tf_op jit(solution)/shard_map/ppermute | solution.py:43
  115.5 13.9 %collective-permute-start.24 = (bf16[8,128,256]{2,1,0:T(8,128)(2,1)S(1)}, bf16[8,128,256]{2,1,0:T(8,128)(2,1)}, u32[]{:S(2)}, u32[]{:S(2)}) collective-permute-start(bf16[8,128,256]{2,1,0:T(8,128)(2,1)S(1)} %add_convert_fusion.8), channel_id=1, source_target_pairs={{0,4},{4,0},{1,5},{5,1},{2,6},{6,2},{3,7},{7,3},{8,12},{12,8},{9,1... | collective-permute-start | bytes 1572872 | tf_op jit(solution)/shard_map/ppermute | solution.py:43
  132.5 23.4 %all-to-all-start = ((f32[128,4,256]{2,1,0:T(4,128)}), f32[128,4,256]{2,1,0:T(4,128)S(1)}, u32[]{:S(2)}, u32[]{:S(2)}) async-start(f32[128,4,256]{2,1,0:T(4,128)} %broadcast_in_dim.10), calls=%async_computation | async-start | bytes 1048576 | tf_op jit(solution)/shard_map/all_to_all | solution.py:381
  177.1 14.4 %collective-permute-start.27 = (bf16[8,128,256]{2,1,0:T(8,128)(2,1)S(1)}, bf16[8,128,256]{2,1,0:T(8,128)(2,1)S(1)}, u32[]{:S(2)}, u32[]{:S(2)}) collective-permute-start(bf16[8,128,256]{2,1,0:T(8,128)(2,1)S(1)} %bitcast.77), channel_id=1, source_target_pairs={{0,4},{4,0},{1,5},{5,1},{2,6},{6,2},{3,7},{7,3},{8,12},{12,8},{9,1... | collective-permute-start | bytes 1572872 | tf_op jit(solution)/shard_map/ppermute | solution.py:43
  178.2 13.3 %collective-permute-start.26 = (bf16[8,128,256]{2,1,0:T(8,128)(2,1)S(1)}, bf16[8,128,256]{2,1,0:T(8,128)(2,1)S(1)}, u32[]{:S(2)}, u32[]{:S(2)}) collective-permute-start(bf16[8,128,256]{2,1,0:T(8,128)(2,1)S(1)} %bitcast.78), channel_id=1, source_target_pairs={{0,3},{4,7},{1,0},{5,4},{2,1},{6,5},{3,2},{7,6},{8,11},{12,15},{9,... | collective-permute-start | bytes 1572872 | tf_op jit(solution)/shard_map/ppermute | solution.py:43
  179.0 13.7 %collective-permute-start.25 = (bf16[8,128,256]{2,1,0:T(8,128)(2,1)S(1)}, bf16[8,128,256]{2,1,0:T(8,128)(2,1)S(1)}, u32[]{:S(2)}, u32[]{:S(2)}) collective-permute-start(bf16[8,128,256]{2,1,0:T(8,128)(2,1)S(1)} %bitcast.79), channel_id=1, source_target_pairs={{0,1},{4,5},{1,2},{5,6},{2,3},{6,7},{3,0},{7,4},{8,9},{12,13},{9,1... | collective-permute-start | bytes 1572872 | tf_op jit(solution)/shard_map/ppermute | solution.py:43
  193.5 20.4 %collective-permute-start.29 = (bf16[8,128,256]{2,1,0:T(8,128)(2,1)}, bf16[8,128,256]{2,1,0:T(8,128)(2,1)S(1)}, u32[]{:S(2)}, u32[]{:S(2)}) collective-permute-start(bf16[8,128,256]{2,1,0:T(8,128)(2,1)} %get-tuple-element.88.refs_5_), channel_id=1, source_target_pairs={{0,3},{4,7},{1,0},{5,4},{2,1},{6,5},{3,2},{7,6},{8,11},{12,15},{9,... | collective-permute-start | bytes 1572872 | tf_op jit(solution)/shard_map/ppermute | solution.py:43
  194.6 19.3 %collective-permute-start.30 = (bf16[8,128,256]{2,1,0:T(8,128)(2,1)}, bf16[8,128,256]{2,1,0:T(8,128)(2,1)}, u32[]{:S(2)}, u32[]{:S(2)}) collective-permute-start(bf16[8,128,256]{2,1,0:T(8,128)(2,1)} %get-tuple-element.87.refs_7_), channel_id=1, source_target_pairs={{0,1},{4,5},{1,2},{5,6},{2,3},{6,7},{3,0},{7,4},{8,9},{12,13},{9,1... | collective-permute-start | bytes 1572872 | tf_op jit(solution)/shard_map/ppermute | solution.py:43
  194.9 19.0 %collective-permute-start.28 = (bf16[8,128,256]{2,1,0:T(8,128)(2,1)}, bf16[8,128,256]{2,1,0:T(8,128)(2,1)S(1)}, u32[]{:S(2)}, u32[]{:S(2)}) collective-permute-start(bf16[8,128,256]{2,1,0:T(8,128)(2,1)} %get-tuple-element.87.refs_7_), channel_id=1, source_target_pairs={{0,4},{4,0},{1,5},{5,1},{2,6},{6,2},{3,7},{7,3},{8,12},{12,8},{9,1... | collective-permute-start | bytes 1572872 | tf_op jit(solution)/shard_map/ppermute | solution.py:43
  247.5 26.9 %collective-permute-start.34 = (bf16[8,128,256]{2,1,0:T(8,128)(2,1)}, bf16[8,128,256]{2,1,0:T(8,128)(2,1)S(1)}, u32[]{:S(2)}, u32[]{:S(2)}) collective-permute-start(bf16[8,128,256]{2,1,0:T(8,128)(2,1)} %get-tuple-element.96), channel_id=1, source_target_pairs={{0,8},{8,0},{16,24},{24,16},{32,40},{40,32},{48,56},{56,48},{64,72... | collective-permute-start | bytes 1572872 | tf_op jit(solution)/shard_map/ppermute | solution.py:33
  247.6 12.6 %collective-permute-start.37 = (bf16[8,128,256]{2,1,0:T(8,128)(2,1)}, bf16[8,128,256]{2,1,0:T(8,128)(2,1)}, u32[]{:S(2)}, u32[]{:S(2)}) collective-permute-start(bf16[8,128,256]{2,1,0:T(8,128)(2,1)} %get-tuple-element.100), channel_id=1, source_target_pairs={{0,8},{8,0},{16,24},{24,16},{32,40},{40,32},{48,56},{56,48},{64,72... | collective-permute-start | bytes 1572872 | tf_op jit(solution)/shard_map/ppermute | solution.py:33
  248.2 16.7 %collective-permute-start.45 = (bf16[8,128,256]{2,1,0:T(8,128)(2,1)}, bf16[8,128,256]{2,1,0:T(8,128)(2,1)S(1)}, u32[]{:S(2)}, u32[]{:S(2)}) collective-permute-start(bf16[8,128,256]{2,1,0:T(8,128)(2,1)} %get-tuple-element.109), channel_id=1, source_target_pairs={{0,8},{8,0},{16,24},{24,16},{32,40},{40,32},{48,56},{56,48},{64,72... | collective-permute-start | bytes 1572872 | tf_op jit(solution)/shard_map/ppermute | solution.py:33
  258.8 17.9 %collective-permute-start.44 = (bf16[8,128,256]{2,1,0:T(8,128)(2,1)}, bf16[8,128,256]{2,1,0:T(8,128)(2,1)S(1)}, u32[]{:S(2)}, u32[]{:S(2)}) collective-permute-start(bf16[8,128,256]{2,1,0:T(8,128)(2,1)} %add_convert_fusion.4), channel_id=1, source_target_pairs={{0,96},{8,104},{16,112},{24,120},{32,0},{40,8},{48,16},{56,24},{64... | collective-permute-start | bytes 1572872 | tf_op jit(solution)/shard_map/ppermute | solution.py:33
  262.4 18.9 %collective-permute-start.42 = (bf16[8,128,256]{2,1,0:T(8,128)(2,1)}, bf16[8,128,256]{2,1,0:T(8,128)(2,1)S(1)}, u32[]{:S(2)}, u32[]{:S(2)}) collective-permute-start(bf16[8,128,256]{2,1,0:T(8,128)(2,1)} %add_convert_fusion.5), channel_id=1, source_target_pairs={{0,16},{8,24},{16,0},{24,8},{32,48},{40,56},{48,32},{56,40},{64,80... | collective-permute-start | bytes 1572872 | tf_op jit(solution)/shard_map/ppermute | solution.py:33
  267.0 14.4 %collective-permute-start.46 = (bf16[8,128,256]{2,1,0:T(8,128)(2,1)}, bf16[8,128,256]{2,1,0:T(8,128)(2,1)S(1)}, u32[]{:S(2)}, u32[]{:S(2)}) collective-permute-start(bf16[8,128,256]{2,1,0:T(8,128)(2,1)} %add_convert_fusion.3), channel_id=1, source_target_pairs={{0,32},{8,40},{16,48},{24,56},{32,64},{40,72},{48,80},{56,88},{64,... | collective-permute-start | bytes 1572872 | tf_op jit(solution)/shard_map/ppermute | solution.py:33
  267.7 15.2 %collective-permute-start.36 = (bf16[8,128,256]{2,1,0:T(8,128)(2,1)}, bf16[8,128,256]{2,1,0:T(8,128)(2,1)}, u32[]{:S(2)}, u32[]{:S(2)}) collective-permute-start(bf16[8,128,256]{2,1,0:T(8,128)(2,1)} %get-tuple-element.98), channel_id=1, source_target_pairs={{0,8},{8,0},{16,24},{24,16},{32,40},{40,32},{48,56},{56,48},{64,72... | collective-permute-start | bytes 1572872 | tf_op jit(solution)/shard_map/ppermute | solution.py:33
  274.4 12.4 %collective-permute-start.48 = (bf16[8,128,256]{2,1,0:T(8,128)(2,1)}, bf16[8,128,256]{2,1,0:T(8,128)(2,1)}, u32[]{:S(2)}, u32[]{:S(2)}) collective-permute-start(bf16[8,128,256]{2,1,0:T(8,128)(2,1)} %get-tuple-element.115), channel_id=1, source_target_pairs={{0,8},{8,0},{16,24},{24,16},{32,40},{40,32},{48,56},{56,48},{64,72... | collective-permute-start | bytes 1572872 | tf_op jit(solution)/shard_map/ppermute | solution.py:33
  276.7 28.3 %collective-permute-start.35 = (bf16[8,128,256]{2,1,0:T(8,128)(2,1)}, bf16[8,128,256]{2,1,0:T(8,128)(2,1)S(1)}, u32[]{:S(2)}, u32[]{:S(2)}) collective-permute-start(bf16[8,128,256]{2,1,0:T(8,128)(2,1)} %add_convert_fusion.6), channel_id=1, source_target_pairs={{0,32},{8,40},{16,48},{24,56},{32,64},{40,72},{48,80},{56,88},{64,... | collective-permute-start | bytes 1572872 | tf_op jit(solution)/shard_map/ppermute | solution.py:33
  284.8 20.2 %collective-permute-start.47 = (bf16[8,128,256]{2,1,0:T(8,128)(2,1)S(1)}, bf16[8,128,256]{2,1,0:T(8,128)(2,1)S(1)}, u32[]{:S(2)}, u32[]{:S(2)}) collective-permute-start(bf16[8,128,256]{2,1,0:T(8,128)(2,1)S(1)} %add_convert_fusion.2), channel_id=1, source_target_pairs={{0,96},{8,104},{16,112},{24,120},{32,0},{40,8},{48,16},{56,24},{64... | collective-permute-start | bytes 1572872 | tf_op jit(solution)/shard_map/ppermute | solution.py:33
  288.3 16.7 %collective-permute-start.49 = (bf16[8,128,256]{2,1,0:T(8,128)(2,1)S(1)}, bf16[8,128,256]{2,1,0:T(8,128)(2,1)S(1)}, u32[]{:S(2)}, u32[]{:S(2)}) collective-permute-start(bf16[8,128,256]{2,1,0:T(8,128)(2,1)S(1)} %add_convert_fusion.1), channel_id=1, source_target_pairs={{0,16},{8,24},{16,0},{24,8},{32,48},{40,56},{48,32},{56,40},{64,80... | collective-permute-start | bytes 1572872 | tf_op jit(solution)/shard_map/ppermute | solution.py:33
  288.4 18.3 %collective-permute-start.33 = (bf16[8,128,256]{2,1,0:T(8,128)(2,1)}, bf16[8,128,256]{2,1,0:T(8,128)(2,1)S(1)}, u32[]{:S(2)}, u32[]{:S(2)}) collective-permute-start(bf16[8,128,256]{2,1,0:T(8,128)(2,1)} %get-tuple-element.94), channel_id=1, source_target_pairs={{0,8},{8,0},{16,24},{24,16},{32,40},{40,32},{48,56},{56,48},{64,72... | collective-permute-start | bytes 1572872 | tf_op jit(solution)/shard_map/ppermute | solution.py:33
  (74 other events, 1131.3 us)

commit v5 on v4

--- a/solution.py
+++ b/solution.py
@@ -10,6 +10,8 @@
 norm_eps = 1e-05
 GROUP = 32
 BF16, F32 = jnp.bfloat16, jnp.float32
+VMEM_LIMIT = 60 * 2**20
+ENLIST = 4
 RING = 4
 PLACES = ((2, 1), (1, 1), (-1, 1), (2, 0), (0, 1), (1, 0), (-1, 0), (0, 0))
 ANY = pl.BlockSpec(memory_space=pl.ANY)
@@ -61,12 +63,10 @@
     )(*arrays)
 
 
-def gather_tree(own, up, down, pair, beside_it=lambda: ()):
+def gather_tree(own, up, down, pair):
     half = own.shape[0] // 2
-    below, above, beside = together(up(own), down(own), pair(own))
-    below_beside, above_beside, far, *others = together(
-        pair(below), down(beside), up(below), *beside_it()
-    )
+    below, above, beside = up(own), down(own), pair(own)
+    below_beside, above_beside, far = pair(below), down(beside), up(below)
     far_beside = [(0, down(above_beside[:half])), (half, up(below_beside[half:]))]
     whole = {
         (0, 0): own,
@@ -77,7 +77,7 @@
         (1, 1): above_beside,
         (2, 0): far,
     }
-    return [far_beside if place == (2, 1) else [(0, whole[place])] for place in PLACES], others
+    return [far_beside if place == (2, 1) else [(0, whole[place])] for place in PLACES]
 
 
 def scatter_first(corner, blocks, up, down):
@@ -90,20 +90,21 @@
     return above_beside.astype(BF16), below_beside.astype(BF16), blocks[2, 0].astype(BF16)
 
 
-def scatter_second(leaving, blocks, up, down, pair, beside_it=()):
+def scatter_second(leaving, blocks, up, down, pair):
     above_beside, below_beside, far = leaving
-    below_beside, far, above_beside, *others = together(
-        pair(below_beside), down(far), up(above_beside), *beside_it
-    )
-    below = blocks[-1, 0].astype(F32) + below_beside.astype(F32) + far.astype(F32)
-    beside = blocks[0, 1].astype(F32) + above_beside.astype(F32)
-    return (below.astype(BF16), beside.astype(BF16), blocks[1, 0].astype(BF16)), others
+    below = blocks[-1, 0].astype(F32) + pair(below_beside).astype(F32) + down(far).astype(F32)
+    beside = blocks[0, 1].astype(F32) + up(above_beside).astype(F32)
+    return below.astype(BF16), beside.astype(BF16), blocks[1, 0].astype(BF16)
 
 
 def scatter_third(leaving, own, up, down, pair):
     below, beside, above = leaving
-    above, below, beside = together(up(above), down(below), pair(beside))
-    return own.astype(F32) + above.astype(F32) + below.astype(F32) + beside.astype(F32)
+    return (
+        own.astype(F32)
+        + up(above).astype(F32)
+        + down(below).astype(F32)
+        + pair(beside).astype(F32)
+    )
 
 
 def run_list(first, last, tile_list, panel_list, key_list, multiply, acc_ref):
@@ -166,13 +167,15 @@
     for i in range(sources):
         source = order_ref[i]
 
-        def enlist(k, count, i=i, source=source):
-            tile_list[count] = i * slots + k
-            panel_list[count] = i * col_tiles + cols_ref[source, k]
-            key_list[count] = rows_ref[source, k]
-            return count + 1
-
-        count = lax.fori_loop(0, counts_ref[source], enlist, count)
+        def enlist(g, count, i=i, source=source):
+            for j in range(ENLIST):
+                k = g * ENLIST + j
+                tile_list[count + j] = i * slots + k
+                panel_list[count + j] = i * col_tiles + cols_ref[source, k]
+                key_list[count + j] = rows_ref[source, k]
+            return count + jnp.minimum(ENLIST, counts_ref[source] - g * ENLIST)
+
+        count = lax.fori_loop(0, (counts_ref[source] + ENLIST - 1) // ENLIST, enlist, count)
         ends.append(count)
     fill_tail(count, spare, tile_list, panel_list, key_list)
 
@@ -253,7 +256,7 @@
             pltpu.SemaphoreType.DMA((sources,)),
             pltpu.SemaphoreType.DMA((len(arrays),)),
         ],
-        compiler_params=pltpu.CompilerParams(vmem_limit_bytes=44 * 2**20),
+        compiler_params=pltpu.CompilerParams(vmem_limit_bytes=VMEM_LIMIT),
         cost_estimate=pl.CostEstimate(flops=6 * 10**9, bytes_accessed=30 * 2**20, transcendentals=0),
         name="forward_tiles",
     )(order, dests, *scalars, tiles, *arrays)
@@ -293,13 +296,15 @@
     for i in range(sources):
         source = order_ref[i]
 
-        def enlist(k, count, i=i, source=source):
-            tile_list[count] = i * slots + k
-            panel_list[count] = rows_ref[source, k]
-            key_list[count] = i * col_tiles + cols_ref[source, k]
-            return count + 1
-
-        count = lax.fori_loop(0, counts_ref[source], enlist, count)
+        def enlist(g, count, i=i, source=source):
+            for j in range(ENLIST):
+                k = g * ENLIST + j
+                tile_list[count + j] = i * slots + k
+                panel_list[count + j] = rows_ref[source, k]
+                key_list[count + j] = i * col_tiles + cols_ref[source, k]
+            return count + jnp.minimum(ENLIST, counts_ref[source] - g * ENLIST)
+
+        count = lax.fori_loop(0, (counts_ref[source] + ENLIST - 1) // ENLIST, enlist, count)
         ends.append(count)
     fill_tail(count, sources * col_tiles, tile_list, panel_list, key_list)
 
@@ -348,10 +353,24 @@
             pltpu.SemaphoreType.DMA((sources,)),
             pltpu.SemaphoreType.DMA((len(arrays),)),
         ],
-        compiler_params=pltpu.CompilerParams(vmem_limit_bytes=52 * 2**20),
+        compiler_params=pltpu.CompilerParams(vmem_limit_bytes=VMEM_LIMIT),
         cost_estimate=pl.CostEstimate(flops=8 * 10**9, bytes_accessed=20 * 2**20, transcendentals=0),
         name="backward_tiles",
     )(order, dests, *scalars, tiles, *arrays, *after)
+
+
+def sum_first_kernel(value_ref, *refs):
+    refs[-1][...] = jnp.sum(value_ref[...], axis=0)
+
+
+def sum_first(value, after):
+    return pl.pallas_call(
+        sum_first_kernel,
+        in_specs=[VMEM] + [ANY] * len(after),
+        out_specs=VMEM,
+        out_shape=jax.ShapeDtypeStruct(value.shape[1:], value.dtype),
+        name="sum_first",
+    )(value, *after)
 
 
 def weight_kernel(aggregate_ref, grad_ref, offset_ref, *refs):
@@ -408,7 +427,7 @@
     *blk_tree, across = blk_links()
     rep_tree = rep_links()
 
-    mine, _ = gather_tree(features.reshape(col_tiles, tile, width), *blk_tree)
+    mine = gather_tree(features.reshape(col_tiles, tile, width), *blk_tree)
     theirs = [[(first, across(array)) for first, array in parts] for parts in mine]
     backwards = slice(None, None, -1)
     scalars = (rows, cols, counts)
@@ -418,7 +437,7 @@
     low, high, *rest, offset = forward_tiles(order, dests, scalars, tiles, shards)
     blocks = dict(zip(PLACES[1:], rest))
     leaving = scatter_first((low, high), blocks, up, down)
-    leaving, _ = scatter_second(leaving, blocks, *rep_tree)
+    leaving = scatter_second(leaving, blocks, *rep_tree)
     shifted = scatter_third(leaving, blocks[0, 0], *rep_tree).reshape(local_rows, width)
     aggregate = shifted.astype(BF16)
     projected = jnp.dot(aggregate, weight, preferred_element_type=F32)
@@ -458,14 +477,11 @@
     sent = lax.dot_general(
         grad_summed, weight, (((1,), (1,)), ((), ())), preferred_element_type=F32
     ).astype(BF16)
-    def weight_pieces():
-        term = weight_terms(aggregate, grad_summed, group_offset, [])
-        return [lax.all_to_all(term.reshape(blk_count, -1, width), "blk", 0, 0)]
-
-    grads, [pieces] = gather_tree(
-        sent.reshape(col_tiles, tile, width), *rep_tree, weight_pieces
-    )
-    piece = jnp.sum(pieces, axis=0)
+    grads = gather_tree(sent.reshape(col_tiles, tile, width), *rep_tree)
+    arrived = {place: parts[0][1] for place, parts in zip(PLACES, grads)}
+    weight_term = weight_terms(aggregate, grad_summed, group_offset, [arrived[1, 0]])
+    pieces = lax.all_to_all(weight_term.reshape(blk_count, -1, width), "blk", 0, 0)
+    piece = sum_first(pieces, [arrived[-1, 1]])
     terms = copies_of_all(piece, "rep")
 
     half = col_tiles // 2
@@ -477,15 +493,17 @@
         scalars,
         tiles,
         grads,
+        [terms],
     )
     given, kept = arrays[: len(sizes)], arrays[len(sizes) :]
     low, high, *rest = [b.astype(F32) + across(a).astype(F32) for a, b in zip(given, kept)]
     products = dict(zip(PLACES[1:], rest))
     up, down, pair = blk_tree
     leaving = scatter_first((low, high), products, up, down)
-    leaving, [terms] = scatter_second(leaving, products, *blk_tree, [terms])
+    leaving = scatter_second(leaving, products, *blk_tree)
+    grad_w = copies_of_all(sum_first(terms, [leaving[0][:1, :16, :128]]), "blk")
     grad_x = scatter_third(leaving, products[0, 0], *blk_tree).astype(BF16)
-    grad_w = copies_of_all(jnp.sum(terms, axis=0), "blk").reshape(weight.shape)
+    grad_w = grad_w.reshape(weight.shape)
     return (output, grad_x.reshape(local_rows, width), grad_w, grad_gamma, grad_beta)
 
 

time: 311 us -> 289 us (0.929)
  local copies, waits for them, and re-layouts: 32.7 us -> 13.4 us
  blocking collectives: 43.1 us -> 29.1 us
  Pallas kernels: 36.9 us -> 42.7 us
  other arithmetic: 28.4 us -> 23 us
  waiting for transfers between devices: 85.6 us -> 90.5 us
  starting transfers between devices: 81.6 us -> 86.3 us
    unnamed x109 -> x61, local copies, waits for them, and re-layouts: 25.8 us -> 5.34 us
    all_to_all x1 -> x0, blocking collectives: 14 us -> none  [weight_pieces(): return [lax.all_to_all(term.reshape(blk_count, -1, width), 'blk', 0, 0)]]
    ppermute x16, starting transfers between devices: 29.3 us -> 21.2 us  [link(): return lambda value: lax.ppermute(value, 'rep', pairs)]
    all_to_all x0 -> x1, starting transfers between devices: none -> 5.47 us  [on_device(): lax.all_to_all(weight_term.reshape(blk_count, -1, width), 'blk', 0, 0)]
    all_to_all x2, starting transfers between devices: 13.4 us -> 17.3 us  [copies_of_all(): lax.all_to_all(jnp.broadcast_to(value[None], (count, *value.shape)), axis...]
    ppermute x34, starting transfers between devices: 39 us -> 42.3 us  [link(): return lambda value: lax.ppermute(value, 'blk', pairs)]
    ppermute x34, waiting for transfers between devices: 29.9 us -> 33 us  [link(): return lambda value: lax.ppermute(value, 'blk', pairs)]
  transfers between devices with their start and end apart: 52 -> 53, of which waited for: 20 -> 20; matrix products, arithmetic and copies ran while one was open for 7% -> 8% of each run, Pallas kernels for 1% -> 2%
where the time goes in v5:
time: 289 us; the launch traced here: 288 us
  waiting for transfers between devices  90.5 us (31%)
  starting transfers between devices  86.3 us (30%)
  Pallas kernels  42.7 us (15%)
  blocking collectives  29.1 us (10%)
  other arithmetic  23 us (8%)
  local copies, waits for them, and re-layouts  13.4 us (5%)
    ppermute x34, starting transfers between devices, link(): return lambda value: lax.ppermute(value, 'blk', pairs)  42.3 us
    ppermute x16, waiting for transfers between devices, link(): return lambda value: lax.ppermute(value, 'rep', pairs)  35.4 us
    ppermute x34, waiting for transfers between devices, link(): return lambda value: lax.ppermute(value, 'blk', pairs)  33 us
    all_to_all x2, blocking collectives, copies_of_all(): lax.all_to_all(jnp.broadcast_to(value[None], (count, *value.shape)), axis...  29.1 us
    ppermute x16, starting transfers between devices, link(): return lambda value: lax.ppermute(value, 'rep', pairs)  21.2 us
    all_to_all x2, waiting for transfers between devices, copies_of_all(): lax.all_to_all(jnp.broadcast_to(value[None], (count, *value.shape)), axis...  20.2 us
    pallas_call x1, Pallas kernels, backward_tiles(): pl.pallas_call(functools.partial(backward_kernel, layout, sizes, len(afte...  19.9 us
    pallas_call x1, Pallas kernels, forward_tiles(): pl.pallas_call(functools.partial(forward_kernel, layout), in_specs=[SMEM]...  17.4 us
  transfers between devices with their start and end apart: 53, of which 20 were waited for; matrix products, arithmetic and copies ran while one was open for 8% of the time, Pallas kernels for 2%

profile of v5, /device:TPU:1, one launch (start us, length us, event | category | flops | bytes accessed | tf_op | source)
XLA Modules:
  0.0 287.8 jit_solution(2725916621092341253)
XLA Ops:
  6.6 7.7 %collective-permute-done.5.refs_6_ = bf16[8,128,256]{2,1,0:T(8,128)(2,1)S(1)} collective-permute-done((bf16[8,128,256]{2,1,0:T(8,128)(2,1)}, bf16[8,128,256]{2,1,0:T(8,128)(2,1)S(1)}, u32[]{:S(2)}, u32[]{:S(2)}) %collective-permute-start.5) | collective-permute-done | bytes 524320 | tf_op jit(solution)/shard_map/ppermute | solution.py:35
  14.3 4.0 %collective-permute-start.11 = (bf16[8,128,256]{2,1,0:T(8,128)(2,1)S(1)}, bf16[8,128,256]{2,1,0:T(8,128)(2,1)S(1)}, u32[]{:S(2)}, u32[]{:S(2)}) collective-permute-start(bf16[8,128,256]{2,1,0:T(8,128)(2,1)S(1)} %collective-permute-done.5.refs_6_), channel_id=1, source_target_pairs={{0,96},{8,104},{16,112},{24,120},{32,0},{40,8},{48,16},{56,24},{64... | collective-permute-start | bytes 1572872 | tf_op jit(solution)/shard_map/ppermute | solution.py:35
  22.2 6.5 %collective-permute-done.11.refs_12_ = bf16[8,128,256]{2,1,0:T(8,128)(2,1)S(1)} collective-permute-done((bf16[8,128,256]{2,1,0:T(8,128)(2,1)S(1)}, bf16[8,128,256]{2,1,0:T(8,128)(2,1)S(1)}, u32[]{:S(2)}, u32[]{:S(2)}) %collective-permute-start.11) | collective-permute-done | bytes 524320 | tf_op jit(solution)/shard_map/ppermute | solution.py:35
  36.3 4.9 %collective-permute-done.7.refs_8_ = bf16[8,128,256]{2,1,0:T(8,128)(2,1)S(1)} collective-permute-done((bf16[8,128,256]{2,1,0:T(8,128)(2,1)S(1)}, bf16[8,128,256]{2,1,0:T(8,128)(2,1)S(1)}, u32[]{:S(2)}, u32[]{:S(2)}) %collective-permute-start.7) | collective-permute-done | bytes 524320 | tf_op jit(solution)/shard_map/ppermute | solution.py:35
  41.2 5.8 %collective-permute-start.10 = (bf16[8,128,256]{2,1,0:T(8,128)(2,1)S(1)}, bf16[8,128,256]{2,1,0:T(8,128)(2,1)}, u32[]{:S(2)}, u32[]{:S(2)}) collective-permute-start(bf16[8,128,256]{2,1,0:T(8,128)(2,1)S(1)} %collective-permute-done.9.refs_10_), channel_id=1, source_target_pairs={{0,8},{8,0},{16,24},{24,16},{32,40},{40,32},{48,56},{56,48},{64,72... | collective-permute-start | bytes 1572872 | tf_op jit(solution)/shard_map/ppermute | solution.py:35
  51.6 17.4 %forward_tiles.1 = (bf16[4,128,256]{2,1,0:T(8,128)(2,1)}, bf16[4,128,256]{2,1,0:T(8,128)(2,1)}, bf16[8,128,256]{2,1,0:T(8,128)(2,1)}, bf16[8,128,256]{2,1,0:T(8,...) custom-call(s32[16]{0:T(128)} %reshape.73.order_ref, ...), custom_call_target="tpu_custom_call" | custom-call | flops 6000000000 | bytes 31457280 | tf_op jit(solution)/shard_map/forward_tiles/pallas_call | solution.py:246
  72.4 6.7 %collective-permute-done.18.refs_0_ = bf16[4,128,256]{2,1,0:T(8,128)(2,1)S(1)} collective-permute-done((bf16[4,128,256]{2,1,0:T(8,128)(2,1)}, bf16[4,128,256]{2,1,0:T(8,128)(2,1)S(1)}, u32[]{:S(2)}, u32[]{:S(2)}) %collective-permute-start.18) | collective-permute-done | bytes 262176 | tf_op jit(solution)/shard_map/ppermute | solution.py:45
  81.7 2.7 collective-permute-start.21
  85.6 2.6 collective-permute-start.20
  88.4 7.3 %collective-permute-done.23 = bf16[8,128,256]{2,1,0:T(8,128)(2,1)S(1)} collective-permute-done((bf16[8,128,256]{2,1,0:T(8,128)(2,1)S(1)}, bf16[8,128,256]{2,1,0:T(8,128)(2,1)S(1)}, u32[]{:S(2)}, u32[]{:S(2)}) %collective-permute-start.23) | collective-permute-done | bytes 524320 | tf_op jit(solution)/shard_map/ppermute | solution.py:45
  96.8 2.3 collective-permute-start.24
  102.2 4.7 %collective-permute-done.17 = bf16[8,128,256]{2,1,0:T(8,128)(2,1)S(1)} collective-permute-done((bf16[8,128,256]{2,1,0:T(8,128)(2,1)}, bf16[8,128,256]{2,1,0:T(8,128)(2,1)S(1)}, u32[]{:S(2)}, u32[]{:S(2)}) %collective-permute-start.17) | collective-permute-done | bytes 524320 | tf_op jit(solution)/shard_map/ppermute | solution.py:45
  114.0 12.4 %all-to-all-start = ((f32[128,4,256]{2,1,0:T(4,128)}), f32[128,4,256]{2,1,0:T(4,128)S(1)}, u32[]{:S(2)}, u32[]{:S(2)}) async-start(f32[128,4,256]{2,1,0:T(4,128)} %broadcast_in_dim.10), calls=%async_computation | async-start | bytes 1048576 | tf_op jit(solution)/shard_map/all_to_all | solution.py:400
  126.5 13.9 %all-to-all-done = f32[128,4,256]{2,1,0:T(4,128)S(1)} async-done(((f32[128,4,256]{2,1,0:T(4,128)}), f32[128,4,256]{2,1,0:T(4,128)S(1)}, u32[]{:S(2)}, u32[]{:S(2)}) %all-to-all-start) | async-done | bytes 524320 | tf_op jit(solution)/shard_map/all_to_all | solution.py:400
  141.6 15.4 %all_to_all.25 = f32[128,2,256]{2,1,0:T(2,128)S(1)} all-to-all(f32[128,2,256]{2,1,0:T(2,128)S(1)} %broadcast_in_dim.11), channel_id=1, replica_groups=mesh['blk'=16,'rep'=8] {'blk','rep'}, dimensions={0} | all-to-all | bytes 524288 | tf_op jit(solution)/shard_map/all_to_all | solution.py:400
  160.9 2.3 collective-permute-start.32
  163.3 10.5 %collective-permute-done.28.refs_7_ = bf16[8,128,256]{2,1,0:T(8,128)(2,1)} collective-permute-done((bf16[8,128,256]{2,1,0:T(8,128)(2,1)S(1)}, bf16[8,128,256]{2,1,0:T(8,128)(2,1)}, u32[]{:S(2)}, u32[]{:S(2)}) %collective-permute-start.28) | collective-permute-done | bytes 524320 | tf_op jit(solution)/shard_map/ppermute | solution.py:45
  177.3 2.3 weight_terms.1
  179.6 5.5 %all-to-all-start.2 = ((f32[16,16,256]{2,1,0:T(8,128)}), f32[16,16,256]{2,1,0:T(8,128)S(1)}, u32[]{:S(2)}, u32[]{:S(2)}) async-start(f32[16,16,256]{2,1,0:T(8,128)} %bitcast.65), calls=%async_computation.2 | async-start | bytes 524288 | tf_op jit(solution)/shard_map/all_to_all | solution.py:483
  185.1 2.3 collective-permute-done.29.refs_0_.refs_3_
  187.6 2.7 collective-permute-start.27
  196.0 4.9 %all-to-all-start.3 = ((f32[8,16,256]{2,1,0:T(8,128)}), f32[8,16,256]{2,1,0:T(8,128)S(1)}, u32[]{:S(2)}, u32[]{:S(2)}) async-start(f32[8,16,256]{2,1,0:T(8,128)} %broadcast_in_dim.13), calls=%async_computation.3 | async-start | bytes 262144 | tf_op jit(solution)/shard_map/all_to_all | solution.py:400
  201.5 6.3 %all-to-all-done.3.refs_9_.value_ref = f32[8,16,256]{2,1,0:T(8,128)S(1)} async-done(((f32[8,16,256]{2,1,0:T(8,128)}), f32[8,16,256]{2,1,0:T(8,128)S(1)}, u32[]{:S(2)}, u32[]{:S(2)}) %all-to-all-start.3) | async-done | bytes 131104 | tf_op jit(solution)/shard_map/all_to_all | solution.py:400
  209.2 19.9 %backward_tiles.1 = (bf16[4,128,256]{2,1,0:T(8,128)(2,1)}, bf16[4,128,256]{2,1,0:T(8,128)(2,1)}, bf16[8,128,256]{2,1,0:T(8,128)(2,1)}, bf16[8,128,256]{2,1,0:T(8...) custom-call(s32[16]{0:T(128)} %concatenate.4.order_ref, ...), custom_call_target="tpu_custom_call" | custom-call | flops 8000000000 | bytes 20971520 | tf_op jit(solution)/shard_map/backward_tiles/pallas_call | solution.py:343
  229.1 2.5 collective-permute-start.38
  235.8 2.4 collective-permute-start.41
  239.4 4.0 %collective-permute-done.39.refs_0_ = bf16[4,128,256]{2,1,0:T(8,128)(2,1)S(1)} collective-permute-done((bf16[4,128,256]{2,1,0:T(8,128)(2,1)S(1)}, bf16[4,128,256]{2,1,0:T(8,128)(2,1)S(1)}, u32[]{:S(2)}, u32[]{:S(2)}) %collective-permute-start.39) | collective-permute-done | bytes 262176 | tf_op jit(solution)/shard_map/ppermute | solution.py:35
  245.1 3.1 %collective-permute-start.44 = (bf16[8,128,256]{2,1,0:T(8,128)(2,1)S(1)}, bf16[8,128,256]{2,1,0:T(8,128)(2,1)S(1)}, u32[]{:S(2)}, u32[]{:S(2)}) collective-permute-start(bf16[8,128,256]{2,1,0:T(8,128)(2,1)S(1)} %add_convert_fusion.4), channel_id=1, source_target_pairs={{0,96},{8,104},{16,112},{24,120},{32,0},{40,8},{48,16},{56,24},{64... | collective-permute-start | bytes 1572872 | tf_op jit(solution)/shard_map/ppermute | solution.py:35
  254.0 5.0 %collective-permute-done.44 = bf16[8,128,256]{2,1,0:T(8,128)(2,1)S(1)} collective-permute-done((bf16[8,128,256]{2,1,0:T(8,128)(2,1)S(1)}, bf16[8,128,256]{2,1,0:T(8,128)(2,1)S(1)}, u32[]{:S(2)}, u32[]{:S(2)}) %collective-permute-start.44) | collective-permute-done | bytes 524320 | tf_op jit(solution)/shard_map/ppermute | solution.py:35
  258.9 3.2 %collective-permute-done.42 = bf16[8,128,256]{2,1,0:T(8,128)(2,1)S(1)} collective-permute-done((bf16[8,128,256]{2,1,0:T(8,128)(2,1)S(1)}, bf16[8,128,256]{2,1,0:T(8,128)(2,1)S(1)}, u32[]{:S(2)}, u32[]{:S(2)}) %collective-permute-start.42) | collective-permute-done | bytes 524320 | tf_op jit(solution)/shard_map/ppermute | solution.py:35
  270.9 13.7 %all_to_all.26 = f32[16,16,256]{2,1,0:T(8,128)S(1)} all-to-all(f32[16,16,256]{2,1,0:T(8,128)S(1)} %broadcast_in_dim.14), channel_id=1, replica_groups=mesh['blk'=16,'rep'=8] {'blk'}, dimensions={0} | all-to-all | bytes 524288 | tf_op jit(solution)/shard_map/all_to_all | solution.py:400
  284.7 2.4 add_convert_fusion
  (196 shorter events, 79.2 us)
Async XLA Ops:
  0.6 13.7 %collective-permute-start.5 = (bf16[8,128,256]{2,1,0:T(8,128)(2,1)}, bf16[8,128,256]{2,1,0:T(8,128)(2,1)S(1)}, u32[]{:S(2)}, u32[]{:S(2)}) collective-permute-start(bf16[8,128,256]{2,1,0:T(8,128)(2,1)} %bitcast.66), channel_id=1, source_target_pairs={{0,16},{8,24},{16,0},{24,8},{32,48},{40,56},{48,32},{56,40},{64,80... | collective-permute-start | bytes 1572872 | tf_op jit(solution)/shard_map/ppermute | solution.py:35
  2.9 15.5 %collective-permute-start.1 = (bf16[8,128,256]{2,1,0:T(8,128)(2,1)}, bf16[8,128,256]{2,1,0:T(8,128)(2,1)S(1)}, u32[]{:S(2)}, u32[]{:S(2)}) collective-permute-start(bf16[8,128,256]{2,1,0:T(8,128)(2,1)} %bitcast.67), channel_id=1, source_target_pairs={{0,32},{8,40},{16,48},{24,56},{32,64},{40,72},{48,80},{56,88},{64,... | collective-permute-start | bytes 1572872 | tf_op jit(solution)/shard_map/ppermute | solution.py:35
  4.5 17.2 %collective-permute-start.3 = (bf16[8,128,256]{2,1,0:T(8,128)(2,1)}, bf16[8,128,256]{2,1,0:T(8,128)(2,1)S(1)}, u32[]{:S(2)}, u32[]{:S(2)}) collective-permute-start(bf16[8,128,256]{2,1,0:T(8,128)(2,1)} %bitcast.68), channel_id=1, source_target_pairs={{0,96},{8,104},{16,112},{24,120},{32,0},{40,8},{48,16},{56,24},{64... | collective-permute-start | bytes 1572872 | tf_op jit(solution)/shard_map/ppermute | solution.py:35
  14.3 14.4 %collective-permute-start.11 = (bf16[8,128,256]{2,1,0:T(8,128)(2,1)S(1)}, bf16[8,128,256]{2,1,0:T(8,128)(2,1)S(1)}, u32[]{:S(2)}, u32[]{:S(2)}) collective-permute-start(bf16[8,128,256]{2,1,0:T(8,128)(2,1)S(1)} %collective-permute-done.5.refs_6_), channel_id=1, source_target_pairs={{0,96},{8,104},{16,112},{24,120},{32,0},{40,8},{48,16},{56,24},{64... | collective-permute-start | bytes 1572872 | tf_op jit(solution)/shard_map/ppermute | solution.py:35
  19.6 14.5 %collective-permute-start = (bf16[8,128,256]{2,1,0:T(8,128)(2,1)}, bf16[8,128,256]{2,1,0:T(8,128)(2,1)S(1)}, u32[]{:S(2)}, u32[]{:S(2)}) collective-permute-start(bf16[8,128,256]{2,1,0:T(8,128)(2,1)} %bitcast.69), channel_id=1, source_target_pairs={{0,8},{8,0},{16,24},{24,16},{32,40},{40,32},{48,56},{56,48},{64,72... | collective-permute-start | bytes 1572872 | tf_op jit(solution)/shard_map/ppermute | solution.py:35
  21.7 13.7 %collective-permute-start.6 = (bf16[8,128,256]{2,1,0:T(8,128)(2,1)S(1)}, bf16[8,128,256]{2,1,0:T(8,128)(2,1)S(1)}, u32[]{:S(2)}, u32[]{:S(2)}) collective-permute-start(bf16[8,128,256]{2,1,0:T(8,128)(2,1)S(1)} %collective-permute-done.5.refs_6_), channel_id=1, source_target_pairs={{0,8},{8,0},{16,24},{24,16},{32,40},{40,32},{48,56},{56,48},{64,72... | collective-permute-start | bytes 1572872 | tf_op jit(solution)/shard_map/ppermute | solution.py:35
  21.7 13.9 %collective-permute-start.4 = (bf16[8,128,256]{2,1,0:T(8,128)(2,1)S(1)}, bf16[8,128,256]{2,1,0:T(8,128)(2,1)S(1)}, u32[]{:S(2)}, u32[]{:S(2)}) collective-permute-start(bf16[8,128,256]{2,1,0:T(8,128)(2,1)S(1)} %collective-permute-done.3.refs_4_), channel_id=1, source_target_pairs={{0,8},{8,0},{16,24},{24,16},{32,40},{40,32},{48,56},{56,48},{64,72... | collective-permute-start | bytes 1572872 | tf_op jit(solution)/shard_map/ppermute | solution.py:35
  30.4 16.6 %collective-permute-start.2 = (bf16[8,128,256]{2,1,0:T(8,128)(2,1)S(1)}, bf16[8,128,256]{2,1,0:T(8,128)(2,1)S(1)}, u32[]{:S(2)}, u32[]{:S(2)}) collective-permute-start(bf16[8,128,256]{2,1,0:T(8,128)(2,1)S(1)} %collective-permute-done.1.refs_2_), channel_id=1, source_target_pairs={{0,8},{8,0},{16,24},{24,16},{32,40},{40,32},{48,56},{56,48},{64,72... | collective-permute-start | bytes 1572872 | tf_op jit(solution)/shard_map/ppermute | solution.py:35
  34.1 13.8 %collective-permute-start.13 = (bf16[4,128,256]{2,1,0:T(8,128)(2,1)}, bf16[4,128,256]{2,1,0:T(8,128)(2,1)S(1)}, u32[]{:S(2)}, u32[]{:S(2)}) collective-permute-start(bf16[4,128,256]{2,1,0:T(8,128)(2,1)} %slice.40), channel_id=1, source_target_pairs={{0,96},{8,104},{16,112},{24,120},{32,0},{40,8},{48,16},{56,24},{64... | collective-permute-start | bytes 786440 | tf_op jit(solution)/shard_map/ppermute | solution.py:35
  35.6 15.7 %collective-permute-start.12 = (bf16[8,128,256]{2,1,0:T(8,128)(2,1)S(1)}, bf16[8,128,256]{2,1,0:T(8,128)(2,1)}, u32[]{:S(2)}, u32[]{:S(2)}) collective-permute-start(bf16[8,128,256]{2,1,0:T(8,128)(2,1)S(1)} %collective-permute-done.11.refs_12_), channel_id=1, source_target_pairs={{0,8},{8,0},{16,24},{24,16},{32,40},{40,32},{48,56},{56,48},{64,72... | collective-permute-start | bytes 1572872 | tf_op jit(solution)/shard_map/ppermute | solution.py:35
  81.6 14.0 %collective-permute-start.23 = (bf16[8,128,256]{2,1,0:T(8,128)(2,1)S(1)}, bf16[8,128,256]{2,1,0:T(8,128)(2,1)S(1)}, u32[]{:S(2)}, u32[]{:S(2)}) collective-permute-start(bf16[8,128,256]{2,1,0:T(8,128)(2,1)S(1)} %add_convert_fusion.9), channel_id=1, source_target_pairs={{0,1},{4,5},{1,2},{5,6},{2,3},{6,7},{3,0},{7,4},{8,9},{12,13},{9,1... | collective-permute-start | bytes 1572872 | tf_op jit(solution)/shard_map/ppermute | solution.py:45
  81.7 17.4 %collective-permute-start.21 = (bf16[8,128,256]{2,1,0:T(8,128)(2,1)}, bf16[8,128,256]{2,1,0:T(8,128)(2,1)S(1)}, u32[]{:S(2)}, u32[]{:S(2)}) collective-permute-start(bf16[8,128,256]{2,1,0:T(8,128)(2,1)} %get-tuple-element.44), channel_id=1, source_target_pairs={{0,3},{4,7},{1,0},{5,4},{2,1},{6,5},{3,2},{7,6},{8,11},{12,15},{9,... | collective-permute-start | bytes 1572872 | tf_op jit(solution)/shard_map/ppermute | solution.py:45
  85.6 13.7 %collective-permute-start.20 = (bf16[8,128,256]{2,1,0:T(8,128)(2,1)S(1)}, bf16[8,128,256]{2,1,0:T(8,128)(2,1)S(1)}, u32[]{:S(2)}, u32[]{:S(2)}) collective-permute-start(bf16[8,128,256]{2,1,0:T(8,128)(2,1)S(1)} %add_convert_fusion.11), channel_id=1, source_target_pairs={{0,4},{4,0},{1,5},{5,1},{2,6},{6,2},{3,7},{7,3},{8,12},{12,8},{9,1... | collective-permute-start | bytes 1572872 | tf_op jit(solution)/shard_map/ppermute | solution.py:45
  88.2 18.7 %collective-permute-start.17 = (bf16[8,128,256]{2,1,0:T(8,128)(2,1)}, bf16[8,128,256]{2,1,0:T(8,128)(2,1)S(1)}, u32[]{:S(2)}, u32[]{:S(2)}) collective-permute-start(bf16[8,128,256]{2,1,0:T(8,128)(2,1)} %get-tuple-element.38), channel_id=1, source_target_pairs={{0,1},{4,5},{1,2},{5,6},{2,3},{6,7},{3,0},{7,4},{8,9},{12,13},{9,1... | collective-permute-start | bytes 1572872 | tf_op jit(solution)/shard_map/ppermute | solution.py:45
  114.0 26.3 %all-to-all-start = ((f32[128,4,256]{2,1,0:T(4,128)}), f32[128,4,256]{2,1,0:T(4,128)S(1)}, u32[]{:S(2)}, u32[]{:S(2)}) async-start(f32[128,4,256]{2,1,0:T(4,128)} %broadcast_in_dim.10), calls=%async_computation | async-start | bytes 1048576 | tf_op jit(solution)/shard_map/all_to_all | solution.py:400
  159.5 14.2 %collective-permute-start.28 = (bf16[8,128,256]{2,1,0:T(8,128)(2,1)S(1)}, bf16[8,128,256]{2,1,0:T(8,128)(2,1)}, u32[]{:S(2)}, u32[]{:S(2)}) collective-permute-start(bf16[8,128,256]{2,1,0:T(8,128)(2,1)S(1)} %bitcast.71), channel_id=1, source_target_pairs={{0,1},{4,5},{1,2},{5,6},{2,3},{6,7},{3,0},{7,4},{8,9},{12,13},{9,1... | collective-permute-start | bytes 1572872 | tf_op jit(solution)/shard_map/ppermute | solution.py:45
  159.9 15.0 %collective-permute-start.25 = (bf16[8,128,256]{2,1,0:T(8,128)(2,1)S(1)}, bf16[8,128,256]{2,1,0:T(8,128)(2,1)}, u32[]{:S(2)}, u32[]{:S(2)}) collective-permute-start(bf16[8,128,256]{2,1,0:T(8,128)(2,1)S(1)} %bitcast.72), channel_id=1, source_target_pairs={{0,4},{4,0},{1,5},{5,1},{2,6},{6,2},{3,7},{7,3},{8,12},{12,8},{9,1... | collective-permute-start | bytes 1572872 | tf_op jit(solution)/shard_map/ppermute | solution.py:45
  160.9 15.5 %collective-permute-start.32 = (bf16[8,128,256]{2,1,0:T(8,128)(2,1)S(1)}, bf16[8,128,256]{2,1,0:T(8,128)(2,1)S(1)}, u32[]{:S(2)}, u32[]{:S(2)}) collective-permute-start(bf16[8,128,256]{2,1,0:T(8,128)(2,1)S(1)} %bitcast.73), channel_id=1, source_target_pairs={{0,3},{4,7},{1,0},{5,4},{2,1},{6,5},{3,2},{7,6},{8,11},{12,15},{9,... | collective-permute-start | bytes 1572872 | tf_op jit(solution)/shard_map/ppermute | solution.py:45
  173.8 13.7 %collective-permute-start.29 = (bf16[8,128,256]{2,1,0:T(8,128)(2,1)}, bf16[8,128,256]{2,1,0:T(8,128)(2,1)S(1)}, u32[]{:S(2)}, u32[]{:S(2)}) collective-permute-start(bf16[8,128,256]{2,1,0:T(8,128)(2,1)} %collective-permute-done.28.refs_7_), channel_id=1, source_target_pairs={{0,4},{4,0},{1,5},{5,1},{2,6},{6,2},{3,7},{7,3},{8,12},{12,8},{9,1... | collective-permute-start | bytes 1572872 | tf_op jit(solution)/shard_map/ppermute | solution.py:45
  176.4 25.1 %collective-permute-start.31 = (bf16[8,128,256]{2,1,0:T(8,128)(2,1)}, bf16[8,128,256]{2,1,0:T(8,128)(2,1)}, u32[]{:S(2)}, u32[]{:S(2)}) collective-permute-start(bf16[8,128,256]{2,1,0:T(8,128)(2,1)} %collective-permute-done.28.refs_7_), channel_id=1, source_target_pairs={{0,1},{4,5},{1,2},{5,6},{2,3},{6,7},{3,0},{7,4},{8,9},{12,13},{9,1... | collective-permute-start | bytes 1572872 | tf_op jit(solution)/shard_map/ppermute | solution.py:45
  187.4 20.4 %collective-permute-start.30 = (bf16[4,128,256]{2,1,0:T(8,128)(2,1)S(1)}, bf16[4,128,256]{2,1,0:T(8,128)(2,1)S(1)}, u32[]{:S(2)}, u32[]{:S(2)}) collective-permute-start(bf16[4,128,256]{2,1,0:T(8,128)(2,1)S(1)} %slice.47), channel_id=1, source_target_pairs={{0,1},{4,5},{1,2},{5,6},{2,3},{6,7},{3,0},{7,4},{8,9},{12,13},{9,1... | collective-permute-start | bytes 786440 | tf_op jit(solution)/shard_map/ppermute | solution.py:45
  187.6 20.2 %collective-permute-start.27 = (bf16[4,128,256]{2,1,0:T(8,128)(2,1)S(1)}, bf16[4,128,256]{2,1,0:T(8,128)(2,1)S(1)}, u32[]{:S(2)}, u32[]{:S(2)}) collective-permute-start(bf16[4,128,256]{2,1,0:T(8,128)(2,1)S(1)} %slice.46), channel_id=1, source_target_pairs={{0,3},{4,7},{1,0},{5,4},{2,1},{6,5},{3,2},{7,6},{8,11},{12,15},{9,... | collective-permute-start | bytes 786440 | tf_op jit(solution)/shard_map/ppermute | solution.py:45
  232.2 19.3 %collective-permute-start.34 = (bf16[8,128,256]{2,1,0:T(8,128)(2,1)}, bf16[8,128,256]{2,1,0:T(8,128)(2,1)S(1)}, u32[]{:S(2)}, u32[]{:S(2)}) collective-permute-start(bf16[8,128,256]{2,1,0:T(8,128)(2,1)} %get-tuple-element.52), channel_id=1, source_target_pairs={{0,8},{8,0},{16,24},{24,16},{32,40},{40,32},{48,56},{56,48},{64,72... | collective-permute-start | bytes 1572872 | tf_op jit(solution)/shard_map/ppermute | solution.py:35
  232.3 12.9 %collective-permute-start.37 = (bf16[8,128,256]{2,1,0:T(8,128)(2,1)}, bf16[8,128,256]{2,1,0:T(8,128)(2,1)S(1)}, u32[]{:S(2)}, u32[]{:S(2)}) collective-permute-start(bf16[8,128,256]{2,1,0:T(8,128)(2,1)} %get-tuple-element.56), channel_id=1, source_target_pairs={{0,8},{8,0},{16,24},{24,16},{32,40},{40,32},{48,56},{56,48},{64,72... | collective-permute-start | bytes 1572872 | tf_op jit(solution)/shard_map/ppermute | solution.py:35
  233.0 16.5 %collective-permute-start.47 = (bf16[8,128,256]{2,1,0:T(8,128)(2,1)}, bf16[8,128,256]{2,1,0:T(8,128)(2,1)S(1)}, u32[]{:S(2)}, u32[]{:S(2)}) collective-permute-start(bf16[8,128,256]{2,1,0:T(8,128)(2,1)} %get-tuple-element.67), channel_id=1, source_target_pairs={{0,8},{8,0},{16,24},{24,16},{32,40},{40,32},{48,56},{56,48},{64,72... | collective-permute-start | bytes 1572872 | tf_op jit(solution)/shard_map/ppermute | solution.py:35
  244.4 19.5 %collective-permute-start.46 = (bf16[8,128,256]{2,1,0:T(8,128)(2,1)}, bf16[8,128,256]{2,1,0:T(8,128)(2,1)}, u32[]{:S(2)}, u32[]{:S(2)}) collective-permute-start(bf16[8,128,256]{2,1,0:T(8,128)(2,1)} %get-tuple-element.65), channel_id=1, source_target_pairs={{0,8},{8,0},{16,24},{24,16},{32,40},{40,32},{48,56},{56,48},{64,72... | collective-permute-start | bytes 1572872 | tf_op jit(solution)/shard_map/ppermute | solution.py:35
  245.1 13.8 %collective-permute-start.44 = (bf16[8,128,256]{2,1,0:T(8,128)(2,1)S(1)}, bf16[8,128,256]{2,1,0:T(8,128)(2,1)S(1)}, u32[]{:S(2)}, u32[]{:S(2)}) collective-permute-start(bf16[8,128,256]{2,1,0:T(8,128)(2,1)S(1)} %add_convert_fusion.4), channel_id=1, source_target_pairs={{0,96},{8,104},{16,112},{24,120},{32,0},{40,8},{48,16},{56,24},{64... | collective-permute-start | bytes 1572872 | tf_op jit(solution)/shard_map/ppermute | solution.py:35
  251.4 13.5 %collective-permute-start.48 = (bf16[8,128,256]{2,1,0:T(8,128)(2,1)S(1)}, bf16[8,128,256]{2,1,0:T(8,128)(2,1)S(1)}, u32[]{:S(2)}, u32[]{:S(2)}) collective-permute-start(bf16[8,128,256]{2,1,0:T(8,128)(2,1)S(1)} %add_convert_fusion.2), channel_id=1, source_target_pairs={{0,32},{8,40},{16,48},{24,56},{32,64},{40,72},{48,80},{56,88},{64,... | collective-permute-start | bytes 1572872 | tf_op jit(solution)/shard_map/ppermute | solution.py:35
  252.7 32.0 %collective-permute-start.33 = (bf16[8,128,256]{2,1,0:T(8,128)(2,1)}, bf16[8,128,256]{2,1,0:T(8,128)(2,1)}, u32[]{:S(2)}, u32[]{:S(2)}) collective-permute-start(bf16[8,128,256]{2,1,0:T(8,128)(2,1)} %get-tuple-element.50), channel_id=1, source_target_pairs={{0,8},{8,0},{16,24},{24,16},{32,40},{40,32},{48,56},{56,48},{64,72... | collective-permute-start | bytes 1572872 | tf_op jit(solution)/shard_map/ppermute | solution.py:35
  258.9 25.8 %collective-permute-start.35 = (bf16[8,128,256]{2,1,0:T(8,128)(2,1)S(1)}, bf16[8,128,256]{2,1,0:T(8,128)(2,1)S(1)}, u32[]{:S(2)}, u32[]{:S(2)}) collective-permute-start(bf16[8,128,256]{2,1,0:T(8,128)(2,1)S(1)} %add_convert_fusion.6), channel_id=1, source_target_pairs={{0,32},{8,40},{16,48},{24,56},{32,64},{40,72},{48,80},{56,88},{64,... | collective-permute-start | bytes 1572872 | tf_op jit(solution)/shard_map/ppermute | solution.py:35
  263.5 21.2 %collective-permute-start.45 = (bf16[8,128,256]{2,1,0:T(8,128)(2,1)S(1)}, bf16[8,128,256]{2,1,0:T(8,128)(2,1)S(1)}, u32[]{:S(2)}, u32[]{:S(2)}) collective-permute-start(bf16[8,128,256]{2,1,0:T(8,128)(2,1)S(1)} %add_convert_fusion.3), channel_id=1, source_target_pairs={{0,96},{8,104},{16,112},{24,120},{32,0},{40,8},{48,16},{56,24},{64... | collective-permute-start | bytes 1572872 | tf_op jit(solution)/shard_map/ppermute | solution.py:35
  267.1 17.6 %collective-permute-start.49 = (bf16[8,128,256]{2,1,0:T(8,128)(2,1)}, bf16[8,128,256]{2,1,0:T(8,128)(2,1)S(1)}, u32[]{:S(2)}, u32[]{:S(2)}) collective-permute-start(bf16[8,128,256]{2,1,0:T(8,128)(2,1)} %add_convert_fusion.1), channel_id=1, source_target_pairs={{0,16},{8,24},{16,0},{24,8},{32,48},{40,56},{48,32},{56,40},{64,80... | collective-permute-start | bytes 1572872 | tf_op jit(solution)/shard_map/ppermute | solution.py:35
  (51 other events, 985.7 us)

commit v6 on v5

--- a/solution.py
+++ b/solution.py
@@ -11,7 +11,6 @@
 GROUP = 32
 BF16, F32 = jnp.bfloat16, jnp.float32
 VMEM_LIMIT = 60 * 2**20
-ENLIST = 4
 RING = 4
 PLACES = ((2, 1), (1, 1), (-1, 1), (2, 0), (0, 1), (1, 0), (-1, 0), (0, 0))
 ANY = pl.BlockSpec(memory_space=pl.ANY)
@@ -63,9 +62,11 @@
     )(*arrays)
 
 
-def gather_tree(own, up, down, pair):
+def gather_tree(own, up, down, pair, tie=False):
     half = own.shape[0] // 2
     below, above, beside = up(own), down(own), pair(own)
+    if tie:
+        above, beside = together(above, beside)
     below_beside, above_beside, far = pair(below), down(beside), up(below)
     far_beside = [(0, down(above_beside[:half])), (half, up(below_beside[half:]))]
     whole = {
@@ -80,14 +81,15 @@
     return [far_beside if place == (2, 1) else [(0, whole[place])] for place in PLACES]
 
 
-def scatter_first(corner, blocks, up, down):
+def scatter_first(corner, blocks, up, down, *later):
     low, high = (part.astype(BF16) for part in corner)
     half = low.shape[0]
     none = ((0, 0), (0, 0))
-    low, high = together(up(low), down(high))
+    low, high, *later = together(up(low), down(high), *later)
     above_beside = blocks[1, 1].astype(F32) + jnp.pad(low.astype(F32), ((0, half), *none))
     below_beside = blocks[-1, 1].astype(F32) + jnp.pad(high.astype(F32), ((half, 0), *none))
-    return above_beside.astype(BF16), below_beside.astype(BF16), blocks[2, 0].astype(BF16)
+    leaving = (above_beside.astype(BF16), below_beside.astype(BF16), blocks[2, 0].astype(BF16))
+    return leaving, *later
 
 
 def scatter_second(leaving, blocks, up, down, pair):
@@ -167,15 +169,13 @@
     for i in range(sources):
         source = order_ref[i]
 
-        def enlist(g, count, i=i, source=source):
-            for j in range(ENLIST):
-                k = g * ENLIST + j
-                tile_list[count + j] = i * slots + k
-                panel_list[count + j] = i * col_tiles + cols_ref[source, k]
-                key_list[count + j] = rows_ref[source, k]
-            return count + jnp.minimum(ENLIST, counts_ref[source] - g * ENLIST)
-
-        count = lax.fori_loop(0, (counts_ref[source] + ENLIST - 1) // ENLIST, enlist, count)
+        def enlist(k, count, i=i, source=source):
+            tile_list[count] = i * slots + k
+            panel_list[count] = i * col_tiles + cols_ref[source, k]
+            key_list[count] = rows_ref[source, k]
+            return count + 1
+
+        count = lax.fori_loop(0, counts_ref[source], enlist, count)
         ends.append(count)
     fill_tail(count, spare, tile_list, panel_list, key_list)
 
@@ -296,15 +296,13 @@
     for i in range(sources):
         source = order_ref[i]
 
-        def enlist(g, count, i=i, source=source):
-            for j in range(ENLIST):
-                k = g * ENLIST + j
-                tile_list[count + j] = i * slots + k
-                panel_list[count + j] = rows_ref[source, k]
-                key_list[count + j] = i * col_tiles + cols_ref[source, k]
-            return count + jnp.minimum(ENLIST, counts_ref[source] - g * ENLIST)
-
-        count = lax.fori_loop(0, (counts_ref[source] + ENLIST - 1) // ENLIST, enlist, count)
+        def enlist(k, count, i=i, source=source):
+            tile_list[count] = i * slots + k
+            panel_list[count] = rows_ref[source, k]
+            key_list[count] = i * col_tiles + cols_ref[source, k]
+            return count + 1
+
+        count = lax.fori_loop(0, counts_ref[source], enlist, count)
         ends.append(count)
     fill_tail(count, sources * col_tiles, tile_list, panel_list, key_list)
 
@@ -436,25 +434,24 @@
     up, down, pair = rep_tree
     low, high, *rest, offset = forward_tiles(order, dests, scalars, tiles, shards)
     blocks = dict(zip(PLACES[1:], rest))
-    leaving = scatter_first((low, high), blocks, up, down)
+    [leaving] = scatter_first((low, high), blocks, up, down)
     leaving = scatter_second(leaving, blocks, *rep_tree)
     shifted = scatter_third(leaving, blocks[0, 0], *rep_tree).reshape(local_rows, width)
     aggregate = shifted.astype(BF16)
     projected = jnp.dot(aggregate, weight, preferred_element_type=F32)
     own_mean = jnp.sum(projected, axis=0) / local_rows
     own_square = jnp.sum((projected - own_mean) ** 2, axis=0)
-    moved = jnp.dot(offset, weight.astype(F32), precision=lax.Precision.HIGHEST)
-    everyone = copies_of_all(
-        jnp.stack([own_mean, own_square, moved[0], offset[0]]), ("blk", "rep")
-    ).reshape(blk_count, rep_count, 4, width)
-    moves = jnp.sum(everyone[:, :, 2], axis=1)
+    everyone = copies_of_all(jnp.stack([own_mean, own_square, offset[0]]), ("blk", "rep"))
+    everyone = everyone.reshape(blk_count, rep_count, 3, width)
+    offsets = jnp.sum(everyone[:, :, 2], axis=1)
+    moves = jnp.dot(offsets, weight.astype(F32), precision=lax.Precision.HIGHEST)
     means = everyone[:, :, 0] + moves[:, None]
     feat_mean = jnp.sum(means, axis=(0, 1)) / (blk_count * rep_count)
     square_sum = jnp.sum(everyone[:, :, 1], axis=(0, 1)) + local_rows * jnp.sum(
         (means - feat_mean) ** 2, axis=(0, 1)
     )
-    group = lax.dynamic_index_in_dim(everyone, blk, 0, keepdims=False)
-    group_moved, group_offset = jnp.sum(group[:, 2], axis=0), jnp.sum(group[:, 3], axis=0)
+    group_moved = lax.dynamic_index_in_dim(moves, blk, 0, keepdims=False)
+    group_offset = lax.dynamic_index_in_dim(offsets, blk, 0, keepdims=False)
     inv_std = lax.rsqrt(square_sum / node_count + norm_eps)
     normed = (projected + (group_moved - feat_mean)) * inv_std
     affine = norm_gain * normed + norm_shift
@@ -477,12 +474,11 @@
     sent = lax.dot_general(
         grad_summed, weight, (((1,), (1,)), ((), ())), preferred_element_type=F32
     ).astype(BF16)
-    grads = gather_tree(sent.reshape(col_tiles, tile, width), *rep_tree)
+    grads = gather_tree(sent.reshape(col_tiles, tile, width), *rep_tree, tie=True)
     arrived = {place: parts[0][1] for place, parts in zip(PLACES, grads)}
     weight_term = weight_terms(aggregate, grad_summed, group_offset, [arrived[1, 0]])
     pieces = lax.all_to_all(weight_term.reshape(blk_count, -1, width), "blk", 0, 0)
     piece = sum_first(pieces, [arrived[-1, 1]])
-    terms = copies_of_all(piece, "rep")
 
     half = col_tiles // 2
     sizes = (half, half, *(col_tiles,) * (len(PLACES) - 1))
@@ -493,17 +489,18 @@
         scalars,
         tiles,
         grads,
-        [terms],
+        [piece],
     )
     given, kept = arrays[: len(sizes)], arrays[len(sizes) :]
     low, high, *rest = [b.astype(F32) + across(a).astype(F32) for a, b in zip(given, kept)]
     products = dict(zip(PLACES[1:], rest))
     up, down, pair = blk_tree
-    leaving = scatter_first((low, high), products, up, down)
-    leaving = scatter_second(leaving, products, *blk_tree)
-    grad_w = copies_of_all(sum_first(terms, [leaving[0][:1, :16, :128]]), "blk")
-    grad_x = scatter_third(leaving, products[0, 0], *blk_tree).astype(BF16)
-    grad_w = grad_w.reshape(weight.shape)
+    leaving, piece = scatter_first((low, high), products, up, down, piece)
+    terms = copies_of_all(piece, "rep")
+    below, beside, above = scatter_second(leaving, products, *blk_tree)
+    beside, terms = together(beside, terms)
+    grad_x = scatter_third((below, beside, above), products[0, 0], *blk_tree).astype(BF16)
+    grad_w = copies_of_all(jnp.sum(terms, axis=0), "blk").reshape(weight.shape)
     return (output, grad_x.reshape(local_rows, width), grad_w, grad_gamma, grad_beta)
 
 

time: 289 us -> 291 us (level)
    ppermute x16, waiting for transfers between devices: 35.4 us -> 42.6 us  [link(): return lambda value: lax.ppermute(value, 'rep', pairs)]
    all_to_all x2, waiting for transfers between devices: 20.2 us -> 13.9 us  [copies_of_all(): lax.all_to_all(jnp.broadcast_to(value[None], (count, *value.shape)), axis...]
    ppermute x34, waiting for transfers between devices: 33 us -> 27.9 us  [link(): return lambda value: lax.ppermute(value, 'blk', pairs)]
    all_to_all x1, waiting for transfers between devices: 2.02 us -> 6.59 us  [on_device(): lax.all_to_all(weight_term.reshape(blk_count, -1, width), 'blk', 0, 0)]
    all_to_all x2, starting transfers between devices: 17.3 us -> 12.9 us  [copies_of_all(): lax.all_to_all(jnp.broadcast_to(value[None], (count, *value.shape)), axis...]
    ppermute x16, starting transfers between devices: 21.2 us -> 25.6 us  [link(): return lambda value: lax.ppermute(value, 'rep', pairs)]
  transfers between devices with their start and end apart: 53 -> 53, of which waited for: 20 -> 19; matrix products, arithmetic and copies ran while one was open for 8% -> 8% of each run, Pallas kernels for 2% -> 1%
where the time goes in v6:
time: 291 us; the launch traced here: 289 us
  waiting for transfers between devices  90.9 us (31%)
  starting transfers between devices  86.5 us (30%)
  Pallas kernels  41.7 us (14%)
  blocking collectives  30.8 us (11%)
  other arithmetic  25.4 us (9%)
  local copies, waits for them, and re-layouts  12.3 us (4%)
    ppermute x16, waiting for transfers between devices, link(): return lambda value: lax.ppermute(value, 'rep', pairs)  42.6 us
    ppermute x34, starting transfers between devices, link(): return lambda value: lax.ppermute(value, 'blk', pairs)  41.7 us
    all_to_all x2, blocking collectives, copies_of_all(): lax.all_to_all(jnp.broadcast_to(value[None], (count, *value.shape)), axis...  30.8 us
    ppermute x34, waiting for transfers between devices, link(): return lambda value: lax.ppermute(value, 'blk', pairs)  27.9 us
    ppermute x16, starting transfers between devices, link(): return lambda value: lax.ppermute(value, 'rep', pairs)  25.6 us
    pallas_call x1, Pallas kernels, backward_tiles(): pl.pallas_call(functools.partial(backward_kernel, layout, sizes, len(afte...  19.9 us
    pallas_call x1, Pallas kernels, forward_tiles(): pl.pallas_call(functools.partial(forward_kernel, layout), in_specs=[SMEM]...  17.9 us
    all_to_all x2, waiting for transfers between devices, copies_of_all(): lax.all_to_all(jnp.broadcast_to(value[None], (count, *value.shape)), axis...  13.9 us
  transfers between devices with their start and end apart: 53, of which 19 were waited for; matrix products, arithmetic and copies ran while one was open for 8% of the time, Pallas kernels for 1%

profile of v6, /device:TPU:1, one launch (start us, length us, event | category | flops | bytes accessed | tf_op | source)
XLA Modules:
  0.0 289.5 jit_solution(3831929688896895384)
XLA Ops:
  6.6 7.7 %collective-permute-done.5.refs_6_ = bf16[8,128,256]{2,1,0:T(8,128)(2,1)S(1)} collective-permute-done((bf16[8,128,256]{2,1,0:T(8,128)(2,1)}, bf16[8,128,256]{2,1,0:T(8,128)(2,1)S(1)}, u32[]{:S(2)}, u32[]{:S(2)}) %collective-permute-start.5) | collective-permute-done | bytes 524320 | tf_op jit(solution)/shard_map/ppermute | solution.py:34
  14.3 4.0 %collective-permute-start.11 = (bf16[8,128,256]{2,1,0:T(8,128)(2,1)S(1)}, bf16[8,128,256]{2,1,0:T(8,128)(2,1)S(1)}, u32[]{:S(2)}, u32[]{:S(2)}) collective-permute-start(bf16[8,128,256]{2,1,0:T(8,128)(2,1)S(1)} %collective-permute-done.5.refs_6_), channel_id=1, source_target_pairs={{0,96},{8,104},{16,112},{24,120},{32,0},{40,8},{48,16},{56,24},{64... | collective-permute-start | bytes 1572872 | tf_op jit(solution)/shard_map/ppermute | solution.py:34
  22.2 6.5 %collective-permute-done.11.refs_12_ = bf16[8,128,256]{2,1,0:T(8,128)(2,1)S(1)} collective-permute-done((bf16[8,128,256]{2,1,0:T(8,128)(2,1)S(1)}, bf16[8,128,256]{2,1,0:T(8,128)(2,1)S(1)}, u32[]{:S(2)}, u32[]{:S(2)}) %collective-permute-start.11) | collective-permute-done | bytes 524320 | tf_op jit(solution)/shard_map/ppermute | solution.py:34
  36.2 5.0 %collective-permute-done.7.refs_8_ = bf16[8,128,256]{2,1,0:T(8,128)(2,1)S(1)} collective-permute-done((bf16[8,128,256]{2,1,0:T(8,128)(2,1)S(1)}, bf16[8,128,256]{2,1,0:T(8,128)(2,1)S(1)}, u32[]{:S(2)}, u32[]{:S(2)}) %collective-permute-start.7) | collective-permute-done | bytes 524320 | tf_op jit(solution)/shard_map/ppermute | solution.py:34
  41.2 5.8 %collective-permute-start.10 = (bf16[8,128,256]{2,1,0:T(8,128)(2,1)S(1)}, bf16[8,128,256]{2,1,0:T(8,128)(2,1)}, u32[]{:S(2)}, u32[]{:S(2)}) collective-permute-start(bf16[8,128,256]{2,1,0:T(8,128)(2,1)S(1)} %collective-permute-done.9.refs_10_), channel_id=1, source_target_pairs={{0,8},{8,0},{16,24},{24,16},{32,40},{40,32},{48,56},{56,48},{64,72... | collective-permute-start | bytes 1572872 | tf_op jit(solution)/shard_map/ppermute | solution.py:34
  51.6 17.9 %forward_tiles.1 = (bf16[4,128,256]{2,1,0:T(8,128)(2,1)}, bf16[4,128,256]{2,1,0:T(8,128)(2,1)}, bf16[8,128,256]{2,1,0:T(8,128)(2,1)}, bf16[8,128,256]{2,1,0:T(8,...) custom-call(s32[16]{0:T(128)} %reshape.73.order_ref, ...), custom_call_target="tpu_custom_call" | custom-call | flops 6000000000 | bytes 31457280 | tf_op jit(solution)/shard_map/forward_tiles/pallas_call | solution.py:246
  72.3 6.0 %collective-permute-done.18.refs_0_ = bf16[4,128,256]{2,1,0:T(8,128)(2,1)S(1)} collective-permute-done((bf16[4,128,256]{2,1,0:T(8,128)(2,1)}, bf16[4,128,256]{2,1,0:T(8,128)(2,1)S(1)}, u32[]{:S(2)}, u32[]{:S(2)}) %collective-permute-start.18) | collective-permute-done | bytes 262176 | tf_op jit(solution)/shard_map/ppermute | solution.py:44
  84.8 4.8 %collective-permute-start.20 = (bf16[8,128,256]{2,1,0:T(8,128)(2,1)S(1)}, bf16[8,128,256]{2,1,0:T(8,128)(2,1)S(1)}, u32[]{:S(2)}, u32[]{:S(2)}) collective-permute-start(bf16[8,128,256]{2,1,0:T(8,128)(2,1)S(1)} %add_convert_fusion.11), channel_id=1, source_target_pairs={{0,4},{4,0},{1,5},{5,1},{2,6},{6,2},{3,7},{7,3},{8,12},{12,8},{9,1... | collective-permute-start | bytes 1572872 | tf_op jit(solution)/shard_map/ppermute | solution.py:44
  89.6 4.5 %collective-permute-done.23 = bf16[8,128,256]{2,1,0:T(8,128)(2,1)S(1)} collective-permute-done((bf16[8,128,256]{2,1,0:T(8,128)(2,1)S(1)}, bf16[8,128,256]{2,1,0:T(8,128)(2,1)S(1)}, u32[]{:S(2)}, u32[]{:S(2)}) %collective-permute-start.23) | collective-permute-done | bytes 524320 | tf_op jit(solution)/shard_map/ppermute | solution.py:44
  95.3 5.8 %collective-permute-start.24 = (bf16[8,128,256]{2,1,0:T(8,128)(2,1)S(1)}, bf16[8,128,256]{2,1,0:T(8,128)(2,1)S(1)}, u32[]{:S(2)}, u32[]{:S(2)}) collective-permute-start(bf16[8,128,256]{2,1,0:T(8,128)(2,1)S(1)} %add_convert_fusion.8), channel_id=1, source_target_pairs={{0,4},{4,0},{1,5},{5,1},{2,6},{6,2},{3,7},{7,3},{8,12},{12,8},{9,1... | collective-permute-start | bytes 1572872 | tf_op jit(solution)/shard_map/ppermute | solution.py:44
  102.9 2.5 collective-permute-done.17
  105.4 5.6 %collective-permute-done.24 = bf16[8,128,256]{2,1,0:T(8,128)(2,1)S(1)} collective-permute-done((bf16[8,128,256]{2,1,0:T(8,128)(2,1)S(1)}, bf16[8,128,256]{2,1,0:T(8,128)(2,1)S(1)}, u32[]{:S(2)}, u32[]{:S(2)}) %collective-permute-start.24) | collective-permute-done | bytes 524320 | tf_op jit(solution)/shard_map/ppermute | solution.py:44
  111.0 2.4 collective-permute-done.22
  116.8 9.3 %all-to-all-start = ((f32[128,3,256]{2,1,0:T(4,128)}), f32[128,3,256]{2,1,0:T(4,128)S(1)}, u32[]{:S(2)}, u32[]{:S(2)}) async-start(f32[128,3,256]{2,1,0:T(4,128)} %broadcast_in_dim.12), calls=%async_computation | async-start | bytes 1048576 | tf_op jit(solution)/shard_map/all_to_all | solution.py:398
  126.1 13.9 %all-to-all-done = f32[128,3,256]{2,1,0:T(4,128)S(1)} async-done(((f32[128,3,256]{2,1,0:T(4,128)}), f32[128,3,256]{2,1,0:T(4,128)S(1)}, u32[]{:S(2)}, u32[]{:S(2)}) %all-to-all-start) | async-done | bytes 393248 | tf_op jit(solution)/shard_map/all_to_all | solution.py:398
  141.4 15.4 %all_to_all.25 = f32[128,2,256]{2,1,0:T(2,128)S(1)} all-to-all(f32[128,2,256]{2,1,0:T(2,128)S(1)} %broadcast_in_dim.13), channel_id=1, replica_groups=mesh['blk'=16,'rep'=8] {'blk','rep'}, dimensions={0} | all-to-all | bytes 524288 | tf_op jit(solution)/shard_map/all_to_all | solution.py:398
  160.7 2.4 collective-permute-start.25
  163.1 10.5 %collective-permute-done.29.refs_7_ = bf16[8,128,256]{2,1,0:T(8,128)(2,1)} collective-permute-done((bf16[8,128,256]{2,1,0:T(8,128)(2,1)S(1)}, bf16[8,128,256]{2,1,0:T(8,128)(2,1)}, u32[]{:S(2)}, u32[]{:S(2)}) %collective-permute-start.29) | collective-permute-done | bytes 524320 | tf_op jit(solution)/shard_map/ppermute | solution.py:44
  177.8 9.4 %collective-permute-done.30.refs_0_.refs_3_ = bf16[8,128,256]{2,1,0:T(8,128)(2,1)S(1)} collective-permute-done((bf16[8,128,256]{2,1,0:T(8,128)(2,1)}, bf16[8,128,256]{2,1,0:T(8,128)(2,1)S(1)}, u32[]{:S(2)}, u32[]{:S(2)}) %collective-permute-start.30) | collective-permute-done | bytes 524320 | tf_op jit(solution)/shard_map/ppermute | solution.py:44
  188.5 2.3 collective-permute-start.28
  191.6 2.3 weight_terms.1
  193.9 6.3 %all-to-all-start.2 = ((f32[16,16,256]{2,1,0:T(8,128)}), f32[16,16,256]{2,1,0:T(8,128)S(1)}, u32[]{:S(2)}, u32[]{:S(2)}) async-start(f32[16,16,256]{2,1,0:T(8,128)} %bitcast.62), calls=%async_computation.2 | async-start | bytes 524288 | tf_op jit(solution)/shard_map/all_to_all | solution.py:480
  200.9 6.6 %all-to-all-done.2.value_ref = f32[16,16,256]{2,1,0:T(8,128)S(1)} async-done(((f32[16,16,256]{2,1,0:T(8,128)}), f32[16,16,256]{2,1,0:T(8,128)S(1)}, u32[]{:S(2)}, u32[]{:S(2)}) %all-to-all-start.2) | async-done | bytes 262176 | tf_op jit(solution)/shard_map/all_to_all | solution.py:480
  209.8 19.9 %backward_tiles.1 = (bf16[4,128,256]{2,1,0:T(8,128)(2,1)}, bf16[4,128,256]{2,1,0:T(8,128)(2,1)}, bf16[8,128,256]{2,1,0:T(8,128)(2,1)}, bf16[8,128,256]{2,1,0:T(8...) custom-call(s32[16]{0:T(128)} %concatenate.4.order_ref, ...), custom_call_target="tpu_custom_call" | custom-call | flops 8000000000 | bytes 20971520 | tf_op jit(solution)/shard_map/backward_tiles/pallas_call | solution.py:341
  235.8 2.6 collective-permute-start.41
  239.5 4.0 %collective-permute-done.39.refs_0_ = bf16[4,128,256]{2,1,0:T(8,128)(2,1)S(1)} collective-permute-done((bf16[4,128,256]{2,1,0:T(8,128)(2,1)S(1)}, bf16[4,128,256]{2,1,0:T(8,128)(2,1)S(1)}, u32[]{:S(2)}, u32[]{:S(2)}) %collective-permute-start.39) | collective-permute-done | bytes 262176 | tf_op jit(solution)/shard_map/ppermute | solution.py:34
  245.2 3.1 %collective-permute-start.44 = (bf16[8,128,256]{2,1,0:T(8,128)(2,1)S(1)}, bf16[8,128,256]{2,1,0:T(8,128)(2,1)}, u32[]{:S(2)}, u32[]{:S(2)}) collective-permute-start(bf16[8,128,256]{2,1,0:T(8,128)(2,1)S(1)} %add_convert_fusion.4), channel_id=1, source_target_pairs={{0,96},{8,104},{16,112},{24,120},{32,0},{40,8},{48,16},{56,24},{64... | collective-permute-start | bytes 1572872 | tf_op jit(solution)/shard_map/ppermute | solution.py:34
  255.2 3.6 %all-to-all-start.3 = ((f32[8,16,256]{2,1,0:T(8,128)}), f32[8,16,256]{2,1,0:T(8,128)S(1)}, u32[]{:S(2)}, u32[]{:S(2)}) async-start(f32[8,16,256]{2,1,0:T(8,128)} %broadcast_in_dim.16), calls=%async_computation.3 | async-start | bytes 262144 | tf_op jit(solution)/shard_map/all_to_all | solution.py:398
  260.4 3.6 %collective-permute-done.42 = bf16[8,128,256]{2,1,0:T(8,128)(2,1)} collective-permute-done((bf16[8,128,256]{2,1,0:T(8,128)(2,1)}, bf16[8,128,256]{2,1,0:T(8,128)(2,1)}, u32[]{:S(2)}, u32[]{:S(2)}) %collective-permute-start.42) | collective-permute-done | bytes 524320 | tf_op jit(solution)/shard_map/ppermute | solution.py:34
  266.2 2.3 add_convert_fusion.1.refs_0_
  270.8 15.4 %all_to_all.26 = f32[16,16,256]{2,1,0:T(8,128)S(1)} all-to-all(f32[16,16,256]{2,1,0:T(8,128)S(1)} %broadcast_in_dim.17), channel_id=1, replica_groups=mesh['blk'=16,'rep'=8] {'blk'}, dimensions={0} | all-to-all | bytes 524288 | tf_op jit(solution)/shard_map/all_to_all | solution.py:398
  286.2 2.5 add_convert_fusion
  (193 shorter events, 74.6 us)
Async XLA Ops:
  0.6 13.7 %collective-permute-start.5 = (bf16[8,128,256]{2,1,0:T(8,128)(2,1)}, bf16[8,128,256]{2,1,0:T(8,128)(2,1)S(1)}, u32[]{:S(2)}, u32[]{:S(2)}) collective-permute-start(bf16[8,128,256]{2,1,0:T(8,128)(2,1)} %bitcast.63), channel_id=1, source_target_pairs={{0,16},{8,24},{16,0},{24,8},{32,48},{40,56},{48,32},{56,40},{64,80... | collective-permute-start | bytes 1572872 | tf_op jit(solution)/shard_map/ppermute | solution.py:34
  2.9 15.5 %collective-permute-start.1 = (bf16[8,128,256]{2,1,0:T(8,128)(2,1)}, bf16[8,128,256]{2,1,0:T(8,128)(2,1)S(1)}, u32[]{:S(2)}, u32[]{:S(2)}) collective-permute-start(bf16[8,128,256]{2,1,0:T(8,128)(2,1)} %bitcast.64), channel_id=1, source_target_pairs={{0,32},{8,40},{16,48},{24,56},{32,64},{40,72},{48,80},{56,88},{64,... | collective-permute-start | bytes 1572872 | tf_op jit(solution)/shard_map/ppermute | solution.py:34
  4.5 17.2 %collective-permute-start.3 = (bf16[8,128,256]{2,1,0:T(8,128)(2,1)}, bf16[8,128,256]{2,1,0:T(8,128)(2,1)S(1)}, u32[]{:S(2)}, u32[]{:S(2)}) collective-permute-start(bf16[8,128,256]{2,1,0:T(8,128)(2,1)} %bitcast.65), channel_id=1, source_target_pairs={{0,96},{8,104},{16,112},{24,120},{32,0},{40,8},{48,16},{56,24},{64... | collective-permute-start | bytes 1572872 | tf_op jit(solution)/shard_map/ppermute | solution.py:34
  14.3 14.4 %collective-permute-start.11 = (bf16[8,128,256]{2,1,0:T(8,128)(2,1)S(1)}, bf16[8,128,256]{2,1,0:T(8,128)(2,1)S(1)}, u32[]{:S(2)}, u32[]{:S(2)}) collective-permute-start(bf16[8,128,256]{2,1,0:T(8,128)(2,1)S(1)} %collective-permute-done.5.refs_6_), channel_id=1, source_target_pairs={{0,96},{8,104},{16,112},{24,120},{32,0},{40,8},{48,16},{56,24},{64... | collective-permute-start | bytes 1572872 | tf_op jit(solution)/shard_map/ppermute | solution.py:34
  19.6 14.5 %collective-permute-start = (bf16[8,128,256]{2,1,0:T(8,128)(2,1)}, bf16[8,128,256]{2,1,0:T(8,128)(2,1)S(1)}, u32[]{:S(2)}, u32[]{:S(2)}) collective-permute-start(bf16[8,128,256]{2,1,0:T(8,128)(2,1)} %bitcast.66), channel_id=1, source_target_pairs={{0,8},{8,0},{16,24},{24,16},{32,40},{40,32},{48,56},{56,48},{64,72... | collective-permute-start | bytes 1572872 | tf_op jit(solution)/shard_map/ppermute | solution.py:34
  21.7 13.7 %collective-permute-start.6 = (bf16[8,128,256]{2,1,0:T(8,128)(2,1)S(1)}, bf16[8,128,256]{2,1,0:T(8,128)(2,1)S(1)}, u32[]{:S(2)}, u32[]{:S(2)}) collective-permute-start(bf16[8,128,256]{2,1,0:T(8,128)(2,1)S(1)} %collective-permute-done.5.refs_6_), channel_id=1, source_target_pairs={{0,8},{8,0},{16,24},{24,16},{32,40},{40,32},{48,56},{56,48},{64,72... | collective-permute-start | bytes 1572872 | tf_op jit(solution)/shard_map/ppermute | solution.py:34
  21.7 13.9 %collective-permute-start.4 = (bf16[8,128,256]{2,1,0:T(8,128)(2,1)S(1)}, bf16[8,128,256]{2,1,0:T(8,128)(2,1)S(1)}, u32[]{:S(2)}, u32[]{:S(2)}) collective-permute-start(bf16[8,128,256]{2,1,0:T(8,128)(2,1)S(1)} %collective-permute-done.3.refs_4_), channel_id=1, source_target_pairs={{0,8},{8,0},{16,24},{24,16},{32,40},{40,32},{48,56},{56,48},{64,72... | collective-permute-start | bytes 1572872 | tf_op jit(solution)/shard_map/ppermute | solution.py:34
  30.4 16.6 %collective-permute-start.2 = (bf16[8,128,256]{2,1,0:T(8,128)(2,1)S(1)}, bf16[8,128,256]{2,1,0:T(8,128)(2,1)S(1)}, u32[]{:S(2)}, u32[]{:S(2)}) collective-permute-start(bf16[8,128,256]{2,1,0:T(8,128)(2,1)S(1)} %collective-permute-done.1.refs_2_), channel_id=1, source_target_pairs={{0,8},{8,0},{16,24},{24,16},{32,40},{40,32},{48,56},{56,48},{64,72... | collective-permute-start | bytes 1572872 | tf_op jit(solution)/shard_map/ppermute | solution.py:34
  34.1 13.9 %collective-permute-start.13 = (bf16[4,128,256]{2,1,0:T(8,128)(2,1)}, bf16[4,128,256]{2,1,0:T(8,128)(2,1)S(1)}, u32[]{:S(2)}, u32[]{:S(2)}) collective-permute-start(bf16[4,128,256]{2,1,0:T(8,128)(2,1)} %slice.28), channel_id=1, source_target_pairs={{0,96},{8,104},{16,112},{24,120},{32,0},{40,8},{48,16},{56,24},{64... | collective-permute-start | bytes 786440 | tf_op jit(solution)/shard_map/ppermute | solution.py:34
  35.6 15.7 %collective-permute-start.12 = (bf16[8,128,256]{2,1,0:T(8,128)(2,1)S(1)}, bf16[8,128,256]{2,1,0:T(8,128)(2,1)}, u32[]{:S(2)}, u32[]{:S(2)}) collective-permute-start(bf16[8,128,256]{2,1,0:T(8,128)(2,1)S(1)} %collective-permute-done.11.refs_12_), channel_id=1, source_target_pairs={{0,8},{8,0},{16,24},{24,16},{32,40},{40,32},{48,56},{56,48},{64,72... | collective-permute-start | bytes 1572872 | tf_op jit(solution)/shard_map/ppermute | solution.py:34
  82.8 18.3 %collective-permute-start.21 = (bf16[8,128,256]{2,1,0:T(8,128)(2,1)}, bf16[8,128,256]{2,1,0:T(8,128)(2,1)S(1)}, u32[]{:S(2)}, u32[]{:S(2)}) collective-permute-start(bf16[8,128,256]{2,1,0:T(8,128)(2,1)} %get-tuple-element.49), channel_id=1, source_target_pairs={{0,3},{4,7},{1,0},{5,4},{2,1},{6,5},{3,2},{7,6},{8,11},{12,15},{9,... | collective-permute-start | bytes 1572872 | tf_op jit(solution)/shard_map/ppermute | solution.py:44
  84.8 16.3 %collective-permute-start.20 = (bf16[8,128,256]{2,1,0:T(8,128)(2,1)S(1)}, bf16[8,128,256]{2,1,0:T(8,128)(2,1)S(1)}, u32[]{:S(2)}, u32[]{:S(2)}) collective-permute-start(bf16[8,128,256]{2,1,0:T(8,128)(2,1)S(1)} %add_convert_fusion.11), channel_id=1, source_target_pairs={{0,4},{4,0},{1,5},{5,1},{2,6},{6,2},{3,7},{7,3},{8,12},{12,8},{9,1... | collective-permute-start | bytes 1572872 | tf_op jit(solution)/shard_map/ppermute | solution.py:44
  89.6 15.8 %collective-permute-start.17 = (bf16[8,128,256]{2,1,0:T(8,128)(2,1)}, bf16[8,128,256]{2,1,0:T(8,128)(2,1)S(1)}, u32[]{:S(2)}, u32[]{:S(2)}) collective-permute-start(bf16[8,128,256]{2,1,0:T(8,128)(2,1)} %get-tuple-element.43), channel_id=1, source_target_pairs={{0,1},{4,5},{1,2},{5,6},{2,3},{6,7},{3,0},{7,4},{8,9},{12,13},{9,1... | collective-permute-start | bytes 1572872 | tf_op jit(solution)/shard_map/ppermute | solution.py:44
  95.3 15.6 %collective-permute-start.24 = (bf16[8,128,256]{2,1,0:T(8,128)(2,1)S(1)}, bf16[8,128,256]{2,1,0:T(8,128)(2,1)S(1)}, u32[]{:S(2)}, u32[]{:S(2)}) collective-permute-start(bf16[8,128,256]{2,1,0:T(8,128)(2,1)S(1)} %add_convert_fusion.8), channel_id=1, source_target_pairs={{0,4},{4,0},{1,5},{5,1},{2,6},{6,2},{3,7},{7,3},{8,12},{12,8},{9,1... | collective-permute-start | bytes 1572872 | tf_op jit(solution)/shard_map/ppermute | solution.py:44
  116.8 23.2 %all-to-all-start = ((f32[128,3,256]{2,1,0:T(4,128)}), f32[128,3,256]{2,1,0:T(4,128)S(1)}, u32[]{:S(2)}, u32[]{:S(2)}) async-start(f32[128,3,256]{2,1,0:T(4,128)} %broadcast_in_dim.12), calls=%async_computation | async-start | bytes 1048576 | tf_op jit(solution)/shard_map/all_to_all | solution.py:398
  159.3 14.2 %collective-permute-start.29 = (bf16[8,128,256]{2,1,0:T(8,128)(2,1)S(1)}, bf16[8,128,256]{2,1,0:T(8,128)(2,1)}, u32[]{:S(2)}, u32[]{:S(2)}) collective-permute-start(bf16[8,128,256]{2,1,0:T(8,128)(2,1)S(1)} %bitcast.68), channel_id=1, source_target_pairs={{0,1},{4,5},{1,2},{5,6},{2,3},{6,7},{3,0},{7,4},{8,9},{12,13},{9,1... | collective-permute-start | bytes 1572872 | tf_op jit(solution)/shard_map/ppermute | solution.py:44
  159.7 15.0 %collective-permute-start.26 = (bf16[8,128,256]{2,1,0:T(8,128)(2,1)S(1)}, bf16[8,128,256]{2,1,0:T(8,128)(2,1)S(1)}, u32[]{:S(2)}, u32[]{:S(2)}) collective-permute-start(bf16[8,128,256]{2,1,0:T(8,128)(2,1)S(1)} %bitcast.69), channel_id=1, source_target_pairs={{0,4},{4,0},{1,5},{5,1},{2,6},{6,2},{3,7},{7,3},{8,12},{12,8},{9,1... | collective-permute-start | bytes 1572872 | tf_op jit(solution)/shard_map/ppermute | solution.py:44
  160.7 14.0 %collective-permute-start.25 = (bf16[8,128,256]{2,1,0:T(8,128)(2,1)S(1)}, bf16[8,128,256]{2,1,0:T(8,128)(2,1)S(1)}, u32[]{:S(2)}, u32[]{:S(2)}) collective-permute-start(bf16[8,128,256]{2,1,0:T(8,128)(2,1)S(1)} %bitcast.70), channel_id=1, source_target_pairs={{0,3},{4,7},{1,0},{5,4},{2,1},{6,5},{3,2},{7,6},{8,11},{12,15},{9,... | collective-permute-start | bytes 1572872 | tf_op jit(solution)/shard_map/ppermute | solution.py:44
  173.5 13.6 %collective-permute-start.30 = (bf16[8,128,256]{2,1,0:T(8,128)(2,1)}, bf16[8,128,256]{2,1,0:T(8,128)(2,1)S(1)}, u32[]{:S(2)}, u32[]{:S(2)}) collective-permute-start(bf16[8,128,256]{2,1,0:T(8,128)(2,1)} %collective-permute-done.29.refs_7_), channel_id=1, source_target_pairs={{0,4},{4,0},{1,5},{5,1},{2,6},{6,2},{3,7},{7,3},{8,12},{12,8},{9,1... | collective-permute-start | bytes 1572872 | tf_op jit(solution)/shard_map/ppermute | solution.py:44
  177.7 32.1 %collective-permute-start.32 = (bf16[8,128,256]{2,1,0:T(8,128)(2,1)}, bf16[8,128,256]{2,1,0:T(8,128)(2,1)}, u32[]{:S(2)}, u32[]{:S(2)}) collective-permute-start(bf16[8,128,256]{2,1,0:T(8,128)(2,1)} %collective-permute-done.29.refs_7_), channel_id=1, source_target_pairs={{0,1},{4,5},{1,2},{5,6},{2,3},{6,7},{3,0},{7,4},{8,9},{12,13},{9,1... | collective-permute-start | bytes 1572872 | tf_op jit(solution)/shard_map/ppermute | solution.py:44
  187.2 22.6 %collective-permute-start.31 = (bf16[4,128,256]{2,1,0:T(8,128)(2,1)S(1)}, bf16[4,128,256]{2,1,0:T(8,128)(2,1)}, u32[]{:S(2)}, u32[]{:S(2)}) collective-permute-start(bf16[4,128,256]{2,1,0:T(8,128)(2,1)S(1)} %slice.34), channel_id=1, source_target_pairs={{0,1},{4,5},{1,2},{5,6},{2,3},{6,7},{3,0},{7,4},{8,9},{12,13},{9,1... | collective-permute-start | bytes 786440 | tf_op jit(solution)/shard_map/ppermute | solution.py:44
  188.5 21.3 %collective-permute-start.28 = (bf16[4,128,256]{2,1,0:T(8,128)(2,1)S(1)}, bf16[4,128,256]{2,1,0:T(8,128)(2,1)}, u32[]{:S(2)}, u32[]{:S(2)}) collective-permute-start(bf16[4,128,256]{2,1,0:T(8,128)(2,1)S(1)} %slice.33), channel_id=1, source_target_pairs={{0,3},{4,7},{1,0},{5,4},{2,1},{6,5},{3,2},{7,6},{8,11},{12,15},{9,... | collective-permute-start | bytes 786440 | tf_op jit(solution)/shard_map/ppermute | solution.py:44
  232.1 20.5 %collective-permute-start.34 = (bf16[8,128,256]{2,1,0:T(8,128)(2,1)}, bf16[8,128,256]{2,1,0:T(8,128)(2,1)S(1)}, u32[]{:S(2)}, u32[]{:S(2)}) collective-permute-start(bf16[8,128,256]{2,1,0:T(8,128)(2,1)} %get-tuple-element.59), channel_id=1, source_target_pairs={{0,8},{8,0},{16,24},{24,16},{32,40},{40,32},{48,56},{56,48},{64,72... | collective-permute-start | bytes 1572872 | tf_op jit(solution)/shard_map/ppermute | solution.py:34
  232.9 17.5 %collective-permute-start.47 = (bf16[8,128,256]{2,1,0:T(8,128)(2,1)}, bf16[8,128,256]{2,1,0:T(8,128)(2,1)S(1)}, u32[]{:S(2)}, u32[]{:S(2)}) collective-permute-start(bf16[8,128,256]{2,1,0:T(8,128)(2,1)} %get-tuple-element.74), channel_id=1, source_target_pairs={{0,8},{8,0},{16,24},{24,16},{32,40},{40,32},{48,56},{56,48},{64,72... | collective-permute-start | bytes 1572872 | tf_op jit(solution)/shard_map/ppermute | solution.py:34
  243.6 15.2 %collective-permute-start.36 = (bf16[8,128,256]{2,1,0:T(8,128)(2,1)}, bf16[8,128,256]{2,1,0:T(8,128)(2,1)S(1)}, u32[]{:S(2)}, u32[]{:S(2)}) collective-permute-start(bf16[8,128,256]{2,1,0:T(8,128)(2,1)} %get-tuple-element.61), channel_id=1, source_target_pairs={{0,8},{8,0},{16,24},{24,16},{32,40},{40,32},{48,56},{56,48},{64,72... | collective-permute-start | bytes 1572872 | tf_op jit(solution)/shard_map/ppermute | solution.py:34
  244.5 21.2 %collective-permute-start.46 = (bf16[8,128,256]{2,1,0:T(8,128)(2,1)}, bf16[8,128,256]{2,1,0:T(8,128)(2,1)}, u32[]{:S(2)}, u32[]{:S(2)}) collective-permute-start(bf16[8,128,256]{2,1,0:T(8,128)(2,1)} %get-tuple-element.72), channel_id=1, source_target_pairs={{0,8},{8,0},{16,24},{24,16},{32,40},{40,32},{48,56},{56,48},{64,72... | collective-permute-start | bytes 1572872 | tf_op jit(solution)/shard_map/ppermute | solution.py:34
  245.2 15.1 %collective-permute-start.44 = (bf16[8,128,256]{2,1,0:T(8,128)(2,1)S(1)}, bf16[8,128,256]{2,1,0:T(8,128)(2,1)}, u32[]{:S(2)}, u32[]{:S(2)}) collective-permute-start(bf16[8,128,256]{2,1,0:T(8,128)(2,1)S(1)} %add_convert_fusion.4), channel_id=1, source_target_pairs={{0,96},{8,104},{16,112},{24,120},{32,0},{40,8},{48,16},{56,24},{64... | collective-permute-start | bytes 1572872 | tf_op jit(solution)/shard_map/ppermute | solution.py:34
  252.6 13.6 %collective-permute-start.48 = (bf16[8,128,256]{2,1,0:T(8,128)(2,1)S(1)}, bf16[8,128,256]{2,1,0:T(8,128)(2,1)}, u32[]{:S(2)}, u32[]{:S(2)}) collective-permute-start(bf16[8,128,256]{2,1,0:T(8,128)(2,1)S(1)} %add_convert_fusion.2), channel_id=1, source_target_pairs={{0,32},{8,40},{16,48},{24,56},{32,64},{40,72},{48,80},{56,88},{64,... | collective-permute-start | bytes 1572872 | tf_op jit(solution)/shard_map/ppermute | solution.py:34
  258.8 27.4 %collective-permute-start.33 = (bf16[8,128,256]{2,1,0:T(8,128)(2,1)}, bf16[8,128,256]{2,1,0:T(8,128)(2,1)}, u32[]{:S(2)}, u32[]{:S(2)}) collective-permute-start(bf16[8,128,256]{2,1,0:T(8,128)(2,1)} %get-tuple-element.57), channel_id=1, source_target_pairs={{0,8},{8,0},{16,24},{24,16},{32,40},{40,32},{48,56},{56,48},{64,72... | collective-permute-start | bytes 1572872 | tf_op jit(solution)/shard_map/ppermute | solution.py:34
  260.4 25.9 %collective-permute-start.35 = (bf16[8,128,256]{2,1,0:T(8,128)(2,1)S(1)}, bf16[8,128,256]{2,1,0:T(8,128)(2,1)S(1)}, u32[]{:S(2)}, u32[]{:S(2)}) collective-permute-start(bf16[8,128,256]{2,1,0:T(8,128)(2,1)S(1)} %add_convert_fusion.6), channel_id=1, source_target_pairs={{0,32},{8,40},{16,48},{24,56},{32,64},{40,72},{48,80},{56,88},{64,... | collective-permute-start | bytes 1572872 | tf_op jit(solution)/shard_map/ppermute | solution.py:34
  265.6 20.6 %collective-permute-start.45 = (bf16[8,128,256]{2,1,0:T(8,128)(2,1)S(1)}, bf16[8,128,256]{2,1,0:T(8,128)(2,1)}, u32[]{:S(2)}, u32[]{:S(2)}) collective-permute-start(bf16[8,128,256]{2,1,0:T(8,128)(2,1)S(1)} %add_convert_fusion.3), channel_id=1, source_target_pairs={{0,96},{8,104},{16,112},{24,120},{32,0},{40,8},{48,16},{56,24},{64... | collective-permute-start | bytes 1572872 | tf_op jit(solution)/shard_map/ppermute | solution.py:34
  269.2 17.0 %collective-permute-start.49 = (bf16[8,128,256]{2,1,0:T(8,128)(2,1)}, bf16[8,128,256]{2,1,0:T(8,128)(2,1)S(1)}, u32[]{:S(2)}, u32[]{:S(2)}) collective-permute-start(bf16[8,128,256]{2,1,0:T(8,128)(2,1)} %get-tuple-element.77), channel_id=1, source_target_pairs={{0,16},{8,24},{16,0},{24,8},{32,48},{40,56},{48,32},{56,40},{64,80... | collective-permute-start | bytes 1572872 | tf_op jit(solution)/shard_map/ppermute | solution.py:34
  (50 other events, 1050.5 us)

commit v7 on v6

--- a/solution.py
+++ b/solution.py
@@ -62,13 +62,17 @@
     )(*arrays)
 
 
-def gather_tree(own, up, down, pair, tie=False):
-    half = own.shape[0] // 2
+def cuts(tiles):
+    return 3 * tiles // 8, 6 * tiles // 8
+
+
+def gather_tree(own, up, down, pair, tie=None):
+    a, b = cuts(own.shape[0])
     below, above, beside = up(own), down(own), pair(own)
-    if tie:
-        above, beside = together(above, beside)
+    if tie is not None:
+        above, beside, tie = together(above, beside, tie)
     below_beside, above_beside, far = pair(below), down(beside), up(below)
-    far_beside = [(0, down(above_beside[:half])), (half, up(below_beside[half:]))]
+    far_beside = [(0, pair(far[:a])), (a, down(above_beside[a:b])), (b, up(below_beside[b:]))]
     whole = {
         (0, 0): own,
         (-1, 0): below,
@@ -78,18 +82,22 @@
         (1, 1): above_beside,
         (2, 0): far,
     }
-    return [far_beside if place == (2, 1) else [(0, whole[place])] for place in PLACES]
-
-
-def scatter_first(corner, blocks, up, down, *later):
-    low, high = (part.astype(BF16) for part in corner)
-    half = low.shape[0]
-    none = ((0, 0), (0, 0))
-    low, high, *later = together(up(low), down(high), *later)
-    above_beside = blocks[1, 1].astype(F32) + jnp.pad(low.astype(F32), ((0, half), *none))
-    below_beside = blocks[-1, 1].astype(F32) + jnp.pad(high.astype(F32), ((half, 0), *none))
-    leaving = (above_beside.astype(BF16), below_beside.astype(BF16), blocks[2, 0].astype(BF16))
-    return leaving, *later
+    return [far_beside if place == (2, 1) else [(0, whole[place])] for place in PLACES], tie
+
+
+def placed(part, first, tiles):
+    return jnp.pad(part.astype(F32), ((first, tiles - first - part.shape[0]), (0, 0), (0, 0)))
+
+
+def scatter_first(corner, blocks, up, down, pair, *later):
+    low, middle, high = (part.astype(BF16) for part in corner)
+    tiles = blocks[2, 0].shape[0]
+    a, b = cuts(tiles)
+    low, middle, high, *later = together(pair(low), up(middle), down(high), *later)
+    far = blocks[2, 0].astype(F32) + placed(low, 0, tiles)
+    above_beside = blocks[1, 1].astype(F32) + placed(middle, a, tiles)
+    below_beside = blocks[-1, 1].astype(F32) + placed(high, b, tiles)
+    return (above_beside.astype(BF16), below_beside.astype(BF16), far.astype(BF16)), *later
 
 
 def scatter_second(leaving, blocks, up, down, pair):
@@ -198,7 +206,8 @@
 def forward_kernel(layout, order_ref, dest_ref, rows_ref, cols_ref, counts_ref, tiles_ref, *refs):
     parts = sum(len(firsts) for firsts in layout)
     shard_refs, refs = refs[:parts], refs[parts:]
-    out_refs, offset_ref, refs = refs[: len(PLACES) + 1], refs[len(PLACES) + 1], refs[len(PLACES) + 2 :]
+    outs = len(PLACES) + 2
+    out_refs, offset_ref, refs = refs[:outs], refs[outs], refs[outs + 1 :]
     acc_ref, tiles_v, shards_v, *lists, tile_sem, part_sem = refs
     slots, col_tiles = rows_ref.shape[1], shards_v.shape[0] // len(layout)
     row_tiles = acc_ref.shape[0] - 1
@@ -216,9 +225,9 @@
     sums = lax.fori_loop(0, row_tiles, total, jnp.zeros((8, acc_ref.shape[2]), F32))
     offset = jnp.sum(sums, axis=0, keepdims=True) / (row_tiles * acc_ref.shape[1])
     offset_ref[...] = offset
-    half = col_tiles // 2
-    spans = [(out_refs[0], 0, 0, half), (out_refs[1], 0, half, half)]
-    spans += [(out_refs[d + 1], d, 0, col_tiles) for d in range(1, len(PLACES))]
+    a, b = cuts(col_tiles)
+    spans = [(out_refs[0], 0, 0, a), (out_refs[1], 0, a, b - a), (out_refs[2], 0, b, col_tiles - b)]
+    spans += [(out_refs[d + 2], d, 0, col_tiles) for d in range(1, len(PLACES))]
     for out_ref, d, first, size in spans:
         base = dest_ref[d] * col_tiles + first
 
@@ -227,6 +236,11 @@
             return carry
 
         lax.fori_loop(0, size, put, 0)
+
+
+def block_sizes(tiles):
+    a, b = cuts(tiles)
+    return (a, b - a, tiles - b, *(tiles,) * (len(PLACES) - 1))
 
 
 def list_shapes(cap):
@@ -240,7 +254,7 @@
     width = arrays[0].shape[2]
     col_tiles = sum(array.shape[0] for _, array in shards[0])
     row_tiles = col_tiles * len(PLACES)
-    sizes = [col_tiles // 2] * 2 + [col_tiles] * (len(PLACES) - 1)
+    sizes = block_sizes(col_tiles)
     out_shape = [jax.ShapeDtypeStruct((size, tile, width), BF16) for size in sizes]
     out_shape.append(jax.ShapeDtypeStruct((1, width), F32))
     return pl.pallas_call(
@@ -355,20 +369,6 @@
         cost_estimate=pl.CostEstimate(flops=8 * 10**9, bytes_accessed=20 * 2**20, transcendentals=0),
         name="backward_tiles",
     )(order, dests, *scalars, tiles, *arrays, *after)
-
-
-def sum_first_kernel(value_ref, *refs):
-    refs[-1][...] = jnp.sum(value_ref[...], axis=0)
-
-
-def sum_first(value, after):
-    return pl.pallas_call(
-        sum_first_kernel,
-        in_specs=[VMEM] + [ANY] * len(after),
-        out_specs=VMEM,
-        out_shape=jax.ShapeDtypeStruct(value.shape[1:], value.dtype),
-        name="sum_first",
-    )(value, *after)
 
 
 def weight_kernel(aggregate_ref, grad_ref, offset_ref, *refs):
@@ -425,35 +425,30 @@
     *blk_tree, across = blk_links()
     rep_tree = rep_links()
 
-    mine = gather_tree(features.reshape(col_tiles, tile, width), *blk_tree)
+    mine, _ = gather_tree(features.reshape(col_tiles, tile, width), *blk_tree)
     theirs = [[(first, across(array)) for first, array in parts] for parts in mine]
     backwards = slice(None, None, -1)
     scalars = (rows, cols, counts)
     order = jnp.stack([own_core[backwards], other_core[backwards]], axis=1).reshape(-1)
     shards = [parts for both in zip(mine[backwards], theirs[backwards]) for parts in both]
-    up, down, pair = rep_tree
-    low, high, *rest, offset = forward_tiles(order, dests, scalars, tiles, shards)
-    blocks = dict(zip(PLACES[1:], rest))
-    [leaving] = scatter_first((low, high), blocks, up, down)
+    *arrays, offset = forward_tiles(order, dests, scalars, tiles, shards)
+    blocks = dict(zip(PLACES[1:], arrays[3:]))
+    [leaving] = scatter_first(arrays[:3], blocks, *rep_tree)
     leaving = scatter_second(leaving, blocks, *rep_tree)
     shifted = scatter_third(leaving, blocks[0, 0], *rep_tree).reshape(local_rows, width)
     aggregate = shifted.astype(BF16)
     projected = jnp.dot(aggregate, weight, preferred_element_type=F32)
+    group_offset = jnp.sum(copies_of_all(offset[0], "rep"), axis=0)
+    moved = jnp.dot(group_offset[None], weight.astype(F32), precision=lax.Precision.HIGHEST)[0]
     own_mean = jnp.sum(projected, axis=0) / local_rows
     own_square = jnp.sum((projected - own_mean) ** 2, axis=0)
-    everyone = copies_of_all(jnp.stack([own_mean, own_square, offset[0]]), ("blk", "rep"))
-    everyone = everyone.reshape(blk_count, rep_count, 3, width)
-    offsets = jnp.sum(everyone[:, :, 2], axis=1)
-    moves = jnp.dot(offsets, weight.astype(F32), precision=lax.Precision.HIGHEST)
-    means = everyone[:, :, 0] + moves[:, None]
-    feat_mean = jnp.sum(means, axis=(0, 1)) / (blk_count * rep_count)
-    square_sum = jnp.sum(everyone[:, :, 1], axis=(0, 1)) + local_rows * jnp.sum(
-        (means - feat_mean) ** 2, axis=(0, 1)
-    )
-    group_moved = lax.dynamic_index_in_dim(moves, blk, 0, keepdims=False)
-    group_offset = lax.dynamic_index_in_dim(offsets, blk, 0, keepdims=False)
+    everyone = copies_of_all(jnp.stack([own_mean + moved, own_square]), ("blk", "rep"))
+    feat_mean = jnp.sum(everyone[:, 0], axis=0) / (blk_count * rep_count)
+    square_sum = jnp.sum(everyone[:, 1], axis=0) + local_rows * jnp.sum(
+        (everyone[:, 0] - feat_mean) ** 2, axis=0
+    )
     inv_std = lax.rsqrt(square_sum / node_count + norm_eps)
-    normed = (projected + (group_moved - feat_mean)) * inv_std
+    normed = (projected + (moved - feat_mean)) * inv_std
     affine = norm_gain * normed + norm_shift
     gate_value = jax.nn.sigmoid(affine)
     output = (affine * gate_value).astype(BF16)
@@ -474,14 +469,12 @@
     sent = lax.dot_general(
         grad_summed, weight, (((1,), (1,)), ((), ())), preferred_element_type=F32
     ).astype(BF16)
-    grads = gather_tree(sent.reshape(col_tiles, tile, width), *rep_tree, tie=True)
-    arrived = {place: parts[0][1] for place, parts in zip(PLACES, grads)}
-    weight_term = weight_terms(aggregate, grad_summed, group_offset, [arrived[1, 0]])
+    weight_term = weight_terms(aggregate, grad_summed, group_offset, [])
     pieces = lax.all_to_all(weight_term.reshape(blk_count, -1, width), "blk", 0, 0)
-    piece = sum_first(pieces, [arrived[-1, 1]])
-
-    half = col_tiles // 2
-    sizes = (half, half, *(col_tiles,) * (len(PLACES) - 1))
+    grads, pieces = gather_tree(sent.reshape(col_tiles, tile, width), *rep_tree, pieces)
+    piece = jnp.sum(pieces, axis=0)
+
+    sizes = block_sizes(col_tiles)
     arrays = backward_tiles(
         sizes * 2,
         jnp.concatenate([other_core, own_core]),
@@ -489,13 +482,11 @@
         scalars,
         tiles,
         grads,
-        [piece],
     )
     given, kept = arrays[: len(sizes)], arrays[len(sizes) :]
-    low, high, *rest = [b.astype(F32) + across(a).astype(F32) for a, b in zip(given, kept)]
-    products = dict(zip(PLACES[1:], rest))
-    up, down, pair = blk_tree
-    leaving, piece = scatter_first((low, high), products, up, down, piece)
+    arrays = [b.astype(F32) + across(a).astype(F32) for a, b in zip(given, kept)]
+    products = dict(zip(PLACES[1:], arrays[3:]))
+    leaving, piece = scatter_first(arrays[:3], products, *blk_tree, piece)
     terms = copies_of_all(piece, "rep")
     below, beside, above = scatter_second(leaving, products, *blk_tree)
     beside, terms = together(beside, terms)

time: 291 us -> 285 us (0.979)
  blocking collectives: 30.8 us -> 73.2 us
  waiting for transfers between devices: 90.9 us -> 56.6 us
  starting transfers between devices: 86.5 us -> 70.6 us
    all_to_all x2 -> x4, blocking collectives: 30.8 us -> 60.6 us  [copies_of_all(): lax.all_to_all(jnp.broadcast_to(value[None], (count, *value.shape)), axis...]
    all_to_all x2 -> x1, waiting for transfers between devices: 13.9 us -> 0.01 us  [copies_of_all(): lax.all_to_all(jnp.broadcast_to(value[None], (count, *value.shape)), axis...]
    all_to_all x0 -> x1, blocking collectives: none -> 12.6 us  [on_device(): lax.all_to_all(weight_term.reshape(blk_count, -1, width), 'blk', 0, 0)]
    ppermute x16 -> x18, waiting for transfers between devices: 42.6 us -> 30.9 us  [link(): return lambda value: lax.ppermute(value, 'rep', pairs)]
    all_to_all x2 -> x1, starting transfers between devices: 12.9 us -> 5.31 us  [copies_of_all(): lax.all_to_all(jnp.broadcast_to(value[None], (count, *value.shape)), axis...]
    all_to_all x1 -> x0, waiting for transfers between devices: 6.59 us -> none  [on_device(): lax.all_to_all(weight_term.reshape(blk_count, -1, width), 'blk', 0, 0)]
    all_to_all x1 -> x0, starting transfers between devices: 6.33 us -> none  [on_device(): lax.all_to_all(weight_term.reshape(blk_count, -1, width), 'blk', 0, 0)]
    ppermute x16 -> x18, starting transfers between devices: 25.6 us -> 20.9 us  [link(): return lambda value: lax.ppermute(value, 'rep', pairs)]
  transfers between devices with their start and end apart: 53 -> 57, of which waited for: 19 -> 18; matrix products, arithmetic and copies ran while one was open for 8% -> 8% of each run, Pallas kernels for 1% -> 1%
where the time goes in v7:
time: 285 us; the launch traced here: 283 us
  blocking collectives  73.2 us (26%)
  starting transfers between devices  70.6 us (25%)
  waiting for transfers between devices  56.6 us (20%)
  Pallas kernels  44.2 us (16%)
  other arithmetic  25.8 us (9%)
  local copies, waits for them, and re-layouts  10.5 us (4%)
    all_to_all x4, blocking collectives, copies_of_all(): lax.all_to_all(jnp.broadcast_to(value[None], (count, *value.shape)), axis...  60.6 us
    ppermute x38, starting transfers between devices, link(): return lambda value: lax.ppermute(value, 'blk', pairs)  44.4 us
    ppermute x18, waiting for transfers between devices, link(): return lambda value: lax.ppermute(value, 'rep', pairs)  30.9 us
    ppermute x38, waiting for transfers between devices, link(): return lambda value: lax.ppermute(value, 'blk', pairs)  25.8 us
    pallas_call x1, Pallas kernels, backward_tiles(): pl.pallas_call(functools.partial(backward_kernel, layout, sizes, len(afte...  22.1 us
    ppermute x18, starting transfers between devices, link(): return lambda value: lax.ppermute(value, 'rep', pairs)  20.9 us
    pallas_call x1, Pallas kernels, forward_tiles(): pl.pallas_call(functools.partial(forward_kernel, layout), in_specs=[SMEM]...  19.8 us
    all_to_all x1, blocking collectives, on_device(): lax.all_to_all(weight_term.reshape(blk_count, -1, width), 'blk', 0, 0)  12.6 us
  transfers between devices with their start and end apart: 57, of which 18 were waited for; matrix products, arithmetic and copies ran while one was open for 8% of the time, Pallas kernels for 1%

profile of v7, /device:TPU:1, one launch (start us, length us, event | category | flops | bytes accessed | tf_op | source)
XLA Modules:
  0.0 283.1 jit_solution(11697259845963399006)
XLA Ops:
  0.6 2.2 collective-permute-start.5
  4.5 2.1 collective-permute-start.3
  7.8 6.5 %collective-permute-done.5.refs_6_ = bf16[8,128,256]{2,1,0:T(8,128)(2,1)S(1)} collective-permute-done((bf16[8,128,256]{2,1,0:T(8,128)(2,1)}, bf16[8,128,256]{2,1,0:T(8,128)(2,1)S(1)}, u32[]{:S(2)}, u32[]{:S(2)}) %collective-permute-start.5) | collective-permute-done | bytes 524320 | tf_op jit(solution)/shard_map/ppermute | solution.py:34
  14.3 4.0 %collective-permute-start.11 = (bf16[8,128,256]{2,1,0:T(8,128)(2,1)S(1)}, bf16[8,128,256]{2,1,0:T(8,128)(2,1)S(1)}, u32[]{:S(2)}, u32[]{:S(2)}) collective-permute-start(bf16[8,128,256]{2,1,0:T(8,128)(2,1)S(1)} %collective-permute-done.5.refs_6_), channel_id=1, source_target_pairs={{0,96},{8,104},{16,112},{24,120},{32,0},{40,8},{48,16},{56,24},{64... | collective-permute-start | bytes 1572872 | tf_op jit(solution)/shard_map/ppermute | solution.py:34
  19.6 2.2 collective-permute-start.6
  21.9 6.8 %collective-permute-done.11.refs_12_ = bf16[8,128,256]{2,1,0:T(8,128)(2,1)S(1)} collective-permute-done((bf16[8,128,256]{2,1,0:T(8,128)(2,1)S(1)}, bf16[8,128,256]{2,1,0:T(8,128)(2,1)S(1)}, u32[]{:S(2)}, u32[]{:S(2)}) %collective-permute-start.11) | collective-permute-done | bytes 524320 | tf_op jit(solution)/shard_map/ppermute | solution.py:34
  30.5 3.5 %collective-permute-start.14 = (bf16[3,128,256]{2,1,0:T(8,128)(2,1)S(1)}, bf16[3,128,256]{2,1,0:T(8,128)(2,1)S(1)}, u32[]{:S(2)}, u32[]{:S(2)}) collective-permute-start(bf16[3,128,256]{2,1,0:T(8,128)(2,1)S(1)} %slice.34), channel_id=1, source_target_pairs={{0,96},{8,104},{16,112},{24,120},{32,0},{40,8},{48,16},{56,24},{64... | collective-permute-start | bytes 589832 | tf_op jit(solution)/shard_map/ppermute | solution.py:34
  37.2 2.0 collective-permute-done.15.refs_16_
  39.2 2.2 collective-permute-start.8
  45.4 19.8 %forward_tiles.1 = (bf16[3,128,256]{2,1,0:T(8,128)(2,1)}, bf16[3,128,256]{2,1,0:T(8,128)(2,1)}, bf16[2,128,256]{2,1,0:T(8,128)(2,1)}, bf16[8,128,256]{2,1,0:T(8,...) custom-call(s32[16]{0:T(128)} %reshape.64.order_ref, ...), custom_call_target="tpu_custom_call" | custom-call | flops 6000000000 | bytes 31457280 | tf_op jit(solution)/shard_map/forward_tiles/pallas_call | solution.py:260
  69.9 2.5 collective-permute-done.22.refs_2_
  79.4 2.3 collective-permute-start.23
  83.0 5.7 %collective-permute-done.24 = bf16[8,128,256]{2,1,0:T(8,128)(2,1)S(1)} collective-permute-done((bf16[8,128,256]{2,1,0:T(8,128)(2,1)S(1)}, bf16[8,128,256]{2,1,0:T(8,128)(2,1)S(1)}, u32[]{:S(2)}, u32[]{:S(2)}) %collective-permute-start.24) | collective-permute-done | bytes 524320 | tf_op jit(solution)/shard_map/ppermute | solution.py:44
  88.7 4.0 %collective-permute-done.23 = bf16[8,128,256]{2,1,0:T(8,128)(2,1)S(1)} collective-permute-done((bf16[8,128,256]{2,1,0:T(8,128)(2,1)S(1)}, bf16[8,128,256]{2,1,0:T(8,128)(2,1)S(1)}, u32[]{:S(2)}, u32[]{:S(2)}) %collective-permute-start.23) | collective-permute-done | bytes 524320 | tf_op jit(solution)/shard_map/ppermute | solution.py:44
  99.1 9.7 %all_to_all.31 = f32[8,1,256]{2,1,0:T(1,128)S(1)} all-to-all(f32[8,1,256]{2,1,0:T(1,128)S(1)} %broadcast_in_dim.12), channel_id=1, replica_groups=mesh['blk'=16,'rep'=8] {'rep'}, dimensions={0} | all-to-all | bytes 16384 | tf_op jit(solution)/shard_map/all_to_all | solution.py:398
  111.0 20.6 %all_to_all.32 = f32[128,2,256]{2,1,0:T(2,128)S(1)} all-to-all(f32[128,2,256]{2,1,0:T(2,128)S(1)} %broadcast_in_dim.13), channel_id=1, replica_groups=mesh['blk'=16,'rep'=8] {'blk','rep'}, dimensions={0} | all-to-all | bytes 524288 | tf_op jit(solution)/shard_map/all_to_all | solution.py:398
  132.7 15.3 %all_to_all.33 = f32[128,2,256]{2,1,0:T(2,128)S(1)} all-to-all(f32[128,2,256]{2,1,0:T(2,128)S(1)} %broadcast_in_dim.14), channel_id=1, replica_groups=mesh['blk'=16,'rep'=8] {'blk','rep'}, dimensions={0} | all-to-all | bytes 524288 | tf_op jit(solution)/shard_map/all_to_all | solution.py:398
  154.0 2.3 weight_terms.1
  156.3 12.6 %all_to_all.34.refs_2_ = f32[16,16,256]{2,1,0:T(8,128)} all-to-all(f32[16,16,256]{2,1,0:T(8,128)} %bitcast.56), channel_id=1, replica_groups=mesh['blk'=16,'rep'=8] {'blk'}, dimensions={0} | all-to-all | bytes 524288 | tf_op jit(solution)/shard_map/all_to_all | solution.py:473
  174.3 8.8 %collective-permute-done.33.refs_3_ = bf16[8,128,256]{2,1,0:T(8,128)(2,1)S(1)} collective-permute-done((bf16[8,128,256]{2,1,0:T(8,128)(2,1)}, bf16[8,128,256]{2,1,0:T(8,128)(2,1)S(1)}, u32[]{:S(2)}, u32[]{:S(2)}) %collective-permute-start.33) | collective-permute-done | bytes 524320 | tf_op jit(solution)/shard_map/ppermute | solution.py:44
  183.1 3.2 %collective-permute-start.34 = (bf16[3,128,256]{2,1,0:T(8,128)(2,1)S(1)}, bf16[3,128,256]{2,1,0:T(8,128)(2,1)S(1)}, u32[]{:S(2)}, u32[]{:S(2)}) collective-permute-start(bf16[3,128,256]{2,1,0:T(8,128)(2,1)S(1)} %slice.39), channel_id=1, source_target_pairs={{0,3},{4,7},{1,0},{5,4},{2,1},{6,5},{3,2},{7,6},{8,11},{12,15},{9,... | collective-permute-start | bytes 589832 | tf_op jit(solution)/shard_map/ppermute | solution.py:44
  189.4 2.1 collective-permute-done.36.refs_2_
  191.5 2.2 collective-permute-done.30.refs_0_
  194.4 22.1 %backward_tiles.1 = (bf16[3,128,256]{2,1,0:T(8,128)(2,1)}, bf16[3,128,256]{2,1,0:T(8,128)(2,1)}, bf16[2,128,256]{2,1,0:T(8,128)(2,1)}, bf16[8,128,256]{2,1,0:T(8...) custom-call(s32[16]{0:T(128)} %concatenate.4.order_ref, ...), custom_call_target="tpu_custom_call" | custom-call | flops 8000000000 | bytes 20971520 | tf_op jit(solution)/shard_map/backward_tiles/pallas_call | solution.py:355
  216.4 2.2 collective-permute-start.42
  232.0 5.3 %all-to-all-start.4 = ((f32[8,16,256]{2,1,0:T(8,128)}), f32[8,16,256]{2,1,0:T(8,128)S(1)}, u32[]{:S(2)}, u32[]{:S(2)}) async-start(f32[8,16,256]{2,1,0:T(8,128)} %broadcast_in_dim.16), calls=%async_computation.4 | async-start | bytes 262144 | tf_op jit(solution)/shard_map/all_to_all | solution.py:398
  241.6 2.9 %collective-permute-start.50 = (bf16[8,128,256]{2,1,0:T(8,128)(2,1)S(1)}, bf16[8,128,256]{2,1,0:T(8,128)(2,1)S(1)}, u32[]{:S(2)}, u32[]{:S(2)}) collective-permute-start(bf16[8,128,256]{2,1,0:T(8,128)(2,1)S(1)} %add_convert_fusion.4), channel_id=1, source_target_pairs={{0,96},{8,104},{16,112},{24,120},{32,0},{40,8},{48,16},{56,24},{64... | collective-permute-start | bytes 1572872 | tf_op jit(solution)/shard_map/ppermute | solution.py:34
  247.6 6.2 %collective-permute-done.48 = bf16[8,128,256]{2,1,0:T(8,128)(2,1)S(1)} collective-permute-done((bf16[8,128,256]{2,1,0:T(8,128)(2,1)S(1)}, bf16[8,128,256]{2,1,0:T(8,128)(2,1)S(1)}, u32[]{:S(2)}, u32[]{:S(2)}) %collective-permute-start.48) | collective-permute-done | bytes 524320 | tf_op jit(solution)/shard_map/ppermute | solution.py:34
  256.8 3.5 %collective-permute-start.51 = (bf16[8,128,256]{2,1,0:T(8,128)(2,1)S(1)}, bf16[8,128,256]{2,1,0:T(8,128)(2,1)S(1)}, u32[]{:S(2)}, u32[]{:S(2)}) collective-permute-start(bf16[8,128,256]{2,1,0:T(8,128)(2,1)S(1)} %add_convert_fusion.3), channel_id=1, source_target_pairs={{0,96},{8,104},{16,112},{24,120},{32,0},{40,8},{48,16},{56,24},{64... | collective-permute-start | bytes 1572872 | tf_op jit(solution)/shard_map/ppermute | solution.py:34
  260.3 2.2 add_convert_fusion.1.refs_0_
  264.9 14.9 %all_to_all.35 = f32[16,16,256]{2,1,0:T(8,128)S(1)} all-to-all(f32[16,16,256]{2,1,0:T(8,128)S(1)} %broadcast_in_dim.17), channel_id=1, replica_groups=mesh['blk'=16,'rep'=8] {'blk'}, dimensions={0} | all-to-all | bytes 524288 | tf_op jit(solution)/shard_map/all_to_all | solution.py:398
  279.9 2.5 add_convert_fusion
  (218 shorter events, 77.4 us)
Async XLA Ops:
  0.6 13.7 %collective-permute-start.5 = (bf16[8,128,256]{2,1,0:T(8,128)(2,1)}, bf16[8,128,256]{2,1,0:T(8,128)(2,1)S(1)}, u32[]{:S(2)}, u32[]{:S(2)}) collective-permute-start(bf16[8,128,256]{2,1,0:T(8,128)(2,1)} %bitcast.57), channel_id=1, source_target_pairs={{0,16},{8,24},{16,0},{24,8},{32,48},{40,56},{48,32},{56,40},{64,80... | collective-permute-start | bytes 1572872 | tf_op jit(solution)/shard_map/ppermute | solution.py:34
  2.9 15.5 %collective-permute-start.1 = (bf16[8,128,256]{2,1,0:T(8,128)(2,1)}, bf16[8,128,256]{2,1,0:T(8,128)(2,1)S(1)}, u32[]{:S(2)}, u32[]{:S(2)}) collective-permute-start(bf16[8,128,256]{2,1,0:T(8,128)(2,1)} %bitcast.58), channel_id=1, source_target_pairs={{0,32},{8,40},{16,48},{24,56},{32,64},{40,72},{48,80},{56,88},{64,... | collective-permute-start | bytes 1572872 | tf_op jit(solution)/shard_map/ppermute | solution.py:34
  4.5 15.1 %collective-permute-start.3 = (bf16[8,128,256]{2,1,0:T(8,128)(2,1)}, bf16[8,128,256]{2,1,0:T(8,128)(2,1)S(1)}, u32[]{:S(2)}, u32[]{:S(2)}) collective-permute-start(bf16[8,128,256]{2,1,0:T(8,128)(2,1)} %bitcast.59), channel_id=1, source_target_pairs={{0,96},{8,104},{16,112},{24,120},{32,0},{40,8},{48,16},{56,24},{64... | collective-permute-start | bytes 1572872 | tf_op jit(solution)/shard_map/ppermute | solution.py:34
  6.6 15.2 %collective-permute-start = (bf16[8,128,256]{2,1,0:T(8,128)(2,1)}, bf16[8,128,256]{2,1,0:T(8,128)(2,1)S(1)}, u32[]{:S(2)}, u32[]{:S(2)}) collective-permute-start(bf16[8,128,256]{2,1,0:T(8,128)(2,1)} %bitcast.60), channel_id=1, source_target_pairs={{0,8},{8,0},{16,24},{24,16},{32,40},{40,32},{48,56},{56,48},{64,72... | collective-permute-start | bytes 1572872 | tf_op jit(solution)/shard_map/ppermute | solution.py:34
  14.3 14.4 %collective-permute-start.11 = (bf16[8,128,256]{2,1,0:T(8,128)(2,1)S(1)}, bf16[8,128,256]{2,1,0:T(8,128)(2,1)S(1)}, u32[]{:S(2)}, u32[]{:S(2)}) collective-permute-start(bf16[8,128,256]{2,1,0:T(8,128)(2,1)S(1)} %collective-permute-done.5.refs_6_), channel_id=1, source_target_pairs={{0,96},{8,104},{16,112},{24,120},{32,0},{40,8},{48,16},{56,24},{64... | collective-permute-start | bytes 1572872 | tf_op jit(solution)/shard_map/ppermute | solution.py:34
  18.3 12.2 %collective-permute-start.9 = (bf16[8,128,256]{2,1,0:T(8,128)(2,1)S(1)}, bf16[8,128,256]{2,1,0:T(8,128)(2,1)S(1)}, u32[]{:S(2)}, u32[]{:S(2)}) collective-permute-start(bf16[8,128,256]{2,1,0:T(8,128)(2,1)S(1)} %collective-permute-done.1.refs_2_), channel_id=1, source_target_pairs={{0,16},{8,24},{16,0},{24,8},{32,48},{40,56},{48,32},{56,40},{64,80... | collective-permute-start | bytes 1572872 | tf_op jit(solution)/shard_map/ppermute | solution.py:34
  19.6 14.4 %collective-permute-start.7 = (bf16[8,128,256]{2,1,0:T(8,128)(2,1)S(1)}, bf16[8,128,256]{2,1,0:T(8,128)(2,1)S(1)}, u32[]{:S(2)}, u32[]{:S(2)}) collective-permute-start(bf16[8,128,256]{2,1,0:T(8,128)(2,1)S(1)} %collective-permute-done.1.refs_2_), channel_id=1, source_target_pairs={{0,32},{8,40},{16,48},{24,56},{32,64},{40,72},{48,80},{56,88},{64,... | collective-permute-start | bytes 1572872 | tf_op jit(solution)/shard_map/ppermute | solution.py:34
  19.6 15.2 %collective-permute-start.6 = (bf16[8,128,256]{2,1,0:T(8,128)(2,1)S(1)}, bf16[8,128,256]{2,1,0:T(8,128)(2,1)S(1)}, u32[]{:S(2)}, u32[]{:S(2)}) collective-permute-start(bf16[8,128,256]{2,1,0:T(8,128)(2,1)S(1)} %collective-permute-done.5.refs_6_), channel_id=1, source_target_pairs={{0,8},{8,0},{16,24},{24,16},{32,40},{40,32},{48,56},{56,48},{64,72... | collective-permute-start | bytes 1572872 | tf_op jit(solution)/shard_map/ppermute | solution.py:34
  21.8 14.3 %collective-permute-start.4 = (bf16[8,128,256]{2,1,0:T(8,128)(2,1)S(1)}, bf16[8,128,256]{2,1,0:T(8,128)(2,1)S(1)}, u32[]{:S(2)}, u32[]{:S(2)}) collective-permute-start(bf16[8,128,256]{2,1,0:T(8,128)(2,1)S(1)} %collective-permute-done.3.refs_4_), channel_id=1, source_target_pairs={{0,8},{8,0},{16,24},{24,16},{32,40},{40,32},{48,56},{56,48},{64,72... | collective-permute-start | bytes 1572872 | tf_op jit(solution)/shard_map/ppermute | solution.py:34
  79.4 13.2 %collective-permute-start.23 = (bf16[8,128,256]{2,1,0:T(8,128)(2,1)S(1)}, bf16[8,128,256]{2,1,0:T(8,128)(2,1)S(1)}, u32[]{:S(2)}, u32[]{:S(2)}) collective-permute-start(bf16[8,128,256]{2,1,0:T(8,128)(2,1)S(1)} %add_convert_fusion.12), channel_id=1, source_target_pairs={{0,4},{4,0},{1,5},{5,1},{2,6},{6,2},{3,7},{7,3},{8,12},{12,8},{9,1... | collective-permute-start | bytes 1572872 | tf_op jit(solution)/shard_map/ppermute | solution.py:44
  82.8 13.1 %collective-permute-start.26 = (bf16[8,128,256]{2,1,0:T(8,128)(2,1)S(1)}, bf16[8,128,256]{2,1,0:T(8,128)(2,1)S(1)}, u32[]{:S(2)}, u32[]{:S(2)}) collective-permute-start(bf16[8,128,256]{2,1,0:T(8,128)(2,1)S(1)} %add_convert_fusion.9), channel_id=1, source_target_pairs={{0,1},{4,5},{1,2},{5,6},{2,3},{6,7},{3,0},{7,4},{8,9},{12,13},{9,1... | collective-permute-start | bytes 1572872 | tf_op jit(solution)/shard_map/ppermute | solution.py:44
  82.9 26.0 %collective-permute-start.19 = (bf16[8,128,256]{2,1,0:T(8,128)(2,1)}, bf16[8,128,256]{2,1,0:T(8,128)(2,1)S(1)}, u32[]{:S(2)}, u32[]{:S(2)}) collective-permute-start(bf16[8,128,256]{2,1,0:T(8,128)(2,1)} %get-tuple-element.49), channel_id=1, source_target_pairs={{0,1},{4,5},{1,2},{5,6},{2,3},{6,7},{3,0},{7,4},{8,9},{12,13},{9,1... | collective-permute-start | bytes 1572872 | tf_op jit(solution)/shard_map/ppermute | solution.py:44
  93.9 15.1 %collective-permute-start.25 = (bf16[8,128,256]{2,1,0:T(8,128)(2,1)S(1)}, bf16[8,128,256]{2,1,0:T(8,128)(2,1)S(1)}, u32[]{:S(2)}, u32[]{:S(2)}) collective-permute-start(bf16[8,128,256]{2,1,0:T(8,128)(2,1)S(1)} %add_convert_fusion.10), channel_id=1, source_target_pairs={{0,3},{4,7},{1,0},{5,4},{2,1},{6,5},{3,2},{7,6},{8,11},{12,15},{9,... | collective-permute-start | bytes 1572872 | tf_op jit(solution)/shard_map/ppermute | solution.py:44
  150.6 18.2 %collective-permute-start.32 = (bf16[8,128,256]{2,1,0:T(8,128)(2,1)S(1)}, bf16[8,128,256]{2,1,0:T(8,128)(2,1)S(1)}, u32[]{:S(2)}, u32[]{:S(2)}) collective-permute-start(bf16[8,128,256]{2,1,0:T(8,128)(2,1)S(1)} %bitcast.62), channel_id=1, source_target_pairs={{0,4},{4,0},{1,5},{5,1},{2,6},{6,2},{3,7},{7,3},{8,12},{12,8},{9,1... | collective-permute-start | bytes 1572872 | tf_op jit(solution)/shard_map/ppermute | solution.py:44
  151.7 17.2 %collective-permute-start.31 = (bf16[8,128,256]{2,1,0:T(8,128)(2,1)S(1)}, bf16[8,128,256]{2,1,0:T(8,128)(2,1)S(1)}, u32[]{:S(2)}, u32[]{:S(2)}) collective-permute-start(bf16[8,128,256]{2,1,0:T(8,128)(2,1)S(1)} %bitcast.63), channel_id=1, source_target_pairs={{0,3},{4,7},{1,0},{5,4},{2,1},{6,5},{3,2},{7,6},{8,11},{12,15},{9,... | collective-permute-start | bytes 1572872 | tf_op jit(solution)/shard_map/ppermute | solution.py:44
  152.5 19.9 %collective-permute-start.28 = (bf16[8,128,256]{2,1,0:T(8,128)(2,1)S(1)}, bf16[8,128,256]{2,1,0:T(8,128)(2,1)}, u32[]{:S(2)}, u32[]{:S(2)}) collective-permute-start(bf16[8,128,256]{2,1,0:T(8,128)(2,1)S(1)} %bitcast.64), channel_id=1, source_target_pairs={{0,1},{4,5},{1,2},{5,6},{2,3},{6,7},{3,0},{7,4},{8,9},{12,13},{9,1... | collective-permute-start | bytes 1572872 | tf_op jit(solution)/shard_map/ppermute | solution.py:44
  170.4 12.6 %collective-permute-start.33 = (bf16[8,128,256]{2,1,0:T(8,128)(2,1)}, bf16[8,128,256]{2,1,0:T(8,128)(2,1)S(1)}, u32[]{:S(2)}, u32[]{:S(2)}) collective-permute-start(bf16[8,128,256]{2,1,0:T(8,128)(2,1)} %get-tuple-element.62.refs_6_), channel_id=1, source_target_pairs={{0,3},{4,7},{1,0},{5,4},{2,1},{6,5},{3,2},{7,6},{8,11},{12,15},{9,... | collective-permute-start | bytes 1572872 | tf_op jit(solution)/shard_map/ppermute | solution.py:44
  172.3 13.9 %collective-permute-start.35 = (bf16[8,128,256]{2,1,0:T(8,128)(2,1)}, bf16[8,128,256]{2,1,0:T(8,128)(2,1)S(1)}, u32[]{:S(2)}, u32[]{:S(2)}) collective-permute-start(bf16[8,128,256]{2,1,0:T(8,128)(2,1)} %collective-permute-done.28.refs_8_), channel_id=1, source_target_pairs={{0,4},{4,0},{1,5},{5,1},{2,6},{6,2},{3,7},{7,3},{8,12},{12,8},{9,1... | collective-permute-start | bytes 1572872 | tf_op jit(solution)/shard_map/ppermute | solution.py:44
  174.3 13.3 %collective-permute-start.29 = (bf16[8,128,256]{2,1,0:T(8,128)(2,1)}, bf16[8,128,256]{2,1,0:T(8,128)(2,1)S(1)}, u32[]{:S(2)}, u32[]{:S(2)}) collective-permute-start(bf16[8,128,256]{2,1,0:T(8,128)(2,1)} %collective-permute-done.28.refs_8_), channel_id=1, source_target_pairs={{0,1},{4,5},{1,2},{5,6},{2,3},{6,7},{3,0},{7,4},{8,9},{12,13},{9,1... | collective-permute-start | bytes 1572872 | tf_op jit(solution)/shard_map/ppermute | solution.py:44
  219.2 18.2 %collective-permute-start.41 = (bf16[8,128,256]{2,1,0:T(8,128)(2,1)}, bf16[8,128,256]{2,1,0:T(8,128)(2,1)S(1)}, u32[]{:S(2)}, u32[]{:S(2)}) collective-permute-start(bf16[8,128,256]{2,1,0:T(8,128)(2,1)} %get-tuple-element.71), channel_id=1, source_target_pairs={{0,8},{8,0},{16,24},{24,16},{32,40},{40,32},{48,56},{56,48},{64,72... | collective-permute-start | bytes 1572872 | tf_op jit(solution)/shard_map/ppermute | solution.py:34
  219.3 20.3 %collective-permute-start.49 = (bf16[8,128,256]{2,1,0:T(8,128)(2,1)}, bf16[8,128,256]{2,1,0:T(8,128)(2,1)S(1)}, u32[]{:S(2)}, u32[]{:S(2)}) collective-permute-start(bf16[8,128,256]{2,1,0:T(8,128)(2,1)} %get-tuple-element.81), channel_id=1, source_target_pairs={{0,8},{8,0},{16,24},{24,16},{32,40},{40,32},{48,56},{56,48},{64,72... | collective-permute-start | bytes 1572872 | tf_op jit(solution)/shard_map/ppermute | solution.py:34
  228.1 17.6 %collective-permute-start.38 = (bf16[8,128,256]{2,1,0:T(8,128)(2,1)}, bf16[8,128,256]{2,1,0:T(8,128)(2,1)S(1)}, u32[]{:S(2)}, u32[]{:S(2)}) collective-permute-start(bf16[8,128,256]{2,1,0:T(8,128)(2,1)} %get-tuple-element.67), channel_id=1, source_target_pairs={{0,8},{8,0},{16,24},{24,16},{32,40},{40,32},{48,56},{56,48},{64,72... | collective-permute-start | bytes 1572872 | tf_op jit(solution)/shard_map/ppermute | solution.py:34
  229.9 17.1 %collective-permute-start.40 = (bf16[8,128,256]{2,1,0:T(8,128)(2,1)}, bf16[8,128,256]{2,1,0:T(8,128)(2,1)S(1)}, u32[]{:S(2)}, u32[]{:S(2)}) collective-permute-start(bf16[8,128,256]{2,1,0:T(8,128)(2,1)} %get-tuple-element.69), channel_id=1, source_target_pairs={{0,8},{8,0},{16,24},{24,16},{32,40},{40,32},{48,56},{56,48},{64,72... | collective-permute-start | bytes 1572872 | tf_op jit(solution)/shard_map/ppermute | solution.py:34
  230.0 30.3 %collective-permute-start.52 = (bf16[8,128,256]{2,1,0:T(8,128)(2,1)}, bf16[8,128,256]{2,1,0:T(8,128)(2,1)}, u32[]{:S(2)}, u32[]{:S(2)}) collective-permute-start(bf16[8,128,256]{2,1,0:T(8,128)(2,1)} %get-tuple-element.84), channel_id=1, source_target_pairs={{0,8},{8,0},{16,24},{24,16},{32,40},{40,32},{48,56},{56,48},{64,72... | collective-permute-start | bytes 1572872 | tf_op jit(solution)/shard_map/ppermute | solution.py:34
  232.0 30.4 %all-to-all-start.4 = ((f32[8,16,256]{2,1,0:T(8,128)}), f32[8,16,256]{2,1,0:T(8,128)S(1)}, u32[]{:S(2)}, u32[]{:S(2)}) async-start(f32[8,16,256]{2,1,0:T(8,128)} %broadcast_in_dim.16), calls=%async_computation.4 | async-start | bytes 262144 | tf_op jit(solution)/shard_map/all_to_all | solution.py:398
  239.6 14.2 %collective-permute-start.48 = (bf16[8,128,256]{2,1,0:T(8,128)(2,1)S(1)}, bf16[8,128,256]{2,1,0:T(8,128)(2,1)S(1)}, u32[]{:S(2)}, u32[]{:S(2)}) collective-permute-start(bf16[8,128,256]{2,1,0:T(8,128)(2,1)S(1)} %add_convert_fusion.5), channel_id=1, source_target_pairs={{0,16},{8,24},{16,0},{24,8},{32,48},{40,56},{48,32},{56,40},{64,80... | collective-permute-start | bytes 1572872 | tf_op jit(solution)/shard_map/ppermute | solution.py:34
  241.6 13.9 %collective-permute-start.50 = (bf16[8,128,256]{2,1,0:T(8,128)(2,1)S(1)}, bf16[8,128,256]{2,1,0:T(8,128)(2,1)S(1)}, u32[]{:S(2)}, u32[]{:S(2)}) collective-permute-start(bf16[8,128,256]{2,1,0:T(8,128)(2,1)S(1)} %add_convert_fusion.4), channel_id=1, source_target_pairs={{0,96},{8,104},{16,112},{24,120},{32,0},{40,8},{48,16},{56,24},{64... | collective-permute-start | bytes 1572872 | tf_op jit(solution)/shard_map/ppermute | solution.py:34
  245.7 14.6 %collective-permute-start.54 = (bf16[8,128,256]{2,1,0:T(8,128)(2,1)S(1)}, bf16[8,128,256]{2,1,0:T(8,128)(2,1)S(1)}, u32[]{:S(2)}, u32[]{:S(2)}) collective-permute-start(bf16[8,128,256]{2,1,0:T(8,128)(2,1)S(1)} %add_convert_fusion.2), channel_id=1, source_target_pairs={{0,32},{8,40},{16,48},{24,56},{32,64},{40,72},{48,80},{56,88},{64,... | collective-permute-start | bytes 1572872 | tf_op jit(solution)/shard_map/ppermute | solution.py:34
  247.0 32.9 %collective-permute-start.37 = (bf16[8,128,256]{2,1,0:T(8,128)(2,1)}, bf16[8,128,256]{2,1,0:T(8,128)(2,1)}, u32[]{:S(2)}, u32[]{:S(2)}) collective-permute-start(bf16[8,128,256]{2,1,0:T(8,128)(2,1)} %get-tuple-element.65), channel_id=1, source_target_pairs={{0,8},{8,0},{16,24},{24,16},{32,40},{40,32},{48,56},{56,48},{64,72... | collective-permute-start | bytes 1572872 | tf_op jit(solution)/shard_map/ppermute | solution.py:34
  253.8 26.0 %collective-permute-start.39 = (bf16[8,128,256]{2,1,0:T(8,128)(2,1)S(1)}, bf16[8,128,256]{2,1,0:T(8,128)(2,1)}, u32[]{:S(2)}, u32[]{:S(2)}) collective-permute-start(bf16[8,128,256]{2,1,0:T(8,128)(2,1)S(1)} %add_convert_fusion.6), channel_id=1, source_target_pairs={{0,32},{8,40},{16,48},{24,56},{32,64},{40,72},{48,80},{56,88},{64,... | collective-permute-start | bytes 1572872 | tf_op jit(solution)/shard_map/ppermute | solution.py:34
  256.8 23.1 %collective-permute-start.51 = (bf16[8,128,256]{2,1,0:T(8,128)(2,1)S(1)}, bf16[8,128,256]{2,1,0:T(8,128)(2,1)S(1)}, u32[]{:S(2)}, u32[]{:S(2)}) collective-permute-start(bf16[8,128,256]{2,1,0:T(8,128)(2,1)S(1)} %add_convert_fusion.3), channel_id=1, source_target_pairs={{0,96},{8,104},{16,112},{24,120},{32,0},{40,8},{48,16},{56,24},{64... | collective-permute-start | bytes 1572872 | tf_op jit(solution)/shard_map/ppermute | solution.py:34
  263.1 16.7 %collective-permute-start.55 = (bf16[8,128,256]{2,1,0:T(8,128)(2,1)}, bf16[8,128,256]{2,1,0:T(8,128)(2,1)S(1)}, u32[]{:S(2)}, u32[]{:S(2)}) collective-permute-start(bf16[8,128,256]{2,1,0:T(8,128)(2,1)} %get-tuple-element.89), channel_id=1, source_target_pairs={{0,16},{8,24},{16,0},{24,8},{32,48},{40,56},{48,32},{56,40},{64,80... | collective-permute-start | bytes 1572872 | tf_op jit(solution)/shard_map/ppermute | solution.py:34
  (59 other events, 928.6 us)

commit v8 on v7

--- a/solution.py
+++ b/solution.py
@@ -66,12 +66,14 @@
     return 3 * tiles // 8, 6 * tiles // 8
 
 
-def gather_tree(own, up, down, pair, tie=None):
+def gather_tree(own, up, down, pair, first=None, second=None):
     a, b = cuts(own.shape[0])
     below, above, beside = up(own), down(own), pair(own)
-    if tie is not None:
-        above, beside, tie = together(above, beside, tie)
+    if second:
+        above, beside, first = together(above, beside, first)
     below_beside, above_beside, far = pair(below), down(beside), up(below)
+    if second:
+        above_beside, first = together(above_beside, second(first))
     far_beside = [(0, pair(far[:a])), (a, down(above_beside[a:b])), (b, up(below_beside[b:]))]
     whole = {
         (0, 0): own,
@@ -82,7 +84,7 @@
         (1, 1): above_beside,
         (2, 0): far,
     }
-    return [far_beside if place == (2, 1) else [(0, whole[place])] for place in PLACES], tie
+    return [far_beside if place == (2, 1) else [(0, whole[place])] for place in PLACES], first
 
 
 def placed(part, first, tiles):
@@ -471,8 +473,12 @@
     ).astype(BF16)
     weight_term = weight_terms(aggregate, grad_summed, group_offset, [])
     pieces = lax.all_to_all(weight_term.reshape(blk_count, -1, width), "blk", 0, 0)
-    grads, pieces = gather_tree(sent.reshape(col_tiles, tile, width), *rep_tree, pieces)
-    piece = jnp.sum(pieces, axis=0)
+    grads, terms = gather_tree(
+        sent.reshape(col_tiles, tile, width),
+        *rep_tree,
+        pieces,
+        lambda pieces: copies_of_all(jnp.sum(pieces, axis=0), "rep"),
+    )
 
     sizes = block_sizes(col_tiles)
     arrays = backward_tiles(
@@ -486,11 +492,9 @@
     given, kept = arrays[: len(sizes)], arrays[len(sizes) :]
     arrays = [b.astype(F32) + across(a).astype(F32) for a, b in zip(given, kept)]
     products = dict(zip(PLACES[1:], arrays[3:]))
-    leaving, piece = scatter_first(arrays[:3], products, *blk_tree, piece)
-    terms = copies_of_all(piece, "rep")
-    below, beside, above = scatter_second(leaving, products, *blk_tree)
-    beside, terms = together(beside, terms)
-    grad_x = scatter_third((below, beside, above), products[0, 0], *blk_tree).astype(BF16)
+    [leaving] = scatter_first(arrays[:3], products, *blk_tree)
+    leaving = scatter_second(leaving, products, *blk_tree)
+    grad_x = scatter_third(leaving, products[0, 0], *blk_tree).astype(BF16)
     grad_w = copies_of_all(jnp.sum(terms, axis=0), "blk").reshape(weight.shape)
     return (output, grad_x.reshape(local_rows, width), grad_w, grad_gamma, grad_beta)
 

time: 285 us -> 281 us (0.986)
  starting transfers between devices: 70.6 us -> 81.6 us
  blocking collectives: 73.2 us -> 65.3 us
  Pallas kernels: 44.2 us -> 40 us
    ppermute x18, waiting for transfers between devices: 30.9 us -> 15.9 us  [link(): return lambda value: lax.ppermute(value, 'rep', pairs)]
    all_to_all x1 -> x0, blocking collectives: 12.6 us -> none  [on_device(): lax.all_to_all(weight_term.reshape(blk_count, -1, width), 'blk', 0, 0)]
    ppermute x18, starting transfers between devices: 20.9 us -> 27.5 us  [link(): return lambda value: lax.ppermute(value, 'rep', pairs)]
    all_to_all x0 -> x1, waiting for transfers between devices: none -> 5.31 us  [on_device(): lax.all_to_all(weight_term.reshape(blk_count, -1, width), 'blk', 0, 0)]
    all_to_all x1, waiting for transfers between devices: 0.01 us -> 5.24 us  [copies_of_all(): lax.all_to_all(jnp.broadcast_to(value[None], (count, *value.shape)), axis...]
    all_to_all x4, blocking collectives: 60.6 us -> 65.3 us  [copies_of_all(): lax.all_to_all(jnp.broadcast_to(value[None], (count, *value.shape)), axis...]
    all_to_all x0 -> x1, starting transfers between devices: none -> 4.65 us  [on_device(): lax.all_to_all(weight_term.reshape(blk_count, -1, width), 'blk', 0, 0)]
    unnamed x69 -> x75, local copies, waits for them, and re-layouts: 4.42 us -> 6.12 us
  transfers between devices with their start and end apart: 57 -> 58, of which waited for: 18 -> 18; matrix products, arithmetic and copies ran while one was open for 8% -> 8% of each run, Pallas kernels for 1% -> 1%
where the time goes in v8:
time: 281 us
  starting transfers between devices  81.6 us (29%)
  blocking collectives  65.3 us (23%)
  waiting for transfers between devices  54.3 us (19%)
  Pallas kernels  40 us (14%)
  other arithmetic  25.4 us (9%)
  local copies, waits for them, and re-layouts  12.3 us (4%)
    all_to_all x4, blocking collectives, copies_of_all(): lax.all_to_all(jnp.broadcast_to(value[None], (count, *value.shape)), axis...  65.3 us
    ppermute x38, starting transfers between devices, link(): return lambda value: lax.ppermute(value, 'blk', pairs)  46.2 us
    ppermute x38, waiting for transfers between devices, link(): return lambda value: lax.ppermute(value, 'blk', pairs)  27.8 us
    ppermute x18, starting transfers between devices, link(): return lambda value: lax.ppermute(value, 'rep', pairs)  27.5 us
    pallas_call x1, Pallas kernels, backward_tiles(): pl.pallas_call(functools.partial(backward_kernel, layout, sizes, len(afte...  20 us
    pallas_call x1, Pallas kernels, forward_tiles(): pl.pallas_call(functools.partial(forward_kernel, layout), in_specs=[SMEM]...  17.7 us
    ppermute x18, waiting for transfers between devices, link(): return lambda value: lax.ppermute(value, 'rep', pairs)  15.9 us
    convert_element_type x5, other arithmetic, scatter_second(): return (below.astype(BF16), beside.astype(BF16), blocks[1, 0].astype(BF16))  7.08 us
  transfers between devices with their start and end apart: 58, of which 18 were waited for; matrix products, arithmetic and copies ran while one was open for 8% of the time, Pallas kernels for 1%

profile of v8, /device:TPU:1, one launch (start us, length us, event | category | flops | bytes accessed | tf_op | source)
XLA Modules:
  0.0 281.1 jit_solution(14083302182582701370)
XLA Ops:
  0.6 2.5 collective-permute-start.1
  7.6 9.5 %collective-permute-done.1.refs_2_ = bf16[8,128,256]{2,1,0:T(8,128)(2,1)S(1)} collective-permute-done((bf16[8,128,256]{2,1,0:T(8,128)(2,1)}, bf16[8,128,256]{2,1,0:T(8,128)(2,1)S(1)}, u32[]{:S(2)}, u32[]{:S(2)}) %collective-permute-start.1) | collective-permute-done | bytes 524320 | tf_op jit(solution)/shard_map/ppermute | solution.py:34
  18.5 2.7 collective-permute-start.11
  23.3 7.2 %collective-permute-done.7.refs_8_ = bf16[8,128,256]{2,1,0:T(8,128)(2,1)S(1)} collective-permute-done((bf16[8,128,256]{2,1,0:T(8,128)(2,1)S(1)}, bf16[8,128,256]{2,1,0:T(8,128)(2,1)S(1)}, u32[]{:S(2)}, u32[]{:S(2)}) %collective-permute-start.7) | collective-permute-done | bytes 524320 | tf_op jit(solution)/shard_map/ppermute | solution.py:34
  35.0 2.6 collective-permute-start.14
  46.2 17.7 %forward_tiles.1 = (bf16[3,128,256]{2,1,0:T(8,128)(2,1)}, bf16[3,128,256]{2,1,0:T(8,128)(2,1)}, bf16[2,128,256]{2,1,0:T(8,128)(2,1)}, bf16[8,128,256]{2,1,0:T(8,...) custom-call(s32[16]{0:T(128)} %reshape.64.order_ref, ...), custom_call_target="tpu_custom_call" | custom-call | flops 6000000000 | bytes 31457280 | tf_op jit(solution)/shard_map/forward_tiles/pallas_call | solution.py:262
  63.9 2.7 collective-permute-start.20
  69.8 2.6 collective-permute-done.22.refs_2_
  80.3 2.3 collective-permute-start.23
  83.0 4.4 %collective-permute-done.26 = bf16[8,128,256]{2,1,0:T(8,128)(2,1)S(1)} collective-permute-done((bf16[8,128,256]{2,1,0:T(8,128)(2,1)S(1)}, bf16[8,128,256]{2,1,0:T(8,128)(2,1)S(1)}, u32[]{:S(2)}, u32[]{:S(2)}) %collective-permute-start.26) | collective-permute-done | bytes 524320 | tf_op jit(solution)/shard_map/ppermute | solution.py:44
  88.6 2.9 %collective-permute-start.27 = (bf16[8,128,256]{2,1,0:T(8,128)(2,1)S(1)}, bf16[8,128,256]{2,1,0:T(8,128)(2,1)S(1)}, u32[]{:S(2)}, u32[]{:S(2)}) collective-permute-start(bf16[8,128,256]{2,1,0:T(8,128)(2,1)S(1)} %add_convert_fusion.8), channel_id=1, source_target_pairs={{0,4},{4,0},{1,5},{5,1},{2,6},{6,2},{3,7},{7,3},{8,12},{12,8},{9,1... | collective-permute-start | bytes 1572872 | tf_op jit(solution)/shard_map/ppermute | solution.py:44
  95.6 12.5 %all_to_all.31 = f32[8,1,256]{2,1,0:T(1,128)S(1)} all-to-all(f32[8,1,256]{2,1,0:T(1,128)S(1)} %broadcast_in_dim.12), channel_id=1, replica_groups=mesh['blk'=16,'rep'=8] {'rep'}, dimensions={0} | all-to-all | bytes 16384 | tf_op jit(solution)/shard_map/all_to_all | solution.py:400
  110.3 23.7 %all_to_all.32 = f32[128,2,256]{2,1,0:T(2,128)S(1)} all-to-all(f32[128,2,256]{2,1,0:T(2,128)S(1)} %broadcast_in_dim.13), channel_id=1, replica_groups=mesh['blk'=16,'rep'=8] {'blk','rep'}, dimensions={0} | all-to-all | bytes 524288 | tf_op jit(solution)/shard_map/all_to_all | solution.py:400
  135.1 15.3 %all_to_all.33 = f32[128,2,256]{2,1,0:T(2,128)S(1)} all-to-all(f32[128,2,256]{2,1,0:T(2,128)S(1)} %broadcast_in_dim.14), channel_id=1, replica_groups=mesh['blk'=16,'rep'=8] {'blk','rep'}, dimensions={0} | all-to-all | bytes 524288 | tf_op jit(solution)/shard_map/all_to_all | solution.py:400
  153.4 2.4 collective-permute-start.31
  159.9 4.6 %all-to-all-start.3 = ((f32[16,16,256]{2,1,0:T(8,128)}), f32[16,16,256]{2,1,0:T(8,128)S(1)}, u32[]{:S(2)}, u32[]{:S(2)}) async-start(f32[16,16,256]{2,1,0:T(8,128)} %bitcast.56), calls=%async_computation.3 | async-start | bytes 524288 | tf_op jit(solution)/shard_map/all_to_all | solution.py:475
  164.6 2.7 collective-permute-done.28.refs_8_
  167.2 5.3 %all-to-all-done.3.refs_2_ = f32[16,16,256]{2,1,0:T(8,128)S(1)} async-done(((f32[16,16,256]{2,1,0:T(8,128)}), f32[16,16,256]{2,1,0:T(8,128)S(1)}, u32[]{:S(2)}, u32[]{:S(2)}) %all-to-all-start.3) | async-done | bytes 262176 | tf_op jit(solution)/shard_map/all_to_all | solution.py:475
  174.2 2.3 collective-permute-start.35
  178.2 3.4 %all-to-all-start.4 = ((f32[8,16,256]{2,1,0:T(8,128)}), f32[8,16,256]{2,1,0:T(8,128)S(1)}, u32[]{:S(2)}, u32[]{:S(2)}) async-start(f32[8,16,256]{2,1,0:T(8,128)} %broadcast_in_dim.16), calls=%async_computation.4 | async-start | bytes 262144 | tf_op jit(solution)/shard_map/all_to_all | solution.py:400
  181.6 3.0 %collective-permute-start.30 = (bf16[3,128,256]{2,1,0:T(8,128)(2,1)S(1)}, bf16[3,128,256]{2,1,0:T(8,128)(2,1)S(1)}, u32[]{:S(2)}, u32[]{:S(2)}) collective-permute-start(bf16[3,128,256]{2,1,0:T(8,128)(2,1)S(1)} %slice.38), channel_id=1, source_target_pairs={{0,4},{4,0},{1,5},{5,1},{2,6},{6,2},{3,7},{7,3},{8,12},{12,8},{9,1... | collective-permute-start | bytes 589832 | tf_op jit(solution)/shard_map/ppermute | solution.py:44
  184.6 5.2 %all-to-all-done.4.refs_1_ = f32[8,16,256]{2,1,0:T(8,128)S(1)} async-done(((f32[8,16,256]{2,1,0:T(8,128)}), f32[8,16,256]{2,1,0:T(8,128)S(1)}, u32[]{:S(2)}, u32[]{:S(2)}) %all-to-all-start.4) | async-done | bytes 131104 | tf_op jit(solution)/shard_map/all_to_all | solution.py:400
  192.2 2.5 collective-permute-start.34
  195.5 4.4 %collective-permute-done.36.refs_2_ = bf16[2,128,256]{2,1,0:T(8,128)(2,1)S(1)} collective-permute-done((bf16[2,128,256]{2,1,0:T(8,128)(2,1)S(1)}, bf16[2,128,256]{2,1,0:T(8,128)(2,1)S(1)}, u32[]{:S(2)}, u32[]{:S(2)}) %collective-permute-start.36) | collective-permute-done | bytes 131104 | tf_op jit(solution)/shard_map/ppermute | solution.py:44
  200.6 20.0 %backward_tiles.1 = (bf16[3,128,256]{2,1,0:T(8,128)(2,1)}, bf16[3,128,256]{2,1,0:T(8,128)(2,1)}, bf16[2,128,256]{2,1,0:T(8,128)(2,1)}, bf16[8,128,256]{2,1,0:T(8...) custom-call(s32[16]{0:T(128)} %concatenate.4.order_ref, ...), custom_call_target="tpu_custom_call" | custom-call | flops 8000000000 | bytes 20971520 | tf_op jit(solution)/shard_map/backward_tiles/pallas_call | solution.py:357
  220.6 6.8 %collective-permute-start.42 = (bf16[3,128,256]{2,1,0:T(8,128)(2,1)}, bf16[3,128,256]{2,1,0:T(8,128)(2,1)S(1)}, u32[]{:S(2)}, u32[]{:S(2)}) collective-permute-start(bf16[3,128,256]{2,1,0:T(8,128)(2,1)} %get-tuple-element.74), channel_id=1, source_target_pairs={{0,8},{8,0},{16,24},{24,16},{32,40},{40,32},{48,56},{56,48},{64,72... | collective-permute-start | bytes 589832 | tf_op jit(solution)/shard_map/ppermute | solution.py:34
  231.8 2.7 collective-permute-start.47
  242.7 2.9 %collective-permute-start.50 = (bf16[8,128,256]{2,1,0:T(8,128)(2,1)S(1)}, bf16[8,128,256]{2,1,0:T(8,128)(2,1)S(1)}, u32[]{:S(2)}, u32[]{:S(2)}) collective-permute-start(bf16[8,128,256]{2,1,0:T(8,128)(2,1)S(1)} %add_convert_fusion.4), channel_id=1, source_target_pairs={{0,96},{8,104},{16,112},{24,120},{32,0},{40,8},{48,16},{56,24},{64... | collective-permute-start | bytes 1572872 | tf_op jit(solution)/shard_map/ppermute | solution.py:34
  250.4 6.0 %collective-permute-done.54 = bf16[8,128,256]{2,1,0:T(8,128)(2,1)S(1)} collective-permute-done((bf16[8,128,256]{2,1,0:T(8,128)(2,1)S(1)}, bf16[8,128,256]{2,1,0:T(8,128)(2,1)S(1)}, u32[]{:S(2)}, u32[]{:S(2)}) %collective-permute-start.54) | collective-permute-done | bytes 524320 | tf_op jit(solution)/shard_map/ppermute | solution.py:34
  261.4 2.6 collective-permute-start.51
  264.1 13.8 %all_to_all.34 = f32[16,16,256]{2,1,0:T(8,128)S(1)} all-to-all(f32[16,16,256]{2,1,0:T(8,128)S(1)} %broadcast_in_dim.17), channel_id=1, replica_groups=mesh['blk'=16,'rep'=8] {'blk'}, dimensions={0} | all-to-all | bytes 524288 | tf_op jit(solution)/shard_map/all_to_all | solution.py:400
  277.9 2.5 add_convert_fusion
  (225 shorter events, 78.0 us)
Async XLA Ops:
  0.6 16.5 %collective-permute-start.1 = (bf16[8,128,256]{2,1,0:T(8,128)(2,1)}, bf16[8,128,256]{2,1,0:T(8,128)(2,1)S(1)}, u32[]{:S(2)}, u32[]{:S(2)}) collective-permute-start(bf16[8,128,256]{2,1,0:T(8,128)(2,1)} %bitcast.57), channel_id=1, source_target_pairs={{0,32},{8,40},{16,48},{24,56},{32,64},{40,72},{48,80},{56,88},{64,... | collective-permute-start | bytes 1572872 | tf_op jit(solution)/shard_map/ppermute | solution.py:34
  3.2 15.3 %collective-permute-start.5 = (bf16[8,128,256]{2,1,0:T(8,128)(2,1)}, bf16[8,128,256]{2,1,0:T(8,128)(2,1)S(1)}, u32[]{:S(2)}, u32[]{:S(2)}) collective-permute-start(bf16[8,128,256]{2,1,0:T(8,128)(2,1)} %bitcast.58), channel_id=1, source_target_pairs={{0,16},{8,24},{16,0},{24,8},{32,48},{40,56},{48,32},{56,40},{64,80... | collective-permute-start | bytes 1572872 | tf_op jit(solution)/shard_map/ppermute | solution.py:34
  4.5 16.7 %collective-permute-start = (bf16[8,128,256]{2,1,0:T(8,128)(2,1)}, bf16[8,128,256]{2,1,0:T(8,128)(2,1)S(1)}, u32[]{:S(2)}, u32[]{:S(2)}) collective-permute-start(bf16[8,128,256]{2,1,0:T(8,128)(2,1)} %bitcast.59), channel_id=1, source_target_pairs={{0,8},{8,0},{16,24},{24,16},{32,40},{40,32},{48,56},{56,48},{64,72... | collective-permute-start | bytes 1572872 | tf_op jit(solution)/shard_map/ppermute | solution.py:34
  5.7 17.5 %collective-permute-start.3 = (bf16[8,128,256]{2,1,0:T(8,128)(2,1)}, bf16[8,128,256]{2,1,0:T(8,128)(2,1)S(1)}, u32[]{:S(2)}, u32[]{:S(2)}) collective-permute-start(bf16[8,128,256]{2,1,0:T(8,128)(2,1)} %bitcast.60), channel_id=1, source_target_pairs={{0,96},{8,104},{16,112},{24,120},{32,0},{40,8},{48,16},{56,24},{64... | collective-permute-start | bytes 1572872 | tf_op jit(solution)/shard_map/ppermute | solution.py:34
  17.2 13.4 %collective-permute-start.7 = (bf16[8,128,256]{2,1,0:T(8,128)(2,1)S(1)}, bf16[8,128,256]{2,1,0:T(8,128)(2,1)S(1)}, u32[]{:S(2)}, u32[]{:S(2)}) collective-permute-start(bf16[8,128,256]{2,1,0:T(8,128)(2,1)S(1)} %collective-permute-done.1.refs_2_), channel_id=1, source_target_pairs={{0,32},{8,40},{16,48},{24,56},{32,64},{40,72},{48,80},{56,88},{64,... | collective-permute-start | bytes 1572872 | tf_op jit(solution)/shard_map/ppermute | solution.py:34
  17.2 15.6 %collective-permute-start.9 = (bf16[8,128,256]{2,1,0:T(8,128)(2,1)S(1)}, bf16[8,128,256]{2,1,0:T(8,128)(2,1)S(1)}, u32[]{:S(2)}, u32[]{:S(2)}) collective-permute-start(bf16[8,128,256]{2,1,0:T(8,128)(2,1)S(1)} %collective-permute-done.1.refs_2_), channel_id=1, source_target_pairs={{0,16},{8,24},{16,0},{24,8},{32,48},{40,56},{48,32},{56,40},{64,80... | collective-permute-start | bytes 1572872 | tf_op jit(solution)/shard_map/ppermute | solution.py:34
  18.5 15.7 %collective-permute-start.11 = (bf16[8,128,256]{2,1,0:T(8,128)(2,1)S(1)}, bf16[8,128,256]{2,1,0:T(8,128)(2,1)S(1)}, u32[]{:S(2)}, u32[]{:S(2)}) collective-permute-start(bf16[8,128,256]{2,1,0:T(8,128)(2,1)S(1)} %collective-permute-done.5.refs_6_), channel_id=1, source_target_pairs={{0,96},{8,104},{16,112},{24,120},{32,0},{40,8},{48,16},{56,24},{64... | collective-permute-start | bytes 1572872 | tf_op jit(solution)/shard_map/ppermute | solution.py:34
  21.2 13.9 %collective-permute-start.2 = (bf16[8,128,256]{2,1,0:T(8,128)(2,1)S(1)}, bf16[8,128,256]{2,1,0:T(8,128)(2,1)S(1)}, u32[]{:S(2)}, u32[]{:S(2)}) collective-permute-start(bf16[8,128,256]{2,1,0:T(8,128)(2,1)S(1)} %collective-permute-done.1.refs_2_), channel_id=1, source_target_pairs={{0,8},{8,0},{16,24},{24,16},{32,40},{40,32},{48,56},{56,48},{64,72... | collective-permute-start | bytes 1572872 | tf_op jit(solution)/shard_map/ppermute | solution.py:34
  23.2 14.4 %collective-permute-start.4 = (bf16[8,128,256]{2,1,0:T(8,128)(2,1)S(1)}, bf16[8,128,256]{2,1,0:T(8,128)(2,1)S(1)}, u32[]{:S(2)}, u32[]{:S(2)}) collective-permute-start(bf16[8,128,256]{2,1,0:T(8,128)(2,1)S(1)} %collective-permute-done.3.refs_4_), channel_id=1, source_target_pairs={{0,8},{8,0},{16,24},{24,16},{32,40},{40,32},{48,56},{56,48},{64,72... | collective-permute-start | bytes 1572872 | tf_op jit(solution)/shard_map/ppermute | solution.py:34
  75.2 12.2 %collective-permute-start.26 = (bf16[8,128,256]{2,1,0:T(8,128)(2,1)S(1)}, bf16[8,128,256]{2,1,0:T(8,128)(2,1)S(1)}, u32[]{:S(2)}, u32[]{:S(2)}) collective-permute-start(bf16[8,128,256]{2,1,0:T(8,128)(2,1)S(1)} %add_convert_fusion.9), channel_id=1, source_target_pairs={{0,1},{4,5},{1,2},{5,6},{2,3},{6,7},{3,0},{7,4},{8,9},{12,13},{9,1... | collective-permute-start | bytes 1572872 | tf_op jit(solution)/shard_map/ppermute | solution.py:44
  78.2 13.3 %collective-permute-start.24 = (bf16[8,128,256]{2,1,0:T(8,128)(2,1)S(1)}, bf16[8,128,256]{2,1,0:T(8,128)(2,1)S(1)}, u32[]{:S(2)}, u32[]{:S(2)}) collective-permute-start(bf16[8,128,256]{2,1,0:T(8,128)(2,1)S(1)} %add_convert_fusion.11), channel_id=1, source_target_pairs={{0,3},{4,7},{1,0},{5,4},{2,1},{6,5},{3,2},{7,6},{8,11},{12,15},{9,... | collective-permute-start | bytes 1572872 | tf_op jit(solution)/shard_map/ppermute | solution.py:44
  82.6 25.7 %collective-permute-start.19 = (bf16[8,128,256]{2,1,0:T(8,128)(2,1)}, bf16[8,128,256]{2,1,0:T(8,128)(2,1)S(1)}, u32[]{:S(2)}, u32[]{:S(2)}) collective-permute-start(bf16[8,128,256]{2,1,0:T(8,128)(2,1)} %get-tuple-element.48), channel_id=1, source_target_pairs={{0,1},{4,5},{1,2},{5,6},{2,3},{6,7},{3,0},{7,4},{8,9},{12,13},{9,1... | collective-permute-start | bytes 1572872 | tf_op jit(solution)/shard_map/ppermute | solution.py:44
  88.6 19.7 %collective-permute-start.27 = (bf16[8,128,256]{2,1,0:T(8,128)(2,1)S(1)}, bf16[8,128,256]{2,1,0:T(8,128)(2,1)S(1)}, u32[]{:S(2)}, u32[]{:S(2)}) collective-permute-start(bf16[8,128,256]{2,1,0:T(8,128)(2,1)S(1)} %add_convert_fusion.8), channel_id=1, source_target_pairs={{0,4},{4,0},{1,5},{5,1},{2,6},{6,2},{3,7},{7,3},{8,12},{12,8},{9,1... | collective-permute-start | bytes 1572872 | tf_op jit(solution)/shard_map/ppermute | solution.py:44
  93.5 14.9 %collective-permute-start.25 = (bf16[8,128,256]{2,1,0:T(8,128)(2,1)S(1)}, bf16[8,128,256]{2,1,0:T(8,128)(2,1)S(1)}, u32[]{:S(2)}, u32[]{:S(2)}) collective-permute-start(bf16[8,128,256]{2,1,0:T(8,128)(2,1)S(1)} %add_convert_fusion.10), channel_id=1, source_target_pairs={{0,3},{4,7},{1,0},{5,4},{2,1},{6,5},{3,2},{7,6},{8,11},{12,15},{9,... | collective-permute-start | bytes 1572872 | tf_op jit(solution)/shard_map/ppermute | solution.py:44
  153.0 14.2 %collective-permute-start.28 = (bf16[8,128,256]{2,1,0:T(8,128)(2,1)S(1)}, bf16[8,128,256]{2,1,0:T(8,128)(2,1)}, u32[]{:S(2)}, u32[]{:S(2)}) collective-permute-start(bf16[8,128,256]{2,1,0:T(8,128)(2,1)S(1)} %bitcast.62), channel_id=1, source_target_pairs={{0,1},{4,5},{1,2},{5,6},{2,3},{6,7},{3,0},{7,4},{8,9},{12,13},{9,1... | collective-permute-start | bytes 1572872 | tf_op jit(solution)/shard_map/ppermute | solution.py:44
  153.4 19.2 %collective-permute-start.31 = (bf16[8,128,256]{2,1,0:T(8,128)(2,1)S(1)}, bf16[8,128,256]{2,1,0:T(8,128)(2,1)S(1)}, u32[]{:S(2)}, u32[]{:S(2)}) collective-permute-start(bf16[8,128,256]{2,1,0:T(8,128)(2,1)S(1)} %bitcast.63), channel_id=1, source_target_pairs={{0,3},{4,7},{1,0},{5,4},{2,1},{6,5},{3,2},{7,6},{8,11},{12,15},{9,... | collective-permute-start | bytes 1572872 | tf_op jit(solution)/shard_map/ppermute | solution.py:44
  155.8 16.8 %collective-permute-start.32 = (bf16[8,128,256]{2,1,0:T(8,128)(2,1)S(1)}, bf16[8,128,256]{2,1,0:T(8,128)(2,1)S(1)}, u32[]{:S(2)}, u32[]{:S(2)}) collective-permute-start(bf16[8,128,256]{2,1,0:T(8,128)(2,1)S(1)} %bitcast.64), channel_id=1, source_target_pairs={{0,4},{4,0},{1,5},{5,1},{2,6},{6,2},{3,7},{7,3},{8,12},{12,8},{9,1... | collective-permute-start | bytes 1572872 | tf_op jit(solution)/shard_map/ppermute | solution.py:44
  159.9 12.7 %all-to-all-start.3 = ((f32[16,16,256]{2,1,0:T(8,128)}), f32[16,16,256]{2,1,0:T(8,128)S(1)}, u32[]{:S(2)}, u32[]{:S(2)}) async-start(f32[16,16,256]{2,1,0:T(8,128)} %bitcast.56), calls=%async_computation.3 | async-start | bytes 524288 | tf_op jit(solution)/shard_map/all_to_all | solution.py:475
  167.2 14.3 %collective-permute-start.29 = (bf16[8,128,256]{2,1,0:T(8,128)(2,1)}, bf16[8,128,256]{2,1,0:T(8,128)(2,1)S(1)}, u32[]{:S(2)}, u32[]{:S(2)}) collective-permute-start(bf16[8,128,256]{2,1,0:T(8,128)(2,1)} %collective-permute-done.28.refs_8_), channel_id=1, source_target_pairs={{0,1},{4,5},{1,2},{5,6},{2,3},{6,7},{3,0},{7,4},{8,9},{12,13},{9,1... | collective-permute-start | bytes 1572872 | tf_op jit(solution)/shard_map/ppermute | solution.py:44
  174.2 15.6 %collective-permute-start.33 = (bf16[8,128,256]{2,1,0:T(8,128)(2,1)}, bf16[8,128,256]{2,1,0:T(8,128)(2,1)S(1)}, u32[]{:S(2)}, u32[]{:S(2)}) collective-permute-start(bf16[8,128,256]{2,1,0:T(8,128)(2,1)} %get-tuple-element.61.refs_6_), channel_id=1, source_target_pairs={{0,3},{4,7},{1,0},{5,4},{2,1},{6,5},{3,2},{7,6},{8,11},{12,15},{9,... | collective-permute-start | bytes 1572872 | tf_op jit(solution)/shard_map/ppermute | solution.py:44
  174.2 20.5 %collective-permute-start.35 = (bf16[8,128,256]{2,1,0:T(8,128)(2,1)}, bf16[8,128,256]{2,1,0:T(8,128)(2,1)S(1)}, u32[]{:S(2)}, u32[]{:S(2)}) collective-permute-start(bf16[8,128,256]{2,1,0:T(8,128)(2,1)} %collective-permute-done.28.refs_8_), channel_id=1, source_target_pairs={{0,4},{4,0},{1,5},{5,1},{2,6},{6,2},{3,7},{7,3},{8,12},{12,8},{9,1... | collective-permute-start | bytes 1572872 | tf_op jit(solution)/shard_map/ppermute | solution.py:44
  181.6 18.2 %collective-permute-start.30 = (bf16[3,128,256]{2,1,0:T(8,128)(2,1)S(1)}, bf16[3,128,256]{2,1,0:T(8,128)(2,1)S(1)}, u32[]{:S(2)}, u32[]{:S(2)}) collective-permute-start(bf16[3,128,256]{2,1,0:T(8,128)(2,1)S(1)} %slice.38), channel_id=1, source_target_pairs={{0,4},{4,0},{1,5},{5,1},{2,6},{6,2},{3,7},{7,3},{8,12},{12,8},{9,1... | collective-permute-start | bytes 589832 | tf_op jit(solution)/shard_map/ppermute | solution.py:44
  228.0 13.3 %collective-permute-start.49 = (bf16[8,128,256]{2,1,0:T(8,128)(2,1)}, bf16[8,128,256]{2,1,0:T(8,128)(2,1)S(1)}, u32[]{:S(2)}, u32[]{:S(2)}) collective-permute-start(bf16[8,128,256]{2,1,0:T(8,128)(2,1)} %get-tuple-element.81), channel_id=1, source_target_pairs={{0,8},{8,0},{16,24},{24,16},{32,40},{40,32},{48,56},{56,48},{64,72... | collective-permute-start | bytes 1572872 | tf_op jit(solution)/shard_map/ppermute | solution.py:34
  236.8 12.8 %collective-permute-start.52 = (bf16[8,128,256]{2,1,0:T(8,128)(2,1)}, bf16[8,128,256]{2,1,0:T(8,128)(2,1)}, u32[]{:S(2)}, u32[]{:S(2)}) collective-permute-start(bf16[8,128,256]{2,1,0:T(8,128)(2,1)} %get-tuple-element.84), channel_id=1, source_target_pairs={{0,8},{8,0},{16,24},{24,16},{32,40},{40,32},{48,56},{56,48},{64,72... | collective-permute-start | bytes 1572872 | tf_op jit(solution)/shard_map/ppermute | solution.py:34
  238.4 20.2 %collective-permute-start.40 = (bf16[8,128,256]{2,1,0:T(8,128)(2,1)}, bf16[8,128,256]{2,1,0:T(8,128)(2,1)S(1)}, u32[]{:S(2)}, u32[]{:S(2)}) collective-permute-start(bf16[8,128,256]{2,1,0:T(8,128)(2,1)} %get-tuple-element.70), channel_id=1, source_target_pairs={{0,8},{8,0},{16,24},{24,16},{32,40},{40,32},{48,56},{56,48},{64,72... | collective-permute-start | bytes 1572872 | tf_op jit(solution)/shard_map/ppermute | solution.py:34
  241.3 15.0 %collective-permute-start.54 = (bf16[8,128,256]{2,1,0:T(8,128)(2,1)S(1)}, bf16[8,128,256]{2,1,0:T(8,128)(2,1)S(1)}, u32[]{:S(2)}, u32[]{:S(2)}) collective-permute-start(bf16[8,128,256]{2,1,0:T(8,128)(2,1)S(1)} %add_convert_fusion.2), channel_id=1, source_target_pairs={{0,32},{8,40},{16,48},{24,56},{32,64},{40,72},{48,80},{56,88},{64,... | collective-permute-start | bytes 1572872 | tf_op jit(solution)/shard_map/ppermute | solution.py:34
  242.7 17.3 %collective-permute-start.50 = (bf16[8,128,256]{2,1,0:T(8,128)(2,1)S(1)}, bf16[8,128,256]{2,1,0:T(8,128)(2,1)S(1)}, u32[]{:S(2)}, u32[]{:S(2)}) collective-permute-start(bf16[8,128,256]{2,1,0:T(8,128)(2,1)S(1)} %add_convert_fusion.4), channel_id=1, source_target_pairs={{0,96},{8,104},{16,112},{24,120},{32,0},{40,8},{48,16},{56,24},{64... | collective-permute-start | bytes 1572872 | tf_op jit(solution)/shard_map/ppermute | solution.py:34
  246.9 13.1 %collective-permute-start.48 = (bf16[8,128,256]{2,1,0:T(8,128)(2,1)S(1)}, bf16[8,128,256]{2,1,0:T(8,128)(2,1)S(1)}, u32[]{:S(2)}, u32[]{:S(2)}) collective-permute-start(bf16[8,128,256]{2,1,0:T(8,128)(2,1)S(1)} %add_convert_fusion.5), channel_id=1, source_target_pairs={{0,16},{8,24},{16,0},{24,8},{32,48},{40,56},{48,32},{56,40},{64,80... | collective-permute-start | bytes 1572872 | tf_op jit(solution)/shard_map/ppermute | solution.py:34
  249.6 28.3 %collective-permute-start.37 = (bf16[8,128,256]{2,1,0:T(8,128)(2,1)}, bf16[8,128,256]{2,1,0:T(8,128)(2,1)}, u32[]{:S(2)}, u32[]{:S(2)}) collective-permute-start(bf16[8,128,256]{2,1,0:T(8,128)(2,1)} %get-tuple-element.66), channel_id=1, source_target_pairs={{0,8},{8,0},{16,24},{24,16},{32,40},{40,32},{48,56},{56,48},{64,72... | collective-permute-start | bytes 1572872 | tf_op jit(solution)/shard_map/ppermute | solution.py:34
  256.4 21.6 %collective-permute-start.39 = (bf16[8,128,256]{2,1,0:T(8,128)(2,1)S(1)}, bf16[8,128,256]{2,1,0:T(8,128)(2,1)S(1)}, u32[]{:S(2)}, u32[]{:S(2)}) collective-permute-start(bf16[8,128,256]{2,1,0:T(8,128)(2,1)S(1)} %add_convert_fusion.6), channel_id=1, source_target_pairs={{0,32},{8,40},{16,48},{24,56},{32,64},{40,72},{48,80},{56,88},{64,... | collective-permute-start | bytes 1572872 | tf_op jit(solution)/shard_map/ppermute | solution.py:34
  258.5 19.4 %collective-permute-start.55 = (bf16[8,128,256]{2,1,0:T(8,128)(2,1)}, bf16[8,128,256]{2,1,0:T(8,128)(2,1)}, u32[]{:S(2)}, u32[]{:S(2)}) collective-permute-start(bf16[8,128,256]{2,1,0:T(8,128)(2,1)} %add_convert_fusion.1), channel_id=1, source_target_pairs={{0,16},{8,24},{16,0},{24,8},{32,48},{40,56},{48,32},{56,40},{64,80... | collective-permute-start | bytes 1572872 | tf_op jit(solution)/shard_map/ppermute | solution.py:34
  261.4 16.5 %collective-permute-start.51 = (bf16[8,128,256]{2,1,0:T(8,128)(2,1)S(1)}, bf16[8,128,256]{2,1,0:T(8,128)(2,1)S(1)}, u32[]{:S(2)}, u32[]{:S(2)}) collective-permute-start(bf16[8,128,256]{2,1,0:T(8,128)(2,1)S(1)} %add_convert_fusion.3), channel_id=1, source_target_pairs={{0,96},{8,104},{16,112},{24,120},{32,0},{40,8},{48,16},{56,24},{64... | collective-permute-start | bytes 1572872 | tf_op jit(solution)/shard_map/ppermute | solution.py:34
  (63 other events, 952.2 us)
